TPU v7x, 128 devices: a whole 4x4x4 slice. The times are simulated.
128 devices in a mesh: cp: 64 (over z, x, y), dp: 2 (over core).
Axes of the slice: x: 4, y: 4, z: 4, core: 2. Of those that a mesh axis runs over, the one named last changes fastest.
Arguments:
- frame_rows: bfloat16 [192, 256, 8, 512], P('dp', 'cp'), parts along dimension 0, may hold values from -6 to 6
- frame_counts: int32 [32], P('dp'), parts along dimension 0, may hold values from 1 to 6, 64 in all
- conv_weight: bfloat16 [3, 3, 512, 512], replicated, may hold values from -0.09375 to 0.09375
- norm_gain: float32 [512], replicated, may hold values from 0.25 to 1.75
- latent_proj: bfloat16 [512, 16], replicated, may hold values from -0.25 to 0.25
- patch_weight: bfloat16 [64, 3072], replicated, may hold values from -0.75 to 0.75
- frame_embed: bfloat16 [6, 3072], replicated, may hold values from -5 to 5
- query_gain: float32 [3072], replicated, may hold values from 0.25 to 1.75
- query_weight: bfloat16 [3072, 3072], P(None, 'cp'), may hold values from -0.109375 to 0.109375
Outputs:
- queries: bfloat16 [24, 65536, 128], P(None, ('dp', 'cp')), parts along dimension 1
There are 2 independent parts, one for each index of `dp`. A program takes and returns all parts, laid end to end along the dimension named above; an argument that names none is the same for every part. Nothing has to cross between parts.
Inputs may be any that keep to these rules, and one draw needn't show every extreme that they name: `frame_counts`: the counts sum to 64 and some clip has exactly 6 frames.
All inputs are finite; a program needn't handle non-finite values.
Results may differ from a plain program's by a relative error of at most 0.0061.
Values may be sent and summed in bfloat16 or wider, within the bound.
No kernel may reach another device: no remote copies, remote signals or barrier semaphores. Data moves between devices by JAX's collectives and lax.ppermute only.
A program may use at most 192 MiB of HBM per device.

v0:
```python
import jax
import jax.numpy as jnp
from jax import lax
from jax.sharding import PartitionSpec as P

LAT = 16
HID = 3072
HEAD_DIM = 128
MAXF = 6


EPSILON = 1e-06


def with_halo(value, sides, width):
    for axis, dim in sides:
        peers, length = (lax.axis_size(axis), value.shape[dim])
        up = [(i, (i + 1) % peers) for i in range(peers - 1)]
        down = [(j, i) for i, j in up]
        last = lax.slice_in_dim(value, length - width, length, axis=dim)
        initial = lax.slice_in_dim(value, 0, width, axis=dim)
        before = lax.ppermute(last, axis, up)
        after = lax.ppermute(initial, axis, down)
        value = jnp.concatenate([before, value, after], axis=dim)
    return value


def rms_scale(values, gain):
    return values * lax.rsqrt(jnp.mean(values * values, axis=-1, keepdims=True) + EPSILON) * gain


def local(
    frame_rows,
    frame_counts,
    conv_weight,
    norm_gain,
    latent_proj,
    patch_weight,
    frame_embed,
    query_gain,
    query_weight,
):
    devices = lax.axis_size("cp")
    own_index = lax.axis_index("cp")
    slot_count = frame_rows.shape[0]
    clip_count = frame_counts.shape[0]
    clip_ends = jnp.cumsum(frame_counts)
    clip_starts = clip_ends - frame_counts
    packed_index = jnp.arange(devices, dtype=jnp.int32)
    clip_index = jnp.sum((clip_ends[None, :] <= packed_index[:, None]).astype(jnp.int32), axis=1)
    selector = clip_index[:, None] == jnp.arange(clip_count, dtype=jnp.int32)[None, :]
    first_frame = jnp.sum(jnp.where(selector, clip_starts[None, :], 0), axis=1)
    frame_offset = packed_index - first_frame
    slot_index = clip_index * MAXF + frame_offset
    row_count = frame_rows.shape[1]
    col_count = frame_rows.shape[2]
    padded = with_halo(frame_rows, (("cp", 1),), 1)
    padded = jnp.pad(padded, ((0, 0), (0, 0), (1, 1), (0, 0)))
    summed = jnp.zeros(frame_rows.shape[:3] + (conv_weight.shape[3],), jnp.float32)
    for row_shift in range(3):
        for col_shift in range(3):
            window = padded[:, row_shift : row_shift + row_count, col_shift : col_shift + col_count]
            summed = summed + jnp.einsum(
                "sijc,cd->sijd",
                window,
                conv_weight[row_shift, col_shift],
                preferred_element_type=jnp.float32,
            )
    residual = frame_rows.astype(jnp.float32) + jax.nn.silu(summed)
    normed = rms_scale(residual, norm_gain).astype(jnp.bfloat16)
    latent = jnp.einsum(
        "sijc,cl->sijl", normed, latent_proj, preferred_element_type=jnp.float32
    ).astype(jnp.bfloat16)
    block_tokens = row_count // 2 * (col_count // 2)
    tokens = (
        latent.reshape(slot_count, row_count // 2, 2, col_count // 2, 2, LAT)
        .transpose(0, 1, 3, 2, 4, 5)
        .reshape(slot_count, block_tokens, 4 * LAT)
    )
    embedded = jnp.einsum(
        "stf,fh->sth", tokens, patch_weight, preferred_element_type=jnp.float32
    ).astype(jnp.bfloat16)
    outgoing = jnp.take(embedded, slot_index, axis=0)
    arrived = lax.all_to_all(outgoing, "cp", split_axis=0, concat_axis=0, tiled=True)
    sequence = arrived.reshape(-1, HID)
    own_offset = jnp.sum(jnp.where(packed_index == own_index, frame_offset, 0))
    picker = jnp.arange(MAXF, dtype=jnp.int32) == own_offset
    position = jnp.sum(jnp.where(picker[:, None], frame_embed.astype(jnp.float32), 0.0), axis=0)
    with_position = sequence.astype(jnp.float32) + position[None, :]
    normalized = rms_scale(with_position, query_gain).astype(jnp.bfloat16)
    projected = jnp.dot(
        normalized,
        lax.all_gather(query_weight, "cp", axis=1, tiled=True),
        preferred_element_type=jnp.float32,
    ).astype(jnp.bfloat16)
    return projected.reshape(-1, HID // HEAD_DIM, HEAD_DIM).transpose(1, 0, 2)


def solution(mesh):
    return jax.shard_map(
        local,
        mesh=mesh,
        in_specs=(P("dp", "cp", None, None), P("dp"), P(), P(), P(), P(), P(), P(), P(None, "cp")),
        out_specs=P(None, ("dp", "cp"), None),
        check_vma=False,
    )
```

profile of v0, /device:TPU:0, one launch (start us, length us, event | category | flops | bytes accessed | tf_op | source)
XLA Modules:
  0.0 196.8 jit_solution(3626470449895704850)
XLA Ops:
  6.5 0.0 copy-start
  6.5 0.7 all-gather.2.cloned.1.call-update
  7.3 0.0 copy-start.2
  7.3 2.8 %fusion.71 = (bf16[96,1,8,512]{3,2,1,0:T(8,128)(2,1)}, bf16[96,1,8,512]{3,2,1,0:T(8,128)(2,1)}) fusion(bf16[96,4,8,512]{3,2,1,0:T(8,128)(2,1)} %param.9), kind=kLoop, calls=%fused_computation.93 | loop fusion | bytes 3145728 | tf_op jit(solution)/shard_map/slice | solution.py:20
  10.0 4.4 %collective-permute-start = (bf16[96,1,8,512]{3,2,1,0:T(8,128)(2,1)}, bf16[96,1,8,512]{3,2,1,0:T(8,128)(2,1)}, u32[]{:S(2)}, u32[]{:S(2)}) collective-permute-start(bf16[96,1,8,512]{3,2,1,0:T(8,128)(2,1)} %get-tuple-element.5), channel_id=1, source_target_pairs={{0,2},{2,4},{4,6},{6,8},{8,10},{10,12},{12,14},{14,16},{16,18},{18... | collective-permute-start | bytes 2359304 | tf_op jit(solution)/shard_map/ppermute | solution.py:22
  14.5 1.3 collective-permute-start.1
  15.8 0.7 copy.26
  16.5 0.1 reduce.1
  16.7 0.7 sub.17
  17.3 0.1 convert_reduce_fusion
  17.4 0.1 select_reduce_fusion.1
  17.5 0.6 pad_clamp_fusion
  18.1 0.6 compare_and_fusion
  18.7 6.6 %fusion.49 = f32[96,4,8,512]{3,2,1,0:T(8,128)} fusion(bf16[96,4,8,512]{3,2,1,0:T(8,128)(2,1)} %param.9, bf16[3,3,512,512]{3,2,1,0:T(8,128)(2,1)} %param.11), kind=kOutput, calls=%fused_computation.56 | convolution fusion | flops 1610612736 | bytes 9961472 | tf_op jit(solution)/shard_map/sijc,cd->sijd/dot_general | solution.py:63
  25.3 7.4 %collective-permute-done = bf16[96,1,8,512]{3,2,1,0:T(8,128)(2,1)} collective-permute-done((bf16[96,1,8,512]{3,2,1,0:T(8,128)(2,1)}, bf16[96,1,8,512]{3,2,1,0:T(8,128)(2,1)}, u32[]{:S(2)}, u32[]{:S(2)}) %collective-permute-start) | collective-permute-done | bytes 786464 | tf_op jit(solution)/shard_map/ppermute | solution.py:22
  32.7 5.7 %fusion.12 = f32[96,4,8,512]{3,2,1,0:T(8,128)} fusion(bf16[96,4,8,512]{3,2,1,0:T(8,128)(2,1)S(1)} %copy-done.2, bf16[96,1,8,512]{3,2,1,0:T(8,128)(2,1)} %collective-permute-done, bf16[3,3,512,512]{3,2,1,0:T(8,128)(2,1)} %param.11), kind=kOutput, calls=%fused_computation.22 | convolution fusion | flops 1618477056 | bytes 10747904 | tf_op jit(solution)/shard_map/sijc,cd->sijd/dot_general | solution.py:63
  38.4 0.5 collective-permute-done.1
  38.8 5.5 %fusion.16 = f32[96,4,8,512]{3,2,1,0:T(8,128)} fusion(bf16[96,1,8,512]{3,2,1,0:T(8,128)(2,1)} %collective-permute-done.1, bf16[96,4,8,512]{3,2,1,0:T(8,128)(2,1)S(1)} %copy-done.2, bf16[3,3,512,512]{3,2,1,0:T(8,128)(2,1)S(1)} %bitcast.115), kind=kOutput, calls=%fused_computation.26 | convolution fusion | flops 1618477056 | bytes 10747904 | tf_op jit(solution)/shard_map/sijc,cd->sijd/dot_general | solution.py:63
  44.4 5.7 %fusion.5 = bf16[96,6,10,512]{3,2,1,0:T(8,128)(2,1)S(1)} fusion(bf16[96,1,8,512]{3,2,1,0:T(8,128)(2,1)} %collective-permute-done.1, bf16[96,4,8,512]{3,2,1,0:T(8,128)(2,1)S(1)} %copy-done.2, bf16[96,1,8,512]{3,2,1,0:T(8,128)(2,1)} %collective-permute-done), kind=kLoop, calls=%fused_computation.8 | loop fusion | flops 35389440 | bytes 10616832 | tf_op jit(solution)/shard_map/concatenate | solution.py:24
  50.1 4.9 %fusion.24 = f32[96,4,8,512]{3,2,1,0:T(8,128)} fusion(bf16[96,6,10,512]{3,2,1,0:T(8,128)(2,1)S(1)} %fusion.5, bf16[3,3,512,512]{3,2,1,0:T(8,128)(2,1)S(1)} %bitcast.115), kind=kOutput, calls=%fused_computation.34 | convolution fusion | flops 1610612736 | bytes 9961472 | tf_op jit(solution)/shard_map/sijc,cd->sijd/dot_general | solution.py:63
  55.0 4.4 %fusion.28 = f32[96,4,8,512]{3,2,1,0:T(8,128)} fusion(bf16[96,6,10,512]{3,2,1,0:T(8,128)(2,1)S(1)} %fusion.5, bf16[3,3,512,512]{3,2,1,0:T(8,128)(2,1)S(1)} %bitcast.115), kind=kOutput, calls=%fused_computation.38 | convolution fusion | flops 1610612736 | bytes 9961472 | tf_op jit(solution)/shard_map/sijc,cd->sijd/dot_general | solution.py:63
  59.4 4.4 %fusion.32 = f32[96,4,8,512]{3,2,1,0:T(8,128)} fusion(bf16[96,6,10,512]{3,2,1,0:T(8,128)(2,1)S(1)} %fusion.5, bf16[3,3,512,512]{3,2,1,0:T(8,128)(2,1)S(1)} %bitcast.115), kind=kOutput, calls=%fused_computation.42 | convolution fusion | flops 1610612736 | bytes 9961472 | tf_op jit(solution)/shard_map/sijc,cd->sijd/dot_general | solution.py:63
  63.9 4.4 %fusion.26 = f32[96,4,8,512]{3,2,1,0:T(8,128)} fusion(bf16[96,6,10,512]{3,2,1,0:T(8,128)(2,1)S(1)} %fusion.5, bf16[3,3,512,512]{3,2,1,0:T(8,128)(2,1)S(1)} %bitcast.115), kind=kOutput, calls=%fused_computation.36 | convolution fusion | flops 1610612736 | bytes 9961472 | tf_op jit(solution)/shard_map/sijc,cd->sijd/dot_general | solution.py:63
  68.3 4.5 %fusion.30 = f32[96,4,8,512]{3,2,1,0:T(8,128)} fusion(bf16[96,6,10,512]{3,2,1,0:T(8,128)(2,1)S(1)} %fusion.5, bf16[3,3,512,512]{3,2,1,0:T(8,128)(2,1)S(1)} %bitcast.115), kind=kOutput, calls=%fused_computation.40 | convolution fusion | flops 1610612736 | bytes 9961472 | tf_op jit(solution)/shard_map/sijc,cd->sijd/dot_general | solution.py:63
  72.9 25.9 %multiply_reduce_fusion = (f32[96,4,8]{2,1,0:T(4,128)}, f32[96,4,8,512]{3,2,1,0:T(8,128)}) fusion(bf16[3,3,512,512]{3,2,1,0:T(8,128)(2,1)S(1)} %bitcast.115, bf16[96,6,10,512]{3,2,1,0:T(8,128)(2,1)} %copy-done.3, f32[96,4,8,512]{3,2,1,0:T(8,128)} %fusion.16, f32[96,4,8,512]{3,2,1,0:T(8,128)} %fusion.24, f32[96,4,8,512]{3,2,1,0:T(8,128)} %fusion.26, ...), kind=kOutput, calls=%fused_computation.18 | convolution fusion | flops 1635775488 | bytes 63451136 | tf_op jit(solution)/shard_map/sijc,cd->sijd/dot_general | solution.py:63
  98.7 1.0 copy.27
  99.8 0.1 copy.28
  99.9 3.8 %fusion.42 = bf16[96,4,8,16]{3,2,1,0:T(8,128)(2,1)S(1)} fusion(f32[96,4,8,512]{3,2,1,0:T(8,128)} %get-tuple-element.8, f32[512]{0:T(512)} %param.12, f32[96,4,8]{2,1,0:T(4,128)S(1)} %copy.28, bf16[512,16]{0,1:T(8,128)(2,1)S(1)} %copy-done.5), kind=kOutput, calls=%fused_computation.51 | convolution fusion | flops 55099392 | bytes 6420480 | tf_op jit(solution)/shard_map/sijc,cl->sijl/dot_general | solution.py:71
  103.8 0.8 copy.29
  104.6 0.2 copy.30
  104.8 3.5 %convolution_convert_fusion = bf16[96,8,3072]{2,1,0:T(8,128)(2,1)} fusion(bf16[96,8,64]{2,1,0:T(8,128)(2,1)S(1)} %copy.30, bf16[64,3072]{1,0:T(8,128)(2,1)S(1)} %copy-done), kind=kOutput, calls=%fused_computation.20 | convolution fusion | flops 304349184 | bytes 5210112 | tf_op jit(solution)/shard_map/stf,fh->sth/dot_general | solution.py:80
  108.3 3.2 %gather_fusion = bf16[64,8,3072]{2,1,0:T(8,128)(2,1)S(1)} fusion(bf16[96,8,3072]{2,1,0:T(8,128)(2,1)} %convolution_convert_fusion, s32[1024]{0:T(1024)} %pad_clamp_fusion), kind=kCustom, calls=%fused_computation | custom fusion | bytes 6291712 | tf_op jit(solution)/shard_map/jit(_take)/gather | solution.py:83
  111.5 0.0 copy-done.6
  111.5 0.0 copy-start.8
  111.5 0.0 copy-start.4
  111.6 2.0 %broadcast_select_fusion = bf16[64,8,3072]{2,1,0:T(8,128)(2,1)} fusion(bf16[64,8,3072]{2,1,0:T(8,128)(2,1)S(1)} %gather_fusion, pred[64]{0:T(512)(128)(4,1)S(1)} %copy-done.6), kind=kLoop, calls=%fused_computation.49 | loop fusion | flops 1572864 | bytes 6291520 | tf_op jit(solution)/shard_map/jit(_take)/select_n | solution.py:83
  113.6 14.4 %all-to-all-start = ((bf16[64,8,3072]{2,1,0:T(8,128)(2,1)}), bf16[64,8,3072]{2,1,0:T(8,128)(2,1)S(1)}, u32[]{:S(2)}, u32[]{:S(2)}) async-start(bf16[64,8,3072]{2,1,0:T(8,128)(2,1)} %broadcast_select_fusion), calls=%async_computation | async-start | bytes 6291456 | tf_op jit(solution)/shard_map/all_to_all | solution.py:84
  128.0 0.7 fusion.66
  128.6 0.6 iota_compare_fusion.4
  129.2 0.0 copy-done.4
  129.3 0.1 select_reduce_fusion
  129.4 40.0 %all-to-all-done = bf16[64,8,3072]{2,1,0:T(8,128)(2,1)S(1)} async-done(((bf16[64,8,3072]{2,1,0:T(8,128)(2,1)}), bf16[64,8,3072]{2,1,0:T(8,128)(2,1)S(1)}, u32[]{:S(2)}, u32[]{:S(2)}) %all-to-all-start) | async-done | bytes 3145760 | tf_op jit(solution)/shard_map/all_to_all | solution.py:84
  169.3 0.9 fusion.11
  170.2 0.1 rsqrt.21
  170.3 0.0 all-gather.2.cloned.1.call-done
  170.3 0.0 copy-start.1
  170.3 15.2 %fusion.39 = bf16[64,24,8,128]{3,2,1,0:T(8,128)(2,1)} fusion(bf16[3072,3072]{0,1:T(8,128)(2,1)} %all-gather.2.cloned.1.call-done, bf16[64,8,3072]{2,1,0:T(8,128)(2,1)S(1)} %all-to-all-done, f32[3072]{0:T(1024)} %param.16, f32[512]{0:T(512)S(1)} %rsqrt.21, f32[3072]{0:T(1024)S(1)} %select_reduce_fusion), kind=kOutput, calls=%fused_computation.50 | convolution fusion | flops 9673113600 | bytes 25192448 | tf_op jit(solution)/shard_map/dot_general | solution.py:91
  185.6 4.4 %copy.44 = bf16[64,24,8,128]{3,2,0,1:T(8,128)(2,1)} copy(bf16[64,24,8,128]{3,2,1,0:T(8,128)(2,1)} %fusion.39) | data formatting | bytes 6291456 | tf_op jit(solution)/shard_map/reshape | solution.py:96
  (21 shorter events, 0.1 us)
Async XLA Ops:
  6.5 98.2 %copy-start = (bf16[64,3072]{1,0:T(8,128)(2,1)S(1)}, bf16[64,3072]{1,0:T(8,128)(2,1)}, u32[]{:S(2)}) copy-start(bf16[64,3072]{1,0:T(8,128)(2,1)} %param.14) | copy-start | bytes 1179652
  6.5 163.8 %all-gather.2.cloned.1.call-start = ((), (), s32[]{:S(2)}) async-start(), calls=%async_computation.1 | async-start | bytes 19169280 | tf_op jit(solution)/shard_map/all_gather | solution.py:93
  7.3 25.4 %copy-start.2 = (bf16[96,4,8,512]{3,2,1,0:T(8,128)(2,1)S(1)}, bf16[96,4,8,512]{3,2,1,0:T(8,128)(2,1)}, u32[]{:S(2)}) copy-start(bf16[96,4,8,512]{3,2,1,0:T(8,128)(2,1)} %param.9) | copy-start | bytes 9437188
  10.0 22.6 %collective-permute-start = (bf16[96,1,8,512]{3,2,1,0:T(8,128)(2,1)}, bf16[96,1,8,512]{3,2,1,0:T(8,128)(2,1)}, u32[]{:S(2)}, u32[]{:S(2)}) collective-permute-start(bf16[96,1,8,512]{3,2,1,0:T(8,128)(2,1)} %get-tuple-element.5), channel_id=1, source_target_pairs={{0,2},{2,4},{4,6},{6,8},{8,10},{10,12},{12,14},{14,16},{16,18},{18... | collective-permute-start | bytes 2359304 | tf_op jit(solution)/shard_map/ppermute | solution.py:22
  14.5 24.4 %collective-permute-start.1 = (bf16[96,1,8,512]{3,2,1,0:T(8,128)(2,1)}, bf16[96,1,8,512]{3,2,1,0:T(8,128)(2,1)}, u32[]{:S(2)}, u32[]{:S(2)}) collective-permute-start(bf16[96,1,8,512]{3,2,1,0:T(8,128)(2,1)} %get-tuple-element.6), channel_id=1, source_target_pairs={{2,0},{4,2},{6,4},{8,6},{10,8},{12,10},{14,12},{16,14},{18,16},{20... | collective-permute-start | bytes 2359304 | tf_op jit(solution)/shard_map/ppermute | solution.py:23
  17.5 0.6 copy-start.7
  18.7 20.1 %slice-start = ((s8[4718592]{0:T(1024)(128)(4,1)}), s8[4194304]{0:T(1024)(128)(4,1)S(1)}, s32[]{:S(2)}) async-start(s8[4718592]{0:T(1024)(128)(4,1)} %bitcast.114), calls=%async_computation.2 | async-start | bytes 8388608
  25.3 13.6 %slice-start.1 = ((s8[4718592]{0:T(1024)(128)(4,1)}), s8[524288]{0:T(1024)(128)(4,1)S(1)}, s32[]{:S(2)}) async-start(s8[4718592]{0:T(1024)(128)(4,1)} %bitcast.114), calls=%async_computation.3 | async-start | bytes 1048576
  50.1 18.2 %copy-start.3 = (bf16[96,6,10,512]{3,2,1,0:T(8,128)(2,1)}, bf16[96,6,10,512]{3,2,1,0:T(8,128)(2,1)S(1)}, u32[]{:S(2)}) copy-start(bf16[96,6,10,512]{3,2,1,0:T(8,128)(2,1)S(1)} %fusion.5) | copy-start | bytes 17694724
  72.9 27.1 %copy-start.5 = (bf16[512,16]{0,1:T(8,128)(2,1)S(1)}, bf16[512,16]{0,1:T(8,128)(2,1)}, u32[]{:S(2)}) copy-start(bf16[512,16]{0,1:T(8,128)(2,1)} %param.13) | copy-start | bytes 49156
  103.8 7.8 %copy-start.6 = (pred[64]{0:T(512)(128)(4,1)S(1)}, pred[64]{0:T(512)(128)(4,1)}, u32[]{:S(2)}) copy-start(pred[64]{0:T(512)(128)(4,1)} %compare_and_fusion) | copy-start | bytes 196
  111.5 16.4 %copy-start.8 = (s32[64]{0:T(128)S(1)}, s32[64]{0:T(128)}, u32[]{:S(2)}) copy-start(s32[64]{0:T(128)} %copy-done.7) | copy-start | bytes 772
  111.5 17.7 %copy-start.4 = (bf16[6,3072]{1,0:T(8,128)(2,1)S(1)}, bf16[6,3072]{1,0:T(8,128)(2,1)}, u32[]{:S(2)}) copy-start(bf16[6,3072]{1,0:T(8,128)(2,1)} %param.15) | copy-start | bytes 110596
  113.6 55.7 %all-to-all-start = ((bf16[64,8,3072]{2,1,0:T(8,128)(2,1)}), bf16[64,8,3072]{2,1,0:T(8,128)(2,1)S(1)}, u32[]{:S(2)}, u32[]{:S(2)}) async-start(bf16[64,8,3072]{2,1,0:T(8,128)(2,1)} %broadcast_select_fusion), calls=%async_computation | async-start | bytes 6291456 | tf_op jit(solution)/shard_map/all_to_all | solution.py:84
  170.3 19.7 %copy-start.1 = (bf16[64,3072]{1,0:T(8,128)(2,1)S(1)}, bf16[64,3072]{1,0:T(8,128)(2,1)}, u32[]{:S(2)}) copy-start(bf16[64,3072]{1,0:T(8,128)(2,1)} %param.14) | copy-start | bytes 1179652
Sparse Core Ops, SparseCore 0:
  10.1 121.4 all-gather.1
where the time goes:
time: 197 us
  matrix products  89 us (45%)
  waiting for transfers between devices  48.6 us (25%)
  starting transfers between devices  20.1 us (10%)
  between operations  13.6 us (7%)
  local copies, waits for them, and re-layouts  13.4 us (7%)
  other arithmetic  12.2 us (6%)
    dot_general x9, matrix products, local(): jnp.einsum('sijc,cd->sijd', window, conv_weight[row_shift, col_shift], pr...  66.4 us
    all_to_all x1, waiting for transfers between devices, local(): lax.all_to_all(outgoing, 'cp', split_axis=0, concat_axis=0, tiled=True)  40 us
    dot_general x1, matrix products, local(): jnp.dot(normalized, lax.all_gather(query_weight, 'cp', axis=1, tiled=True...  15.2 us
    all_to_all x1, starting transfers between devices, local(): lax.all_to_all(outgoing, 'cp', split_axis=0, concat_axis=0, tiled=True)  14.4 us
    ppermute x1, waiting for transfers between devices, with_halo(): before = lax.ppermute(last, axis, up)  7.4 us
    concatenate x1, other arithmetic, with_halo(): value = jnp.concatenate([before, value, after], axis=dim)  5.68 us
    ppermute x1, starting transfers between devices, with_halo(): before = lax.ppermute(last, axis, up)  4.44 us
    reshape x1, local copies, waits for them, and re-layouts, local(): return projected.reshape(-1, HID // HEAD_DIM, HEAD_DIM).transpose(1, 0, 2)  4.42 us
  transfers between devices with their start and end apart: 4, of which 3 were waited for; matrix products, arithmetic and copies ran while one was open for 48% of the time, Pallas kernels for 0%

commit v1 on v0

v1 whole, which is shorter than its diff:
```python
import jax
import jax.numpy as jnp
from jax import lax
from jax.sharding import PartitionSpec as P

LAT = 16
HID = 3072
HEAD_DIM = 128
MAXF = 6
EPSILON = 1e-06
BF = jnp.bfloat16
F32 = jnp.float32


def split(value):
    high = lax.reduce_precision(value, 8, 7)
    return high.astype(BF), (value - high).astype(BF)


def local(
    frame_rows,
    frame_counts,
    conv_weight,
    norm_gain,
    latent_proj,
    patch_weight,
    frame_embed,
    query_gain,
    query_weight,
):
    devices = lax.axis_size("cp")
    own_index = lax.axis_index("cp")
    clip_count = frame_counts.shape[0]
    clip_ends = jnp.cumsum(frame_counts)
    clip_starts = clip_ends - frame_counts
    packed_index = jnp.arange(devices, dtype=jnp.int32)
    clip_index = jnp.sum((clip_ends[None, :] <= packed_index[:, None]).astype(jnp.int32), axis=1)
    selector = clip_index[:, None] == jnp.arange(clip_count, dtype=jnp.int32)[None, :]
    first_frame = jnp.sum(jnp.where(selector, clip_starts[None, :], 0), axis=1)
    frame_offset = packed_index - first_frame
    slot_index = clip_index * MAXF + frame_offset

    table = jnp.concatenate([patch_weight, frame_embed], axis=0).astype(F32) * query_gain[None, :]
    high, low = split(table)
    dims = (((0,), (1,)), ((), ()))
    folded = lax.dot_general(query_weight, high, dims, preferred_element_type=F32)
    folded = folded + lax.dot_general(query_weight, low, dims, preferred_element_type=F32)
    folded = lax.all_gather(folded.astype(BF), "cp", axis=0, tiled=True)

    frames = jnp.take(frame_rows, slot_index, axis=0)
    up = [(i, i + 1) for i in range(devices - 1)]
    down = [(j, i) for i, j in up]
    before = lax.ppermute(frames[:, 3:4], "cp", up)
    after = lax.ppermute(frames[:, 0:1], "cp", down)
    padded = jnp.concatenate([before, frames, after], axis=1)
    summed = lax.conv_general_dilated(
        padded, conv_weight, (1, 1), ((0, 0), (1, 1)),
        dimension_numbers=("NHWC", "HWIO", "NHWC"), preferred_element_type=F32,
    )
    residual = frames.astype(F32) + jax.nn.silu(summed)
    normed = residual * lax.rsqrt(jnp.mean(residual * residual, axis=-1, keepdims=True) + EPSILON) * norm_gain
    latent = jnp.einsum(
        "sijc,cl->sijl", normed.astype(BF), latent_proj, preferred_element_type=F32
    ).astype(BF)
    tokens = (
        latent.reshape(devices, 2, 2, 4, 2, LAT)
        .transpose(0, 1, 3, 2, 4, 5)
        .reshape(devices, 4, 128)
    )
    arrived = lax.all_to_all(tokens, "cp", split_axis=0, concat_axis=0, tiled=True)
    tokens = arrived.reshape(-1, 4 * LAT)

    own_offset = jnp.sum(jnp.where(packed_index == own_index, frame_offset, 0))
    picker = jnp.arange(MAXF, dtype=jnp.int32) == own_offset
    position = jnp.sum(jnp.where(picker[:, None], frame_embed.astype(F32), 0.0), axis=0)
    embedded = jnp.dot(tokens, patch_weight, preferred_element_type=F32) + position[None, :]
    scale = lax.rsqrt(jnp.mean(embedded * embedded, axis=-1, keepdims=True) + EPSILON)
    extra = jnp.broadcast_to(picker.astype(BF)[None, :], (tokens.shape[0], MAXF))
    full = jnp.concatenate([tokens, extra], axis=1)
    by_head = folded.reshape(HID // HEAD_DIM, HEAD_DIM, -1)
    projected = lax.dot_general(by_head, full, (((2,), (1,)), ((), ())), preferred_element_type=F32)
    projected = projected.transpose(0, 2, 1) * scale[None]
    return projected.astype(BF)


def solution(mesh):
    return jax.shard_map(
        local,
        mesh=mesh,
        in_specs=(P("dp", "cp", None, None), P("dp"), P(), P(), P(), P(), P(), P(), P(None, "cp")),
        out_specs=P(None, ("dp", "cp"), None),
        check_vma=False,
    )
```

time: 197 us -> 269 us (1.37)
  blocking collectives: 0 us -> 193 us
  matrix products: 89 us -> 34.8 us
  waiting for transfers between devices: 48.6 us -> 9.48 us
  between operations: 13.6 us -> 0.16 us
  starting transfers between devices: 20.1 us -> 10.3 us
  other arithmetic: 12.2 us -> 7.73 us
    all_gather x0 -> x1, blocking collectives: none -> 193 us  [local(): folded = lax.all_gather(folded.astype(BF), 'cp', axis=0, tiled=True)]
    dot_general x12 -> x5, matrix products: 89 us -> 9.84 us  [the longest x1 2.7 us: local(): lax.dot_general(by_head, full, (((2,), (1,)), ((), ())), preferred_elemen...]
    all_to_all x1, waiting for transfers between devices: 40 us -> 9.47 us  [local(): lax.all_to_all(tokens, 'cp', split_axis=0, concat_axis=0, tiled=True)]
    conv_general_dilated x0 -> x1, matrix products: none -> 24.9 us  [local(): lax.conv_general_dilated(padded, conv_weight, (1, 1), ((0, 0), (1, 1)), d...]
    all_to_all x1, starting transfers between devices: 14.4 us -> 4.62 us  [local(): lax.all_to_all(tokens, 'cp', split_axis=0, concat_axis=0, tiled=True)]
    ppermute x2, waiting for transfers between devices: 7.88 us -> 0.01 us  [the longest x1 0.01 us: local(): before = lax.ppermute(frames[:, 3:4], 'cp', up)]
    concatenate x1 -> x0, other arithmetic: 5.68 us -> none  [with_halo(): value = jnp.concatenate([before, value, after], axis=dim)]
    convert_element_type x0 -> x1, local copies, waits for them, and re-layouts: none -> 4.63 us  [local(): return projected.astype(BF)]
  transfers between devices with their start and end apart: 4 -> 3, of which waited for: 3 -> 1; matrix products, arithmetic and copies ran while one was open for 48% -> 2% of each run, Pallas kernels for 0% -> 0%
where the time goes in v1:
time: 269 us; the launch traced here: 268 us
  blocking collectives  193 us (72%)
  matrix products  34.8 us (13%)
  local copies, waits for them, and re-layouts  12.6 us (5%)
  starting transfers between devices  10.3 us (4%)
  waiting for transfers between devices  9.48 us (4%)
  other arithmetic  7.73 us (3%)
    all_gather x1, blocking collectives, local(): folded = lax.all_gather(folded.astype(BF), 'cp', axis=0, tiled=True)  193 us
    conv_general_dilated x1, matrix products, local(): lax.conv_general_dilated(padded, conv_weight, (1, 1), ((0, 0), (1, 1)), d...  24.9 us
    all_to_all x1, waiting for transfers between devices, local(): lax.all_to_all(tokens, 'cp', split_axis=0, concat_axis=0, tiled=True)  9.47 us
  transfers between devices with their start and end apart: 3, of which 1 were waited for; matrix products, arithmetic and copies ran while one was open for 2% of the time, Pallas kernels for 0%

profile of v1, /device:TPU:0, one launch (start us, length us, event | category | flops | bytes accessed | tf_op | source)
XLA Modules:
  0.0 268.3 jit_solution(4269974271311004881)
XLA Ops:
  0.0 0.0 copy-start
  0.0 0.9 copy.30
  0.9 0.1 reduce
  1.0 0.1 convert_reduce_fusion
  1.1 0.7 sub.21
  1.8 0.1 select_reduce_fusion.1
  1.9 0.0 copy-done
  1.9 2.0 gather_fusion
  3.9 0.0 copy-start.3
  3.9 0.0 copy-start.6
  3.9 4.0 %copy_select_fusion = bf16[64,4,8,512]{3,0,2,1:T(8,128)(2,1)S(1)} fusion(bf16[64,4,8,512]{3,2,1,0:T(8,128)(2,1)} %gather_fusion, pred[64]{0:T(512)(128)(4,1)S(1)} %compare_and_fusion), kind=kLoop, calls=%fused_computation.15 | loop fusion | flops 1048576 | bytes 4194368 | tf_op jit(solution)/shard_map/jit(_take)/select_n | solution.py:50
  8.0 0.0 copy-start.1
  8.0 1.3 copy-done.1
  9.3 1.1 fusion.32
  10.4 4.4 %collective-permute-start = (bf16[64,1,8,512]{3,0,2,1:T(8,128)(2,1)}, bf16[64,1,8,512]{3,0,2,1:T(8,128)(2,1)}, u32[]{:S(2)}, u32[]{:S(2)}) collective-permute-start(bf16[64,1,8,512]{3,0,2,1:T(8,128)(2,1)} %get-tuple-element.5), channel_id=1, source_target_pairs={{0,2},{2,4},{4,6},{6,8},{8,10},{10,12},{12,14},{14,16},{16,18},{18... | collective-permute-start | bytes 1572872 | tf_op jit(solution)/shard_map/ppermute | solution.py:53
  14.8 1.3 collective-permute-start.1
  16.0 0.7 fusion.24
  16.8 0.7 fusion.31
  17.5 0.1 pad.1.clone
  17.5 0.0 copy-done.3
  17.5 0.0 copy-done.6
  17.5 1.4 fusion.18
  18.9 0.7 iota_compare_fusion.2
  19.6 1.4 fusion.15
  21.0 193.3 %all_gather.3 = bf16[3072,70]{1,0:T(8,128)(2,1)} all-gather(bf16[48,70]{1,0:T(8,128)(2,1)S(1)} %fusion.15), channel_id=1, replica_groups=mesh['cp'=64,'dp'=2] {'cp'}, dimensions={0}, use_global_device_ids=true | all-gather | bytes 436800 | tf_op jit(solution)/shard_map/all_gather | solution.py:48
  214.3 0.0 copy-start.4
  214.3 0.0 collective-permute-done
  214.3 0.0 collective-permute-done.1
  214.3 24.9 %multiply_reduce_fusion.1 = (f32[64,4,8]{0,2,1:T(8,128)S(1)}, f32[64,4,8,512]{3,0,2,1:T(8,128)S(1)}) fusion(bf16[3,3,512,512]{3,2,1,0:T(8,128)(2,1)} %param.11, bf16[64,1,8,512]{3,0,2,1:T(8,128)(2,1)} %collective-permute-done.1, bf16[64,4,8,512]{3,0,2,1:T(8,128)(2,1)} %copy-done.1, bf16[64,1,8,512]{3,0,2,1:T(8,128)(2,1)} %collective-permute-done), kind=kOutput, calls=%fused_computation.4 | convolution fusion | flops 8876193792 | bytes 12066816 | tf_op jit(solution)/shard_map/conv_general_dilated | solution.py:56
  239.3 0.0 copy-start.5
  239.3 0.0 copy-done.4
  239.3 0.5 multiply_convert_fusion.1
  239.8 0.2 copy-done.5
  240.0 2.3 fusion.11
  242.3 1.4 copy.33
  243.7 0.7 copy.34
  244.4 4.6 %all-to-all-start = ((bf16[64,4,128]{2,1,0:T(4,128)(2,1)}), bf16[64,4,128]{2,1,0:T(4,128)(2,1)S(1)}, u32[]{:S(2)}, u32[]{:S(2)}) async-start(bf16[64,4,128]{2,1,0:T(4,128)(2,1)} %copy.34), calls=%async_computation | async-start | bytes 131072 | tf_op jit(solution)/shard_map/all_to_all | solution.py:70
  249.1 0.1 select_reduce_fusion
  249.2 9.5 %all-to-all-done = bf16[64,4,128]{2,1,0:T(4,128)(2,1)S(1)} async-done(((bf16[64,4,128]{2,1,0:T(4,128)(2,1)}), bf16[64,4,128]{2,1,0:T(4,128)(2,1)S(1)}, u32[]{:S(2)}, u32[]{:S(2)}) %all-to-all-start) | async-done | bytes 65568 | tf_op jit(solution)/shard_map/all_to_all | solution.py:70
  258.6 0.1 reshape.110
  258.8 0.1 copy.35
  258.9 0.0 copy-start.2
  258.9 2.1 multiply_reduce_fusion
  261.0 0.0 copy-done.2
  261.0 2.7 %fusion = bf16[24,512,128]{1,2,0:T(8,128)(2,1)} fusion(f32[512]{0:T(512)S(1)} %add_rsqrt_fusion.1, bf16[24,128,70]{2,1,0:T(8,128)(2,1)S(1)} %bitcast.34, bf16[512,64]{0,1:T(8,128)(2,1)S(1)} %copy.35, bf16[70]{0:T(256)(128)(2,1)S(1)} %pad.1.clone), kind=kOutput, calls=%fused_computation.6 | convolution fusion | flops 223490048 | bytes 3643532 | tf_op jit(solution)/shard_map/dot_general | solution.py:81
  263.7 4.6 %copy.37 = bf16[24,512,128]{2,1,0:T(8,128)(2,1)} copy(bf16[24,512,128]{1,2,0:T(8,128)(2,1)} %fusion) | data formatting | bytes 6291456 | tf_op jit(solution)/shard_map/convert_element_type | solution.py:83
  (6 shorter events, 0.1 us)
Async XLA Ops:
  0.0 1.9 copy-start
  3.9 13.6 %copy-start.3 = (bf16[6,3072]{1,0:T(8,128)(2,1)S(1)}, bf16[6,3072]{1,0:T(8,128)(2,1)}, u32[]{:S(2)}) copy-start(bf16[6,3072]{1,0:T(8,128)(2,1)} %param.15) | copy-start | bytes 110596
  3.9 13.6 %copy-start.6 = (f32[3072]{0:T(1024)S(1)}, f32[3072]{0:T(1024)}, u32[]{:S(2)}) copy-start(f32[3072]{0:T(1024)} %param.16) | copy-start | bytes 36868
  8.0 1.3 copy-start.1
  10.4 203.9 %collective-permute-start = (bf16[64,1,8,512]{3,0,2,1:T(8,128)(2,1)}, bf16[64,1,8,512]{3,0,2,1:T(8,128)(2,1)}, u32[]{:S(2)}, u32[]{:S(2)}) collective-permute-start(bf16[64,1,8,512]{3,0,2,1:T(8,128)(2,1)} %get-tuple-element.5), channel_id=1, source_target_pairs={{0,2},{2,4},{4,6},{6,8},{8,10},{10,12},{12,14},{14,16},{16,18},{18... | collective-permute-start | bytes 1572872 | tf_op jit(solution)/shard_map/ppermute | solution.py:53
  14.8 199.6 %collective-permute-start.1 = (bf16[64,1,8,512]{3,0,2,1:T(8,128)(2,1)}, bf16[64,1,8,512]{3,0,2,1:T(8,128)(2,1)}, u32[]{:S(2)}, u32[]{:S(2)}) collective-permute-start(bf16[64,1,8,512]{3,0,2,1:T(8,128)(2,1)} %get-tuple-element.6), channel_id=1, source_target_pairs={{2,0},{4,2},{6,4},{8,6},{10,8},{12,10},{14,12},{16,14},{18,16},{20... | collective-permute-start | bytes 1572872 | tf_op jit(solution)/shard_map/ppermute | solution.py:54
  214.3 25.0 %copy-start.4 = (f32[512]{0:T(512)S(1)}, f32[512]{0:T(512)}, u32[]{:S(2)}) copy-start(f32[512]{0:T(512)} %param.12) | copy-start | bytes 6148
  239.3 0.7 copy-start.5
  244.4 14.2 %all-to-all-start = ((bf16[64,4,128]{2,1,0:T(4,128)(2,1)}), bf16[64,4,128]{2,1,0:T(4,128)(2,1)S(1)}, u32[]{:S(2)}, u32[]{:S(2)}) async-start(bf16[64,4,128]{2,1,0:T(4,128)(2,1)} %copy.34), calls=%async_computation | async-start | bytes 131072 | tf_op jit(solution)/shard_map/all_to_all | solution.py:70
  258.9 2.1 copy-start.2

commit v2 on v1

v2 whole, which is shorter than its diff:
```python
import functools

import jax
import jax.numpy as jnp
import numpy as np
from jax import lax
from jax.experimental import pallas as pl
from jax.experimental.pallas import tpu as pltpu
from jax.sharding import PartitionSpec as P

LAT = 16
HID = 3072
HEAD_DIM = 128
HEADS = HID // HEAD_DIM
MAXF = 6
C = 512
WIDTH = 8
STRIP = 4
FRAMES = 64
CLIPS = 16
PART = HID // FRAMES
TOKENS = 512
LANES = 128
MESSAGE = 32
EPSILON = 1e-06
BF = jnp.bfloat16
F32 = jnp.float32
VMEM = pl.BlockSpec(memory_space=pltpu.VMEM)
SMEM = pl.BlockSpec(memory_space=pltpu.SMEM)
ANY = pl.BlockSpec(memory_space=pl.ANY)
MIB = 1 << 20


def nt(left, right):
    return lax.dot_general(left, right, (((1,), (1,)), ((), ())), preferred_element_type=F32)


def dot(left, right):
    return jnp.dot(left, right, preferred_element_type=F32)


def split(value):
    high = value.astype(BF)
    return high, (value - high.astype(F32)).astype(BF)


def each_clip(counts, body):
    def step(clip, start):
        body(clip, start, counts[clip])
        return start + counts[clip]

    lax.fori_loop(0, CLIPS, step, 0)


def edges_kernel(counts, frames, first, last, sems):
    def clip(index, start, count):
        for row, target, sem in ((0, first, 0), (STRIP - 1, last, 1)):
            pltpu.make_async_copy(
                frames.at[pl.ds(index * MAXF, count), row], target.at[pl.ds(start, count)], sems.at[sem]
            ).start()

    each_clip(counts, clip)
    pltpu.make_async_copy(first, first, sems.at[0]).wait()
    pltpu.make_async_copy(last, last, sems.at[1]).wait()


def edges(counts, frames):
    shape = jax.ShapeDtypeStruct((FRAMES, WIDTH, C), BF)
    return pl.pallas_call(
        edges_kernel,
        out_shape=(shape, shape),
        in_specs=[SMEM, ANY],
        out_specs=(ANY, ANY),
        scratch_shapes=[pltpu.SemaphoreType.DMA((2,))],
        cost_estimate=pl.CostEstimate(flops=0, bytes_accessed=2 * MIB, transcendentals=0),
        name="edges",
    )(counts, frames)


def fold_kernel(weight, patch, embed, gain, folded, placed, padded):
    scale = gain[...]
    padded[...] = jnp.zeros_like(padded)
    padded[64 : 64 + PART, :] = weight[...]
    high, low = split(patch[...].astype(F32) * scale)
    both = nt(weight[...], jnp.concatenate([high, high], axis=0)) + nt(
        weight[...], jnp.concatenate([low, low], axis=0)
    )
    lane = lax.broadcasted_iota(jnp.int32, (PART // 2, LANES), 1)
    folded[...] = jnp.where(lane < 64, both[: PART // 2], both[PART // 2 :])
    high, low = split(embed[...].astype(F32) * scale)
    placed[...] = nt(high, padded[...]) + nt(low, padded[...])


def fold(weight, patch, embed, gain):
    return pl.pallas_call(
        fold_kernel,
        out_shape=(
            jax.ShapeDtypeStruct((PART // 2, LANES), F32),
            jax.ShapeDtypeStruct((MAXF, LANES), F32),
        ),
        in_specs=[VMEM] * 4,
        out_specs=(VMEM, VMEM),
        scratch_shapes=[pltpu.VMEM((LANES, HID), BF)],
        compiler_params=pltpu.CompilerParams(vmem_limit_bytes=16 * MIB),
        cost_estimate=pl.CostEstimate(flops=400_000_000, bytes_accessed=MIB, transcendentals=0),
        name="fold",
    )(weight, patch, embed, gain)


def latent_of(summed, frame, gain, proj):
    residual = frame.astype(F32) + 0.5 * summed * (1.0 + jnp.tanh(0.5 * summed))
    mean = jnp.mean(residual * residual, axis=-1, keepdims=True)
    normed = (residual * lax.rsqrt(mean + EPSILON) * gain).astype(BF)
    return nt(normed, proj)


def in_patch(latent, row):
    lane = lax.broadcasted_iota(jnp.int32, (FRAMES, LANES), 1) // LAT
    tokens = []
    for patch in range(WIDTH // 2):
        total = jnp.zeros((FRAMES, LANES), F32)
        for side in range(2):
            column = 2 * patch + side
            block = latent[column * FRAMES : (column + 1) * FRAMES]
            total = total + jnp.where(lane == (row % 2) * 2 + side, block, 0.0)
        tokens.append(total)
    return tokens


def spread_proj(proj, copies):
    copies[...] = jnp.zeros_like(copies)
    for copy in range(4):
        copies[copy * LAT : (copy + 1) * LAT, :] = proj[...]


def by_column(row, wide, cols, lane):
    row = row.astype(F32).reshape(FRAMES * WIDTH, C)
    for piece in range(C // LANES):
        wide[piece] = row[:, piece * LANES : (piece + 1) * LANES]
    for column in range(WIDTH):
        blocks = [wide[piece, pl.ds(column, FRAMES, stride=WIDTH), :] for piece in range(C // LANES)]
        block = jnp.concatenate(blocks, axis=1).astype(BF)
        cols[column * FRAMES : (column + 1) * FRAMES, lane : lane + C] = block


def inner_kernel(
    counts, frames, weight, gain, proj, sums, own, tokens, stage, wide, cols, taps, total, copies, frame_sem, tap_sems
):
    def clip(index, start, count):
        pltpu.make_async_copy(
            frames.at[pl.ds(index * MAXF, count)], stage.at[pl.ds(start, count)], frame_sem
        ).start()

    each_clip(counts, clip)
    order = (1, 0, 2)
    loads = {}
    for side in order:
        for row in range(3):
            loads[side, row] = pltpu.make_async_copy(
                weight.at[row, side], taps.at[side, pl.ds(row * C, C)], tap_sems.at[side, row]
            )
            loads[side, row].start()
    spread_proj(proj, copies)
    pltpu.make_async_copy(stage, stage, frame_sem).wait()
    for row in range(STRIP):
        by_column(stage[:, row], wide, cols, row * C)
    for place, row in enumerate((0, STRIP - 1)):
        own[place] = cols[:, row * C : (row + 1) * C]
    count = FRAMES * WIDTH
    for side in order:
        for row in range(3):
            loads[side, row].wait()
        begin, end = max(0, side - 1) * FRAMES, count - max(0, 1 - side) * FRAMES
        shift = (1 - side) * FRAMES
        for row in range(STRIP):
            low, high = max(row - 1, 0), min(row + 2, STRIP)
            skip = low - (row - 1)
            part = dot(
                cols[begin:end, low * C : high * C],
                taps[side, skip * C : (skip + high - low) * C, :],
            )
            if side == 1:
                total[row] = part
            else:
                total[row, begin + shift : end + shift, :] += part
    sums[0] = total[0]
    sums[1] = total[STRIP - 1]
    for row in (1, 2):
        latent = latent_of(total[row], cols[:, row * C : (row + 1) * C], gain[...], copies[...])
        for patch, value in enumerate(in_patch(latent, row)):
            tokens[(row // 2) * 4 + patch] = value


def inner(counts, frames, weight, gain, proj):
    return pl.pallas_call(
        inner_kernel,
        out_shape=(
            jax.ShapeDtypeStruct((2, FRAMES * WIDTH, C), F32),
            jax.ShapeDtypeStruct((2, FRAMES * WIDTH, C), BF),
            jax.ShapeDtypeStruct((8, FRAMES, LANES), F32),
        ),
        in_specs=[SMEM, ANY, ANY, VMEM, VMEM],
        out_specs=(VMEM, VMEM, VMEM),
        scratch_shapes=[
            pltpu.VMEM((FRAMES, STRIP, WIDTH, C), BF),
            pltpu.VMEM((C // LANES, FRAMES * WIDTH, LANES), F32),
            pltpu.VMEM((FRAMES * WIDTH, STRIP * C), BF),
            pltpu.VMEM((3, 3 * C, C), BF),
            pltpu.VMEM((STRIP, FRAMES * WIDTH, C), F32),
            pltpu.VMEM((LANES, C), BF),
            pltpu.SemaphoreType.DMA,
            pltpu.SemaphoreType.DMA((3, 3)),
        ],
        compiler_params=pltpu.CompilerParams(vmem_limit_bytes=40 * MIB),
        cost_estimate=pl.CostEstimate(flops=8_000_000_000, bytes_accessed=9 * MIB, transcendentals=MIB // 2),
        name="inner",
    )(counts, frames, weight, gain, proj)


def outer_kernel(
    counts, before, after, weight, sums, own, tokens, gain, proj, folded, placed, message, wide, cols, total, copies, flat
):
    spread_proj(proj, copies)
    count = FRAMES * WIDTH
    parts = [tokens[index] for index in range(8)]
    for place, (halo, tap, row) in enumerate(((before, 0, 0), (after, 2, STRIP - 1))):
        by_column(halo[...], wide, cols, 0)
        total[...] = sums[place]
        for side in range(3):
            begin, end = max(0, side - 1) * FRAMES, count - max(0, 1 - side) * FRAMES
            shift = (1 - side) * FRAMES
            total[begin + shift : end + shift, :] += dot(cols[begin:end], weight[tap, side])
        latent = latent_of(total[...], own[place], gain[...], copies[...])
        for patch, value in enumerate(in_patch(latent, row)):
            parts[(row // 2) * 4 + patch] += value
    frame = lax.broadcasted_iota(jnp.int32, (FRAMES, 1), 0)
    begin = jnp.zeros((FRAMES, 1), jnp.int32)
    start = 0
    for clip in range(CLIPS):
        begin = jnp.where(frame >= start, start, begin)
        start = start + counts[clip]
    position = jnp.zeros((FRAMES, LANES), F32)
    for offset in range(MAXF):
        position = position + jnp.where(frame - begin == offset, placed[offset : offset + 1, :], 0.0)
    high, low = split(position)
    parts[0] = parts[0] + high.astype(F32)
    parts[1] = parts[1] + low.astype(F32)
    for index in range(8):
        flat[pl.ds(index, FRAMES, stride=8), :] = parts[index]
    rest = jnp.broadcast_to(folded[...][None], (FRAMES, PART // 2, LANES))
    message[...] = jnp.concatenate([flat[...].reshape(FRAMES, 8, LANES), rest], axis=1).astype(BF)


def outer(counts, before, after, weight, sums, own, tokens, gain, proj, folded, placed):
    return pl.pallas_call(
        outer_kernel,
        out_shape=jax.ShapeDtypeStruct((FRAMES, MESSAGE, LANES), BF),
        in_specs=[SMEM] + [VMEM] * 10,
        out_specs=VMEM,
        scratch_shapes=[
            pltpu.VMEM((C // LANES, FRAMES * WIDTH, LANES), F32),
            pltpu.VMEM((FRAMES * WIDTH, C), BF),
            pltpu.VMEM((FRAMES * WIDTH, C), F32),
            pltpu.VMEM((LANES, C), BF),
            pltpu.VMEM((TOKENS, LANES), F32),
        ],
        compiler_params=pltpu.CompilerParams(vmem_limit_bytes=32 * MIB),
        cost_estimate=pl.CostEstimate(flops=1_700_000_000, bytes_accessed=7 * MIB, transcendentals=MIB // 2),
        name="outer",
    )(counts, before, after, weight, sums, own, tokens, gain, proj, folded, placed)


BLOCK = 4


def project_kernel(counts, index, arrived, patch, embed, spread, out, flat, query, scale, columns, shift):
    @pl.when(pl.program_id(0) == 0)
    def _():
        got = arrived[...].astype(F32)
        flat[...] = got[:, 0:8].reshape(TOKENS, LANES)
        lane = lax.broadcasted_iota(jnp.int32, (TOKENS, LANES), 1)
        token = jnp.where(lane < 64, flat[...], 0.0)
        query[...] = (token + pltpu.roll(token, 64, 1)).astype(BF)
        rest = got[:, 8:MESSAGE]
        lane = lax.broadcasted_iota(jnp.int32, rest.shape, 2)
        low, high = jnp.where(lane < 64, rest, 0.0), jnp.where(lane < 64, 0.0, rest)
        columns[...] = jnp.concatenate([low, high], axis=1).reshape(HID, LANES).astype(BF)
        lane = lax.broadcasted_iota(jnp.int32, (FRAMES, HID), 1)
        line = lax.broadcasted_iota(jnp.int32, (FRAMES, HID), 0) * PART
        sums = jnp.zeros((FRAMES, HID), F32)
        for row in range(2):
            sums = sums + dot(flat[pl.ds(row, FRAMES, stride=8), :].astype(BF), spread[...])
        shift[...] = jnp.sum(
            jnp.where((lane >= line) & (lane < line + PART), sums, 0.0), axis=0, keepdims=True
        )

        def clip(at, carry):
            start, begin = carry
            begin = jnp.where(start <= index[0], start, begin)
            return start + counts[at], begin

        _, begin = lax.fori_loop(0, CLIPS, clip, (0, 0))
        line = lax.broadcasted_iota(jnp.int32, (MAXF, HID), 0)
        position = jnp.sum(
            jnp.where(line == index[0] - begin, embed[...].astype(F32), 0.0), axis=0, keepdims=True
        )
        squares = jnp.zeros((TOKENS, LANES), F32)
        for block in range(HID // C):
            part = slice(block * C, (block + 1) * C)
            value = dot(query[:, 0:64], patch[:, part]) + position[:, part]
            value = value * value
            for piece in range(C // LANES):
                squares = squares + value[:, piece * LANES : (piece + 1) * LANES]
        mean = jnp.sum(squares, axis=-1, keepdims=True) * (1.0 / HID)
        scale[...] = jnp.broadcast_to(lax.rsqrt(mean + EPSILON), (TOKENS, LANES))

    step = pl.program_id(0)
    for head in range(BLOCK):
        at = pl.multiple_of((step * BLOCK + head) * HEAD_DIM, HEAD_DIM)
        value = nt(query[...], columns[pl.ds(at, HEAD_DIM), :]) + shift[:, pl.ds(at, HEAD_DIM)]
        out[head] = (value * scale[...]).astype(BF)


def project(counts, index, arrived, patch, embed, spread):
    def whole(*shape):
        return pl.BlockSpec(shape, lambda step: (0,) * len(shape))

    return pl.pallas_call(
        project_kernel,
        out_shape=jax.ShapeDtypeStruct((HEADS, TOKENS, HEAD_DIM), BF),
        grid=(HEADS // BLOCK,),
        in_specs=[
            SMEM,
            SMEM,
            whole(FRAMES, MESSAGE, LANES),
            whole(64, HID),
            whole(MAXF, HID),
            whole(LANES, HID),
        ],
        out_specs=pl.BlockSpec((BLOCK, TOKENS, HEAD_DIM), lambda step: (step, 0, 0)),
        scratch_shapes=[
            pltpu.VMEM((TOKENS, LANES), F32),
            pltpu.VMEM((TOKENS, LANES), BF),
            pltpu.VMEM((TOKENS, LANES), F32),
            pltpu.VMEM((HID, LANES), BF),
            pltpu.VMEM((1, HID), F32),
        ],
        compiler_params=pltpu.CompilerParams(vmem_limit_bytes=32 * MIB),
        cost_estimate=pl.CostEstimate(flops=800_000_000, bytes_accessed=5 * MIB, transcendentals=0),
        name="project",
    )(counts, index, arrived, patch, embed, spread)


def spread_table():
    table = np.zeros((LANES, HID), np.float32)
    for column in range(HID):
        table[64 + column % PART, column] = 1.0
    return table


def local(
    frame_rows,
    frame_counts,
    conv_weight,
    norm_gain,
    latent_proj,
    patch_weight,
    frame_embed,
    query_gain,
    query_weight,
):
    devices = lax.axis_size("cp")
    up = [(i, i + 1) for i in range(devices - 1)]
    down = [(j, i) for i, j in up]
    first, last = edges(frame_counts, frame_rows)
    before = lax.ppermute(last, "cp", up)
    after = lax.ppermute(first, "cp", down)
    gain = norm_gain[None, :]
    folded, placed = fold(query_weight.T, patch_weight, frame_embed, query_gain[None, :])
    sums, own, tokens = inner(frame_counts, frame_rows, conv_weight, gain, latent_proj.T)
    message = outer(
        frame_counts, before, after, conv_weight, sums, own, tokens, gain, latent_proj.T, folded, placed
    )
    arrived = lax.all_to_all(message, "cp", split_axis=0, concat_axis=0, tiled=True)
    index = lax.axis_index("cp").astype(jnp.int32)[None]
    spread = jnp.asarray(spread_table(), BF)
    return project(frame_counts, index, arrived, patch_weight, frame_embed, spread)


def solution(mesh):
    return jax.shard_map(
        local,
        mesh=mesh,
        in_specs=(P("dp", "cp", None, None), P("dp"), P(), P(), P(), P(), P(), P(), P(None, "cp")),
        out_specs=P(None, ("dp", "cp"), None),
        check_vma=False,
    )
```

time: 269 us -> 95.7 us (0.36)
  blocking collectives: 193 us -> 0 us
  Pallas kernels: 0 us -> 58.5 us
  matrix products: 34.8 us -> 0 us
  other arithmetic: 7.73 us -> 0 us
  starting transfers between devices: 10.3 us -> 17.3 us
  local copies, waits for them, and re-layouts: 12.6 us -> 6.54 us
  waiting for transfers between devices: 9.48 us -> 12.7 us
    all_gather x1 -> x0, blocking collectives: 193 us -> none  [local(): folded = lax.all_gather(folded.astype(BF), 'cp', axis=0, tiled=True)]
    pallas_call x0 -> x5, Pallas kernels: none -> 58.5 us  [the longest x1 33.7 us: edges(): pl.pallas_call(edges_kernel, out_shape=(shape, shape), in_specs=[SMEM, AN...]
    conv_general_dilated x1 -> x0, matrix products: 24.9 us -> none  [local(): lax.conv_general_dilated(padded, conv_weight, (1, 1), ((0, 0), (1, 1)), d...]
    dot_general x5 -> x0, matrix products: 9.84 us -> none  [the longest x1 2.7 us: local(): lax.dot_general(by_head, full, (((2,), (1,)), ((), ())), preferred_elemen...]
    all_to_all x1, starting transfers between devices: 4.62 us -> 12.5 us  [local(): lax.all_to_all(message, 'cp', split_axis=0, concat_axis=0, tiled=True)]
    unnamed x14 -> x24, local copies, waits for them, and re-layouts: 1.56 us -> 6.54 us
    convert_element_type x1 -> x0, local copies, waits for them, and re-layouts: 4.63 us -> none  [local(): return projected.astype(BF)]
    select_n x2 -> x0, other arithmetic: 4.04 us -> none  [local(): frames = jnp.take(frame_rows, slot_index, axis=0)]
  transfers between devices with their start and end apart: 3 -> 3, of which waited for: 1 -> 1; matrix products, arithmetic and copies ran while one was open for 2% -> 0% of each run, Pallas kernels for 0% -> 15%
where the time goes in v2:
time: 95.7 us; the launch traced here: 95.3 us
  Pallas kernels  58.5 us (61%)
  starting transfers between devices  17.3 us (18%)
  waiting for transfers between devices  12.7 us (13%)
  local copies, waits for them, and re-layouts  6.54 us (7%)
    pallas_call x1, Pallas kernels, edges(): pl.pallas_call(edges_kernel, out_shape=(shape, shape), in_specs=[SMEM, AN...  33.7 us
    pallas_call x1, Pallas kernels, inner(): pl.pallas_call(inner_kernel, out_shape=(jax.ShapeDtypeStruct((2, FRAMES *...  13.8 us
    all_to_all x1, waiting for transfers between devices, local(): lax.all_to_all(message, 'cp', split_axis=0, concat_axis=0, tiled=True)  12.7 us
    all_to_all x1, starting transfers between devices, local(): lax.all_to_all(message, 'cp', split_axis=0, concat_axis=0, tiled=True)  12.5 us
    unnamed x24, local copies, waits for them, and re-layouts  6.54 us
    pallas_call x1, Pallas kernels, project(): pl.pallas_call(project_kernel, out_shape=jax.ShapeDtypeStruct((HEADS, TOK...  6.02 us
    pallas_call x1, Pallas kernels, outer(): pl.pallas_call(outer_kernel, out_shape=jax.ShapeDtypeStruct((FRAMES, MESS...  4.1 us
    ppermute x1, starting transfers between devices, local(): before = lax.ppermute(last, 'cp', up)  3.6 us
  transfers between devices with their start and end apart: 3, of which 1 were waited for; matrix products, arithmetic and copies ran while one was open for 0% of the time, Pallas kernels for 15%

profile of v2, /device:TPU:0, one launch (start us, length us, event | category | flops | bytes accessed | tf_op | source)
XLA Modules:
  0.0 95.3 jit_solution(6774010191088127748)
XLA Ops:
  0.0 0.0 copy-start.1
  0.0 0.0 copy-start.8
  0.0 0.0 copy-start.9
  0.0 33.7 %edges.1 = (bf16[64,8,512]{2,1,0:T(8,128)(2,1)}, bf16[64,8,512]{2,1,0:T(8,128)(2,1)}) custom-call(s32[16]{0:T(128)} %counts.7, bf16[96,4,8,512]{3,2,1,0:T(8,128)(2,1)} %frames.3), custom_call_target="tpu_custom_call" | custom-call | bytes 2097152 | tf_op jit(solution)/shard_map/edges/pallas_call | solution.py:69
  33.7 3.6 %collective-permute-start = (bf16[64,8,512]{2,1,0:T(8,128)(2,1)}, bf16[64,8,512]{2,1,0:T(8,128)(2,1)S(1)}, u32[]{:S(2)}, u32[]{:S(2)}) collective-permute-start(bf16[64,8,512]{2,1,0:T(8,128)(2,1)} %get-tuple-element.12), channel_id=1, source_target_pairs={{0,2},{2,4},{4,6},{6,8},{8,10},{10,12},{12,14},{14,16},{16,18},{18... | collective-permute-start | bytes 1572872 | tf_op jit(solution)/shard_map/ppermute | solution.py:376
  37.3 1.3 %collective-permute-start.1 = (bf16[64,8,512]{2,1,0:T(8,128)(2,1)}, bf16[64,8,512]{2,1,0:T(8,128)(2,1)S(1)}, u32[]{:S(2)}, u32[]{:S(2)}) collective-permute-start(bf16[64,8,512]{2,1,0:T(8,128)(2,1)} %get-tuple-element.13), channel_id=1, source_target_pairs={{2,0},{4,2},{6,4},{8,6},{10,8},{12,10},{14,12},{16,14},{18,16},{20... | collective-permute-start | bytes 1572872 | tf_op jit(solution)/shard_map/ppermute | solution.py:377
  38.6 0.0 copy-start.3
  38.6 1.0 %copy-done.3 = bf16[64,3072]{1,0:T(8,128)(2,1)S(1)} copy-done((bf16[64,3072]{1,0:T(8,128)(2,1)S(1)}, bf16[64,3072]{1,0:T(8,128)(2,1)}, u32[]{:S(2)}) %copy-start.3) | copy-done | bytes 393240
  39.6 0.0 copy-start.5
  39.6 0.8 copy-done.5
  40.4 0.0 copy-start.10
  40.4 1.0 %copy-done.10 = bf16[3072,48]{0,1:T(8,128)(2,1)S(1)} copy-done((bf16[3072,48]{0,1:T(8,128)(2,1)S(1)}, bf16[3072,48]{0,1:T(8,128)(2,1)}, u32[]{:S(2)}) %copy-start.10) | copy-done | bytes 294936
  41.4 0.0 copy-start.11
  41.4 0.7 copy-done.11
  42.1 0.9 fold.1
  43.0 0.0 copy-done.1
  43.0 0.0 copy-done.8
  43.0 0.0 copy-done.9
  43.1 0.0 copy-start
  43.1 2.3 %copy-done = bf16[3,3,512,512]{3,2,1,0:T(8,128)(2,1)S(1)} copy-done((bf16[3,3,512,512]{3,2,1,0:T(8,128)(2,1)S(1)}, bf16[3,3,512,512]{3,2,1,0:T(8,128)(2,1)}, u32[]{:S(2)}) %copy-start) | copy-done | bytes 4718616
  45.4 0.0 copy-start.7
  45.4 0.7 copy-done.7
  46.1 13.8 %inner.1 = (f32[2,512,512]{2,1,0:T(8,128)S(1)}, bf16[2,512,512]{2,1,0:T(8,128)(2,1)S(1)}, f32[8,64,128]{2,1,0:T(8,128)S(1)}) custom-call(s32[16]{0:T(128)S(1)} %copy-done.8, bf16[96,4,8,512]{3,2,1,0:T(8,128)(2,1)S(1)} %copy-done.1, bf16[3,3,512,512]{3,2,1,0:T(8,128)(2,1)S(1)} %copy-done, f32[1,512]{1,0:T(1,128)S(1)} %bitcast.7, bf16[16,512]{1,0:T(8,128)(2,1)S(1)} %bitcast.5), custom_call_target="tpu_custom_call" | custom-call | flops 8000000000 | bytes 9437184 | tf_op jit(solution)/shard_map/inner/pallas_call | solution.py:195
  59.9 0.0 collective-permute-done.before
  59.9 0.0 collective-permute-done.1.after
  59.9 0.0 copy-start.2
  59.9 0.0 copy-start.4
  60.0 0.0 copy-start.6
  60.0 4.1 %outer.1 = bf16[64,32,128]{2,1,0:T(8,128)(2,1)} custom-call(s32[16]{0:T(128)S(1)} %copy-done.8, bf16[64,8,512]{2,1,0:T(8,128)(2,1)S(1)} %collective-permute-done.before, bf16[64,8,512]{2,1,0:T(8,128)(2,1)S(1)} %collective-permute-done.1.after, bf16[3,3,512,512]{3,2,1,0:T(8,128)(2,1)S(1)} %copy-done, f32[2,512,512]{2,1,0:T(8,128)S(1)} %get-tuple-element.14.sums, ...), custom_call_target="tpu_custom_call" | custom-call | flops 1700000000 | bytes 7340032 | tf_op jit(solution)/shard_map/outer/pallas_call | solution.py:255
  64.1 12.5 %all-to-all-start = ((bf16[64,32,128]{2,1,0:T(8,128)(2,1)}), bf16[64,32,128]{2,1,0:T(8,128)(2,1)S(1)}, u32[]{:S(2)}, u32[]{:S(2)}) async-start(bf16[64,32,128]{2,1,0:T(8,128)(2,1)} %outer.1), calls=%async_computation | async-start | bytes 1048576 | tf_op jit(solution)/shard_map/all_to_all | solution.py:384
  76.5 12.7 %all-to-all-done.arrived = bf16[64,32,128]{2,1,0:T(8,128)(2,1)S(1)} async-done(((bf16[64,32,128]{2,1,0:T(8,128)(2,1)}), bf16[64,32,128]{2,1,0:T(8,128)(2,1)S(1)}, u32[]{:S(2)}, u32[]{:S(2)}) %all-to-all-start) | async-done | bytes 524320 | tf_op jit(solution)/shard_map/all_to_all | solution.py:384
  89.2 0.0 copy-done.2
  89.2 0.0 copy-done.4
  89.2 0.0 copy-done.6
  89.2 6.0 %project.1 = bf16[24,512,128]{2,1,0:T(8,128)(2,1)} custom-call(s32[16]{0:T(128)S(1)} %copy-done.8, s32[1]{0:T(128)} %bitcast.index, bf16[64,32,128]{2,1,0:T(8,128)(2,1)S(1)} %all-to-all-done.arrived, bf16[64,3072]{1,0:T(8,128)(2,1)S(1)} %copy-done.4, bf16[6,3072]{1,0:T(8,128)(2,1)S(1)} %copy-done.6, bf16[128,3072]{1,0:T(8,128)(2,1)S(1)} %copy-done.2), custom_call_target="tpu_custom_call" | custom-call | flops 800000000 | bytes 5242880 | tf_op jit(solution)/shard_map/project/pallas_call | solution.py:328
Async XLA Ops:
  0.0 43.0 %copy-start.1 = (bf16[96,4,8,512]{3,2,1,0:T(8,128)(2,1)S(1)}, bf16[96,4,8,512]{3,2,1,0:T(8,128)(2,1)}, u32[]{:S(2)}) copy-start(bf16[96,4,8,512]{3,2,1,0:T(8,128)(2,1)} %frames.3) | copy-start | bytes 9437188
  0.0 43.0 %copy-start.8 = (s32[16]{0:T(128)S(1)}, s32[16]{0:T(128)}, u32[]{:S(2)}) copy-start(s32[16]{0:T(128)} %counts.7) | copy-start | bytes 196
  0.0 43.0 %copy-start.9 = (f32[512]{0:T(512)S(1)}, f32[512]{0:T(512)}, u32[]{:S(2)}) copy-start(f32[512]{0:T(512)} %param.13) | copy-start | bytes 6148
  33.7 26.2 %collective-permute-start = (bf16[64,8,512]{2,1,0:T(8,128)(2,1)}, bf16[64,8,512]{2,1,0:T(8,128)(2,1)S(1)}, u32[]{:S(2)}, u32[]{:S(2)}) collective-permute-start(bf16[64,8,512]{2,1,0:T(8,128)(2,1)} %get-tuple-element.12), channel_id=1, source_target_pairs={{0,2},{2,4},{4,6},{6,8},{8,10},{10,12},{12,14},{14,16},{16,18},{18... | collective-permute-start | bytes 1572872 | tf_op jit(solution)/shard_map/ppermute | solution.py:376
  37.3 22.6 %collective-permute-start.1 = (bf16[64,8,512]{2,1,0:T(8,128)(2,1)}, bf16[64,8,512]{2,1,0:T(8,128)(2,1)S(1)}, u32[]{:S(2)}, u32[]{:S(2)}) collective-permute-start(bf16[64,8,512]{2,1,0:T(8,128)(2,1)} %get-tuple-element.13), channel_id=1, source_target_pairs={{2,0},{4,2},{6,4},{8,6},{10,8},{12,10},{14,12},{16,14},{18,16},{20... | collective-permute-start | bytes 1572872 | tf_op jit(solution)/shard_map/ppermute | solution.py:377
  38.6 1.0 %copy-start.3 = (bf16[64,3072]{1,0:T(8,128)(2,1)S(1)}, bf16[64,3072]{1,0:T(8,128)(2,1)}, u32[]{:S(2)}) copy-start(bf16[64,3072]{1,0:T(8,128)(2,1)} %patch.3) | copy-start | bytes 1179652
  39.6 0.8 copy-start.5
  40.4 1.0 %copy-start.10 = (bf16[3072,48]{0,1:T(8,128)(2,1)S(1)}, bf16[3072,48]{0,1:T(8,128)(2,1)}, u32[]{:S(2)}) copy-start(bf16[3072,48]{0,1:T(8,128)(2,1)} %param.18) | copy-start | bytes 884740
  41.4 0.7 copy-start.11
  43.1 2.3 %copy-start = (bf16[3,3,512,512]{3,2,1,0:T(8,128)(2,1)S(1)}, bf16[3,3,512,512]{3,2,1,0:T(8,128)(2,1)}, u32[]{:S(2)}) copy-start(bf16[3,3,512,512]{3,2,1,0:T(8,128)(2,1)} %weight.3) | copy-start | bytes 14155780
  45.4 0.7 copy-start.7
  59.9 29.3 %copy-start.2 = (bf16[128,3072]{1,0:T(8,128)(2,1)S(1)}, bf16[128,3072]{1,0:T(8,128)(2,1)}, u32[]{:S(2)}) copy-start(bf16[128,3072]{1,0:T(8,128)(2,1)} %constant.8.clone.spread) | copy-start | bytes 2359300
  59.9 29.3 %copy-start.4 = (bf16[64,3072]{1,0:T(8,128)(2,1)S(1)}, bf16[64,3072]{1,0:T(8,128)(2,1)}, u32[]{:S(2)}) copy-start(bf16[64,3072]{1,0:T(8,128)(2,1)} %patch.3) | copy-start | bytes 1179652
  60.0 29.3 %copy-start.6 = (bf16[6,3072]{1,0:T(8,128)(2,1)S(1)}, bf16[6,3072]{1,0:T(8,128)(2,1)}, u32[]{:S(2)}) copy-start(bf16[6,3072]{1,0:T(8,128)(2,1)} %embed.3) | copy-start | bytes 110596
  64.1 25.2 %all-to-all-start = ((bf16[64,32,128]{2,1,0:T(8,128)(2,1)}), bf16[64,32,128]{2,1,0:T(8,128)(2,1)S(1)}, u32[]{:S(2)}, u32[]{:S(2)}) async-start(bf16[64,32,128]{2,1,0:T(8,128)(2,1)} %outer.1), calls=%async_computation | async-start | bytes 1048576 | tf_op jit(solution)/shard_map/all_to_all | solution.py:384

commit v3 on v2

v3 whole, which is shorter than its diff:
```python
import functools

import jax
import jax.numpy as jnp
import numpy as np
from jax import lax
from jax.experimental import pallas as pl
from jax.experimental.pallas import tpu as pltpu
from jax.sharding import PartitionSpec as P

LAT = 16
HID = 3072
HEAD_DIM = 128
HEADS = HID // HEAD_DIM
MAXF = 6
C = 512
WIDTH = 8
STRIP = 4
FRAMES = 64
CLIPS = 16
PART = HID // FRAMES
TOKENS = 512
LANES = 128
MESSAGE = 32
EPSILON = 1e-06
BF = jnp.bfloat16
F32 = jnp.float32
VMEM = pl.BlockSpec(memory_space=pltpu.VMEM)
SMEM = pl.BlockSpec(memory_space=pltpu.SMEM)
HBM = pl.BlockSpec(memory_space=pltpu.HBM)
MIB = 1 << 20


def in_hbm(value):
    return pltpu.with_memory_space_constraint(value, pltpu.HBM)


def nt(left, right):
    return lax.dot_general(left, right, (((1,), (1,)), ((), ())), preferred_element_type=F32)


def dot(left, right):
    return jnp.dot(left, right, preferred_element_type=F32)


def split(value):
    high = value.astype(BF)
    return high, (value - high.astype(F32)).astype(BF)


def each_clip(counts, body):
    def step(clip, start):
        body(clip, start, counts[clip])
        return start + counts[clip]

    lax.fori_loop(0, CLIPS, step, 0)


def edges_kernel(counts, index, frames, odd_pair, even_pair, sems):
    low = (index[0] % 2) * (STRIP - 1)

    def clip(at, start, count):
        for row, target, sem in ((low, odd_pair, 0), (STRIP - 1 - low, even_pair, 1)):
            pltpu.make_async_copy(
                frames.at[pl.ds(at * MAXF, count), row], target.at[pl.ds(start, count)], sems.at[sem]
            ).start()

    each_clip(counts, clip)
    pltpu.make_async_copy(odd_pair, odd_pair, sems.at[0]).wait()
    pltpu.make_async_copy(even_pair, even_pair, sems.at[1]).wait()


def edges(counts, index, frames):
    shape = jax.ShapeDtypeStruct((FRAMES, WIDTH, C), BF)
    return pl.pallas_call(
        edges_kernel,
        out_shape=(shape, shape),
        in_specs=[SMEM, SMEM, HBM],
        out_specs=(VMEM, VMEM),
        scratch_shapes=[pltpu.SemaphoreType.DMA((2,))],
        cost_estimate=pl.CostEstimate(flops=0, bytes_accessed=2 * MIB, transcendentals=0),
        name="edges",
    )(counts, index, in_hbm(frames))


def latent_of(summed, frame, gain, proj):
    residual = frame.astype(F32) + 0.5 * summed * (1.0 + jnp.tanh(0.5 * summed))
    mean = jnp.mean(residual * residual, axis=-1, keepdims=True)
    normed = (residual * lax.rsqrt(mean + EPSILON) * gain).astype(BF)
    return nt(normed, proj)


def in_patch(latent, row):
    lane = lax.broadcasted_iota(jnp.int32, (FRAMES, LANES), 1) // LAT
    tokens = []
    for patch in range(WIDTH // 2):
        total = jnp.zeros((FRAMES, LANES), F32)
        for side in range(2):
            column = 2 * patch + side
            block = latent[column * FRAMES : (column + 1) * FRAMES]
            total = total + jnp.where(lane == (row % 2) * 2 + side, block, 0.0)
        tokens.append(total)
    return tokens


def spread_proj(proj, copies):
    copies[...] = jnp.zeros_like(copies)
    for copy in range(4):
        copies[copy * LAT : (copy + 1) * LAT, :] = proj[...]


def by_column(row, wide, cols, lane):
    row = row.astype(F32).reshape(FRAMES * WIDTH, C)
    for piece in range(C // LANES):
        wide[piece] = row[:, piece * LANES : (piece + 1) * LANES]
    for column in range(WIDTH):
        blocks = [wide[piece, pl.ds(column, FRAMES, stride=WIDTH), :] for piece in range(C // LANES)]
        block = jnp.concatenate(blocks, axis=1).astype(BF)
        cols[column * FRAMES : (column + 1) * FRAMES, lane : lane + C] = block


def fold(weight, table, scale, padded, folded, placed, gram):
    padded[...] = jnp.zeros_like(padded)
    padded[64 : 64 + PART, :] = weight[...]
    high, low = split(table[...].astype(F32) * scale)
    both = nt(weight[...], jnp.concatenate([high[:64], high[:64]], axis=0))
    both = both + nt(weight[...], jnp.concatenate([low[:64], low[:64]], axis=0))
    lane = lax.broadcasted_iota(jnp.int32, (PART // 2, LANES), 1)
    folded[...] = jnp.where(lane < 64, both[: PART // 2], both[PART // 2 :])
    placed[...] = nt(high[64:], padded[...]) + nt(low[64:], padded[...])
    gram[...] = nt(table[...], table[...])


def inner_kernel(
    counts,
    frames,
    weight,
    gain,
    proj,
    columns,
    patch,
    embed,
    scale,
    sums,
    own,
    tokens,
    taps,
    copies,
    norm,
    folded,
    placed,
    gram,
    stage,
    wide,
    cols,
    total,
    projs,
    held,
    table,
    embeds,
    gains,
    padded,
    sems,
    tap_sems,
):
    small = [
        pltpu.make_async_copy(source, target, sems.at[place])
        for place, (source, target) in enumerate(
            (
                (columns, held),
                (patch, table.at[pl.ds(0, 64)]),
                (embed, embeds),
                (scale, gains),
                (proj, projs),
                (gain, norm),
            )
        )
    ]
    for copy in small:
        copy.start()

    def clip(index, start, count):
        pltpu.make_async_copy(
            frames.at[pl.ds(index * MAXF, count)], stage.at[pl.ds(start, count)], sems.at[6]
        ).start()

    each_clip(counts, clip)
    order = (1, 0, 2)
    loads = {}
    for side in order:
        for row in range(3):
            loads[side, row] = pltpu.make_async_copy(
                weight.at[row, side], taps.at[side, pl.ds(row * C, C)], tap_sems.at[side, row]
            )
            loads[side, row].start()
    for copy in small:
        copy.wait()
    spread_proj(projs, copies)
    table[64:80, :] = jnp.concatenate(
        [embeds[...].astype(F32), jnp.zeros((16 - MAXF, HID), F32)], axis=0
    ).astype(BF)
    fold(held, table, gains[...], padded, folded, placed, gram)
    pltpu.make_async_copy(stage, stage, sems.at[6]).wait()
    for row in range(STRIP):
        by_column(stage[:, row], wide.at[row], cols, row * C)
    for place, row in enumerate((0, STRIP - 1)):
        own[place] = cols[:, row * C : (row + 1) * C]
    count = FRAMES * WIDTH
    for side in order:
        for row in range(3):
            loads[side, row].wait()
        begin, end = max(0, side - 1) * FRAMES, count - max(0, 1 - side) * FRAMES
        shift = (1 - side) * FRAMES
        for row in range(STRIP):
            low, high = max(row - 1, 0), min(row + 2, STRIP)
            skip = low - (row - 1)
            part = dot(
                cols[begin:end, low * C : high * C],
                taps[side, skip * C : (skip + high - low) * C, :],
            )
            if side == 1:
                total[row] = part
            else:
                total[row, begin + shift : end + shift, :] += part
    sums[0] = total[0]
    sums[1] = total[STRIP - 1]
    for row in (1, 2):
        latent = latent_of(total[row], cols[:, row * C : (row + 1) * C], norm[...], copies[...])
        for patch_index, value in enumerate(in_patch(latent, row)):
            tokens[(row // 2) * 4 + patch_index] = value


def inner(counts, frames, weight, gain, proj, columns, patch, embed, scale):
    return pl.pallas_call(
        inner_kernel,
        out_shape=(
            jax.ShapeDtypeStruct((2, FRAMES * WIDTH, C), F32),
            jax.ShapeDtypeStruct((2, FRAMES * WIDTH, C), BF),
            jax.ShapeDtypeStruct((8, FRAMES, LANES), F32),
            jax.ShapeDtypeStruct((3, 3 * C, C), BF),
            jax.ShapeDtypeStruct((LANES, C), BF),
            jax.ShapeDtypeStruct((1, C), F32),
            jax.ShapeDtypeStruct((PART // 2, LANES), F32),
            jax.ShapeDtypeStruct((16, LANES), F32),
            jax.ShapeDtypeStruct((80, 80), F32),
        ),
        in_specs=[SMEM] + [HBM] * 8,
        out_specs=(VMEM,) * 9,
        scratch_shapes=[
            pltpu.VMEM((FRAMES, STRIP, WIDTH, C), BF),
            pltpu.VMEM((STRIP, C // LANES, FRAMES * WIDTH, LANES), F32),
            pltpu.VMEM((FRAMES * WIDTH, STRIP * C), BF),
            pltpu.VMEM((STRIP, FRAMES * WIDTH, C), F32),
            pltpu.VMEM((LAT, C), BF),
            pltpu.VMEM((PART, HID), BF),
            pltpu.VMEM((80, HID), BF),
            pltpu.VMEM((MAXF, HID), BF),
            pltpu.VMEM((1, HID), F32),
            pltpu.VMEM((LANES, HID), BF),
            pltpu.SemaphoreType.DMA((7,)),
            pltpu.SemaphoreType.DMA((3, 3)),
        ],
        compiler_params=pltpu.CompilerParams(vmem_limit_bytes=36 * MIB),
        cost_estimate=pl.CostEstimate(flops=8_000_000_000, bytes_accessed=9 * MIB, transcendentals=MIB // 2),
        name="inner",
    )(counts, *map(in_hbm, (frames, weight, gain, proj, columns, patch, embed, scale)))


def outer_kernel(
    counts, index, odd_pair, even_pair, taps, sums, own, tokens, copies, gain, folded, placed, message, wide, cols, total, flat
):
    count = FRAMES * WIDTH
    parts = [tokens[index] for index in range(8)]
    odd = index[0] % 2 == 1
    for place, (tap, row) in enumerate(((0, 0), (2, STRIP - 1))):
        ours, other = (even_pair, odd_pair) if place == 0 else (odd_pair, even_pair)
        by_column(jnp.where(odd, ours[...], other[...]), wide, cols, 0)
        total[...] = sums[place]
        for side in range(3):
            begin, end = max(0, side - 1) * FRAMES, count - max(0, 1 - side) * FRAMES
            shift = (1 - side) * FRAMES
            total[begin + shift : end + shift, :] += dot(cols[begin:end], taps[side, tap * C : (tap + 1) * C, :])
        latent = latent_of(total[...], own[place], gain[...], copies[...])
        for patch, value in enumerate(in_patch(latent, row)):
            parts[(row // 2) * 4 + patch] += value
    frame = lax.broadcasted_iota(jnp.int32, (FRAMES, 1), 0)
    begin = jnp.zeros((FRAMES, 1), jnp.int32)
    start = 0
    for clip in range(CLIPS):
        begin = jnp.where(frame >= start, start, begin)
        start = start + counts[clip]
    position = jnp.zeros((FRAMES, LANES), F32)
    for offset in range(MAXF):
        position = position + jnp.where(frame - begin == offset, placed[offset : offset + 1, :], 0.0)
    high, low = split(position)
    parts[0] = parts[0] + high.astype(F32)
    parts[1] = parts[1] + low.astype(F32)
    for index in range(8):
        flat[pl.ds(index, FRAMES, stride=8), :] = parts[index]
    rest = jnp.broadcast_to(folded[...][None], (FRAMES, PART // 2, LANES))
    message[...] = jnp.concatenate([flat[...].reshape(FRAMES, 8, LANES), rest], axis=1).astype(BF)


def outer(counts, index, odd_pair, even_pair, taps, sums, own, tokens, copies, gain, folded, placed):
    return pl.pallas_call(
        outer_kernel,
        out_shape=jax.ShapeDtypeStruct((FRAMES, MESSAGE, LANES), BF),
        in_specs=[SMEM, SMEM] + [VMEM] * 10,
        out_specs=VMEM,
        scratch_shapes=[
            pltpu.VMEM((C // LANES, FRAMES * WIDTH, LANES), F32),
            pltpu.VMEM((FRAMES * WIDTH, C), BF),
            pltpu.VMEM((FRAMES * WIDTH, C), F32),
            pltpu.VMEM((TOKENS, LANES), F32),
        ],
        compiler_params=pltpu.CompilerParams(vmem_limit_bytes=32 * MIB),
        cost_estimate=pl.CostEstimate(flops=1_700_000_000, bytes_accessed=7 * MIB, transcendentals=MIB // 2),
        name="outer",
    )(counts, index, odd_pair, even_pair, taps, sums, own, tokens, copies, gain, folded, placed)


BLOCK = 4


def project_kernel(counts, index, arrived, gram, spread, out, flat, query, scale, columns, shift):
    @pl.when(pl.program_id(0) == 0)
    def _():
        got = arrived[...].astype(F32)
        flat[...] = got[:, 0:8].reshape(TOKENS, LANES)
        lane = lax.broadcasted_iota(jnp.int32, (TOKENS, LANES), 1)
        token = jnp.where(lane < 64, flat[...], 0.0)
        query[...] = (token + pltpu.roll(token, 64, 1)).astype(BF)
        rest = got[:, 8:MESSAGE]
        lane = lax.broadcasted_iota(jnp.int32, rest.shape, 2)
        low, high = jnp.where(lane < 64, rest, 0.0), jnp.where(lane < 64, 0.0, rest)
        columns[...] = jnp.concatenate([low, high], axis=1).reshape(HID, LANES).astype(BF)
        lane = lax.broadcasted_iota(jnp.int32, (FRAMES, HID), 1)
        line = lax.broadcasted_iota(jnp.int32, (FRAMES, HID), 0) * PART
        sums = jnp.zeros((FRAMES, HID), F32)
        for row in range(2):
            piece = pltpu.roll(flat[pl.ds(row, FRAMES, stride=8), :], 64, 1)
            sums = sums + dot(piece[:, 0:64].astype(BF), spread[...])
        shift[...] = jnp.sum(
            jnp.where((lane >= line) & (lane < line + PART), sums, 0.0), axis=0, keepdims=True
        )

        def clip(at, carry):
            start, begin = carry
            begin = jnp.where(start <= index[0], start, begin)
            return start + counts[at], begin

        _, begin = lax.fori_loop(0, CLIPS, clip, (0, 0))
        matrix = gram[...]
        line = lax.broadcasted_iota(jnp.int32, (16, 80), 0)
        position = jnp.sum(jnp.where(line == index[0] - begin, matrix[64:], 0.0), axis=0, keepdims=True)
        lane = lax.broadcasted_iota(jnp.int32, (1, 80), 1)
        square = jnp.sum(jnp.where(lane == 64 + index[0] - begin, position, 0.0), axis=1, keepdims=True)
        token = token[:, 0:64]
        total = jnp.zeros((TOKENS, 64), F32) + 2.0 * position[:, 0:64]
        matrix = matrix[:64, :64]
        for _ in range(3):
            piece = matrix.astype(BF)
            total = total + dot(token.astype(BF), piece)
            matrix = matrix - piece.astype(F32)
        total = jnp.sum(total * token, axis=-1, keepdims=True) + square
        mean = jnp.maximum(total, 0.0) * (1.0 / HID)
        scale[...] = jnp.broadcast_to(lax.rsqrt(mean + EPSILON), (TOKENS, LANES))

    step = pl.program_id(0)
    for head in range(BLOCK):
        at = pl.multiple_of((step * BLOCK + head) * HEAD_DIM, HEAD_DIM)
        value = nt(query[...], columns[pl.ds(at, HEAD_DIM), :]) + shift[:, pl.ds(at, HEAD_DIM)]
        out[head] = (value * scale[...]).astype(BF)


def project(counts, index, arrived, gram, spread):
    return pl.pallas_call(
        project_kernel,
        out_shape=jax.ShapeDtypeStruct((HEADS, TOKENS, HEAD_DIM), BF),
        grid=(HEADS // BLOCK,),
        in_specs=[SMEM, SMEM, VMEM, VMEM, VMEM],
        out_specs=pl.BlockSpec((BLOCK, TOKENS, HEAD_DIM), lambda step: (step, 0, 0)),
        scratch_shapes=[
            pltpu.VMEM((TOKENS, LANES), F32),
            pltpu.VMEM((TOKENS, LANES), BF),
            pltpu.VMEM((TOKENS, LANES), F32),
            pltpu.VMEM((HID, LANES), BF),
            pltpu.VMEM((1, HID), F32),
        ],
        compiler_params=pltpu.CompilerParams(vmem_limit_bytes=24 * MIB),
        cost_estimate=pl.CostEstimate(flops=800_000_000, bytes_accessed=5 * MIB, transcendentals=0),
        name="project",
    )(counts, index, arrived, gram, spread)


def spread_table():
    table = np.zeros((64, HID), np.float32)
    table[np.arange(HID) % PART, np.arange(HID)] = 1.0
    return table


def local(
    frame_rows,
    frame_counts,
    conv_weight,
    norm_gain,
    latent_proj,
    patch_weight,
    frame_embed,
    query_gain,
    query_weight,
):
    devices = lax.axis_size("cp")
    index = lax.axis_index("cp").astype(jnp.int32)[None]
    odd_pair, even_pair = edges(frame_counts, index, frame_rows)
    pairs = [[(i, i + 1) for i in range(begin, devices - 1, 2)] for begin in (1, 0)]
    swaps = [pair + [(j, i) for i, j in pair] for pair in pairs]
    odd_pair = lax.ppermute(odd_pair, "cp", swaps[0])
    even_pair = lax.ppermute(even_pair, "cp", swaps[1])
    sums, own, tokens, taps, copies, gain, folded, placed, gram = inner(
        frame_counts,
        frame_rows,
        conv_weight,
        norm_gain[None, :],
        latent_proj.T,
        query_weight.T,
        patch_weight,
        frame_embed,
        query_gain[None, :],
    )
    message = outer(frame_counts, index, odd_pair, even_pair, taps, sums, own, tokens, copies, gain, folded, placed)
    arrived = lax.all_to_all(message, "cp", split_axis=0, concat_axis=0, tiled=True)
    return project(frame_counts, index, arrived, gram, jnp.asarray(spread_table(), BF))


def solution(mesh):
    return jax.shard_map(
        local,
        mesh=mesh,
        in_specs=(P("dp", "cp", None, None), P("dp"), P(), P(), P(), P(), P(), P(), P(None, "cp")),
        out_specs=P(None, ("dp", "cp"), None),
        check_vma=False,
    )
```

time: 95.7 us -> 55 us (0.57)
  Pallas kernels: 58.5 us -> 24.6 us
  blocking collectives: 0 us -> 24.9 us
  waiting for transfers between devices: 12.7 us -> 0.01 us
  starting transfers between devices: 17.3 us -> 5.22 us
  local copies, waits for them, and re-layouts: 6.54 us -> 0.01 us
    pallas_call x2 -> x1, Pallas kernels: 34.6 us -> 3.03 us  [edges(): pl.pallas_call(edges_kernel, out_shape=(shape, shape), in_specs=[SMEM, SM...]
    all_to_all x0 -> x1, blocking collectives: none -> 24.9 us  [local(): lax.all_to_all(message, 'cp', split_axis=0, concat_axis=0, tiled=True)]
    all_to_all x1 -> x0, waiting for transfers between devices: 12.7 us -> none  [local(): lax.all_to_all(message, 'cp', split_axis=0, concat_axis=0, tiled=True)]
    all_to_all x1 -> x0, starting transfers between devices: 12.5 us -> none  [local(): lax.all_to_all(message, 'cp', split_axis=0, concat_axis=0, tiled=True)]
    unnamed x24 -> x4, local copies, waits for them, and re-layouts: 6.54 us -> 0.01 us
  transfers between devices with their start and end apart: 3 -> 2, of which waited for: 1 -> 0; matrix products, arithmetic and copies ran while one was open for 0% -> 0% of each run, Pallas kernels for 15% -> 24%
where the time goes in v3:
time: 55 us; the launch traced here: 54.8 us
  blocking collectives  24.9 us (45%)
  Pallas kernels  24.6 us (45%)
  starting transfers between devices  5.22 us (9%)
    all_to_all x1, blocking collectives, local(): lax.all_to_all(message, 'cp', split_axis=0, concat_axis=0, tiled=True)  24.9 us
    pallas_call x1, Pallas kernels, inner(): pl.pallas_call(inner_kernel, out_shape=(jax.ShapeDtypeStruct((2, FRAMES *...  12.9 us
    pallas_call x1, Pallas kernels, project(): pl.pallas_call(project_kernel, out_shape=jax.ShapeDtypeStruct((HEADS, TOK...  5.33 us
    ppermute x1, starting transfers between devices, local(): even_pair = lax.ppermute(even_pair, 'cp', swaps[1])  4.53 us
    pallas_call x1, Pallas kernels, outer(): pl.pallas_call(outer_kernel, out_shape=jax.ShapeDtypeStruct((FRAMES, MESS...  3.34 us
    pallas_call x1, Pallas kernels, edges(): pl.pallas_call(edges_kernel, out_shape=(shape, shape), in_specs=[SMEM, SM...  3.03 us
  transfers between devices with their start and end apart: 2, of which 0 were waited for; matrix products, arithmetic and copies ran while one was open for 0% of the time, Pallas kernels for 24%

profile of v3, /device:TPU:0, one launch (start us, length us, event | category | flops | bytes accessed | tf_op | source)
XLA Modules:
  0.0 54.8 jit_solution(1933601286339662691)
XLA Ops:
  0.0 0.0 copy-start.1
  0.0 3.0 %edges.1 = (bf16[64,8,512]{2,1,0:T(8,128)(2,1)}, bf16[64,8,512]{2,1,0:T(8,128)(2,1)}) custom-call(s32[16]{0:T(128)} %counts.7, s32[1]{0:T(128)} %bitcast.index, bf16[96,4,8,512]{3,2,1,0:T(8,128)(2,1)} %frames.3), custom_call_target="tpu_custom_call" | custom-call | bytes 2097152 | tf_op jit(solution)/shard_map/edges/pallas_call | solution.py:75
  3.0 0.7 %collective-permute-start = (bf16[64,8,512]{2,1,0:T(8,128)(2,1)}, bf16[64,8,512]{2,1,0:T(8,128)(2,1)S(1)}, u32[]{:S(2)}, u32[]{:S(2)}) collective-permute-start(bf16[64,8,512]{2,1,0:T(8,128)(2,1)} %get-tuple-element.16), channel_id=1, source_target_pairs={{2,4},{6,8},{10,12},{14,16},{18,20},{22,24},{26,28},{30,32},{34,36... | collective-permute-start | bytes 1572872 | tf_op jit(solution)/shard_map/ppermute | solution.py:418
  3.7 4.5 %collective-permute-start.1 = (bf16[64,8,512]{2,1,0:T(8,128)(2,1)}, bf16[64,8,512]{2,1,0:T(8,128)(2,1)S(1)}, u32[]{:S(2)}, u32[]{:S(2)}) collective-permute-start(bf16[64,8,512]{2,1,0:T(8,128)(2,1)} %get-tuple-element.17), channel_id=1, source_target_pairs={{0,2},{4,6},{8,10},{12,14},{16,18},{20,22},{24,26},{28,30},{32,34}... | collective-permute-start | bytes 1572872 | tf_op jit(solution)/shard_map/ppermute | solution.py:419
  8.3 0.0 copy-done.1
  8.3 12.9 %inner.1 = (f32[2,512,512]{2,1,0:T(8,128)S(1)}, bf16[2,512,512]{2,1,0:T(8,128)(2,1)S(1)}, f32[8,64,128]{2,1,0:T(8,128)S(1)}, bf16[3,1536,512]{2,1,0:T(8,128)(2,1...) custom-call(s32[16]{0:T(128)S(1)} %copy-done.1, ...), custom_call_target="tpu_custom_call" | custom-call | flops 8000000000 | bytes 9437184 | tf_op jit(solution)/shard_map/inner/pallas_call | solution.py:234
  21.2 0.0 collective-permute-done.odd_pair
  21.2 0.0 collective-permute-done.1.even_pair
  21.2 0.0 copy-start
  21.2 3.3 %outer.1 = bf16[64,32,128]{2,1,0:T(8,128)(2,1)S(1)} custom-call(s32[16]{0:T(128)S(1)} %copy-done.1, s32[1]{0:T(128)} %bitcast.index, bf16[64,8,512]{2,1,0:T(8,128)(2,1)S(1)} %collective-permute-done.odd_pair, bf16[64,8,512]{2,1,0:T(8,128)(2,1)S(1)} %collective-permute-done.1.even_pair, bf16[3,1536,512]{2,1,0:T(8,128)(2,1)S(1)} %get-tuple-element.18.taps, ...), custom_call_target="tpu_custom_call" | custom-call | flops 1700000000 | bytes 7340032 | tf_op jit(solution)/shard_map/outer/pallas_call | solution.py:305
  24.6 24.9 %all_to_all.5.arrived = bf16[64,32,128]{2,1,0:T(8,128)(2,1)S(1)} all-to-all(bf16[64,32,128]{2,1,0:T(8,128)(2,1)S(1)} %outer.1), channel_id=1, replica_groups=mesh['cp'=64,'dp'=2] {'cp'}, dimensions={0} | all-to-all | bytes 1048576 | tf_op jit(solution)/shard_map/all_to_all | solution.py:432
  49.4 0.0 copy-done
  49.4 5.3 %project.1 = bf16[24,512,128]{2,1,0:T(8,128)(2,1)} custom-call(s32[16]{0:T(128)S(1)} %copy-done.1, s32[1]{0:T(128)} %bitcast.index, bf16[64,32,128]{2,1,0:T(8,128)(2,1)S(1)} %all_to_all.5.arrived, f32[80,80]{1,0:T(8,128)S(1)} %get-tuple-element.26.gram, bf16[64,3072]{1,0:T(8,128)(2,1)S(1)} %copy-done), custom_call_target="tpu_custom_call" | custom-call | flops 800000000 | bytes 5242880 | tf_op jit(solution)/shard_map/project/pallas_call | solution.py:377
Async XLA Ops:
  0.0 8.3 %copy-start.1 = (s32[16]{0:T(128)S(1)}, s32[16]{0:T(128)}, u32[]{:S(2)}) copy-start(s32[16]{0:T(128)} %counts.7) | copy-start | bytes 196
  3.0 18.2 %collective-permute-start = (bf16[64,8,512]{2,1,0:T(8,128)(2,1)}, bf16[64,8,512]{2,1,0:T(8,128)(2,1)S(1)}, u32[]{:S(2)}, u32[]{:S(2)}) collective-permute-start(bf16[64,8,512]{2,1,0:T(8,128)(2,1)} %get-tuple-element.16), channel_id=1, source_target_pairs={{2,4},{6,8},{10,12},{14,16},{18,20},{22,24},{26,28},{30,32},{34,36... | collective-permute-start | bytes 1572872 | tf_op jit(solution)/shard_map/ppermute | solution.py:418
  3.7 17.5 %collective-permute-start.1 = (bf16[64,8,512]{2,1,0:T(8,128)(2,1)}, bf16[64,8,512]{2,1,0:T(8,128)(2,1)S(1)}, u32[]{:S(2)}, u32[]{:S(2)}) collective-permute-start(bf16[64,8,512]{2,1,0:T(8,128)(2,1)} %get-tuple-element.17), channel_id=1, source_target_pairs={{0,2},{4,6},{8,10},{12,14},{16,18},{20,22},{24,26},{28,30},{32,34}... | collective-permute-start | bytes 1572872 | tf_op jit(solution)/shard_map/ppermute | solution.py:419
  21.2 28.2 %copy-start = (bf16[64,3072]{1,0:T(8,128)(2,1)S(1)}, bf16[64,3072]{1,0:T(8,128)(2,1)}, u32[]{:S(2)}) copy-start(bf16[64,3072]{1,0:T(8,128)(2,1)} %constant.8.clone.spread) | copy-start | bytes 1179652

commit v4 on v3

v4 whole, which is shorter than its diff:
```python
import functools

import jax
import jax.numpy as jnp
import numpy as np
from jax import lax
from jax.experimental import pallas as pl
from jax.experimental.pallas import tpu as pltpu
from jax.sharding import PartitionSpec as P

LAT = 16
HID = 3072
HEAD_DIM = 128
HEADS = HID // HEAD_DIM
MAXF = 6
C = 512
WIDTH = 8
STRIP = 4
FRAMES = 64
CLIPS = 16
PART = HID // FRAMES
TOKENS = 512
LANES = 128
MESSAGE = 32
EPSILON = 1e-06
BF = jnp.bfloat16
F32 = jnp.float32
VMEM = pl.BlockSpec(memory_space=pltpu.VMEM)
SMEM = pl.BlockSpec(memory_space=pltpu.SMEM)
HBM = pl.BlockSpec(memory_space=pltpu.HBM)
MIB = 1 << 20


def in_hbm(value):
    return pltpu.with_memory_space_constraint(value, pltpu.HBM)


def nt(left, right):
    return lax.dot_general(left, right, (((1,), (1,)), ((), ())), preferred_element_type=F32)


def dot(left, right):
    return jnp.dot(left, right, preferred_element_type=F32)


def split(value):
    high = value.astype(BF)
    return high, (value - high.astype(F32)).astype(BF)


def each_clip(counts, body):
    def step(clip, start):
        body(clip, start, counts[clip])
        return start + counts[clip]

    lax.fori_loop(0, CLIPS, step, 0)


def is_odd():
    return lax.rem(lax.axis_index("cp"), 2)


def fetch_kernel(counts, frames, odd_rows, even_rows, stage, sem):
    def clip(at, start, count):
        pltpu.make_async_copy(
            frames.at[pl.ds(at * MAXF, count)], stage.at[pl.ds(start, count)], sem
        ).start()

    each_clip(counts, clip)
    pltpu.make_async_copy(stage, stage, sem).wait()
    row = is_odd() * (STRIP - 1)
    odd_rows[...] = stage[:, row]
    even_rows[...] = stage[:, STRIP - 1 - row]


def fetch(counts, frames):
    return pl.pallas_call(
        fetch_kernel,
        out_shape=(
            pltpu.VMEM((FRAMES, WIDTH, C), BF),
            pltpu.VMEM((FRAMES, WIDTH, C), BF),
            pltpu.VMEM((FRAMES, STRIP, WIDTH, C), BF),
        ),
        in_specs=[SMEM, HBM],
        out_specs=(VMEM,) * 3,
        scratch_shapes=[pltpu.SemaphoreType.DMA],
        cost_estimate=pl.CostEstimate(flops=0, bytes_accessed=4 * MIB, transcendentals=0),
        name="fetch",
    )(in_hbm(counts), in_hbm(frames))


def latent_of(summed, frame, gain, proj):
    residual = frame.astype(F32) + 0.5 * summed * (1.0 + jnp.tanh(0.5 * summed))
    mean = jnp.mean(residual * residual, axis=-1, keepdims=True)
    normed = (residual * lax.rsqrt(mean + EPSILON) * gain).astype(BF)
    return nt(normed, proj)


def in_patch(latent, below):
    lane = lax.broadcasted_iota(jnp.int32, (FRAMES, LANES), 1) // LAT
    tokens = []
    for patch in range(WIDTH // 2):
        total = jnp.zeros((FRAMES, LANES), F32)
        for side in range(2):
            column = 2 * patch + side
            block = latent[column * FRAMES : (column + 1) * FRAMES]
            total = total + jnp.where(lane == below * 2 + side, block, 0.0)
        tokens.append(total)
    return tokens


def spread_proj(proj, copies):
    copies[...] = jnp.zeros_like(copies)
    for copy in range(4):
        copies[copy * LAT : (copy + 1) * LAT, :] = proj[...]


def by_column(row, wide, cols, lane):
    row = row.astype(F32).reshape(FRAMES * WIDTH, C)
    for piece in range(C // LANES):
        wide[piece] = row[:, piece * LANES : (piece + 1) * LANES]
    for column in range(WIDTH):
        blocks = [wide[piece, pl.ds(column, FRAMES, stride=WIDTH), :] for piece in range(C // LANES)]
        block = jnp.concatenate(blocks, axis=1).astype(BF)
        cols[column * FRAMES : (column + 1) * FRAMES, lane : lane + C] = block


def fold(weight, table, scale, padded, folded, placed, gram):
    padded[...] = jnp.zeros_like(padded)
    padded[64 : 64 + PART, :] = weight[...]
    high, low = split(table[...].astype(F32) * scale)
    both = nt(weight[...], jnp.concatenate([high[:64], high[:64]], axis=0))
    both = both + nt(weight[...], jnp.concatenate([low[:64], low[:64]], axis=0))
    lane = lax.broadcasted_iota(jnp.int32, (PART // 2, LANES), 1)
    folded[...] = jnp.where(lane < 64, both[: PART // 2], both[PART // 2 :])
    placed[...] = nt(high[64:], padded[...]) + nt(low[64:], padded[...])
    gram[...] = nt(table[...], table[...])


def inner_kernel(
    stage,
    weight,
    columns,
    patch,
    embed,
    scale,
    proj,
    gain,
    sums,
    own,
    tokens,
    taps,
    copies,
    norm,
    folded,
    placed,
    gram,
    wide,
    cols,
    total,
    held,
    table,
    embeds,
    scales,
    projs,
    padded,
    small_sems,
    sems,
):
    small = [
        pltpu.make_async_copy(source, target, small_sems.at[place])
        for place, (source, target) in enumerate(
            (
                (columns, held),
                (patch, table.at[pl.ds(0, 64)]),
                (embed, embeds),
                (scale, scales),
                (proj, projs),
                (gain, norm),
            )
        )
    ]
    for copy in small:
        copy.start()
    order = (1, 0, 2)
    loads = {}
    for side in order:
        for row in range(3):
            loads[side, row] = pltpu.make_async_copy(
                weight.at[row, side], taps.at[side, pl.ds(row * C, C)], sems.at[side, row]
            )
            loads[side, row].start()
    for row in range(2):
        by_column(stage[:, row], wide.at[row], cols, row * C)
    for copy in small:
        copy.wait()
    table[64:80, :] = jnp.concatenate(
        [embeds[...].astype(F32), jnp.zeros((16 - MAXF, HID), F32)], axis=0
    ).astype(BF)
    fold(held, table, scales[...], padded, folded, placed, gram)
    spread_proj(projs, copies)
    count = FRAMES * WIDTH
    ready = 2
    for side in order:
        begin, end = max(0, side - 1) * FRAMES, count - max(0, 1 - side) * FRAMES
        shift = (1 - side) * FRAMES
        for row in range(STRIP):
            low, high = max(row - 1, 0), min(row + 2, STRIP)
            while ready < high:
                by_column(stage[:, ready], wide.at[ready], cols, ready * C)
                ready += 1
            if row == 0:
                for tap in range(3):
                    loads[side, tap].wait()
            skip = low - (row - 1)
            part = dot(
                cols[begin:end, low * C : high * C],
                taps[side, skip * C : (skip + high - low) * C, :],
            )
            target = sums.at[row // 2] if row in (0, STRIP - 1) else total.at[row - 1]
            if side == 1:
                target[...] = part
            else:
                target[begin + shift : end + shift, :] += part
    for place, row in enumerate((0, STRIP - 1)):
        own[place] = cols[:, row * C : (row + 1) * C]
    for row in (1, 2):
        latent = latent_of(total[row - 1], cols[:, row * C : (row + 1) * C], norm[...], copies[...])
        for patch_index, value in enumerate(in_patch(latent, row % 2)):
            tokens[(row // 2) * 4 + patch_index] = value


def inner(stage, *operands):
    return pl.pallas_call(
        inner_kernel,
        out_shape=(
            jax.ShapeDtypeStruct((2, FRAMES * WIDTH, C), F32),
            jax.ShapeDtypeStruct((2, FRAMES * WIDTH, C), BF),
            jax.ShapeDtypeStruct((8, FRAMES, LANES), F32),
            jax.ShapeDtypeStruct((3, 3 * C, C), BF),
            jax.ShapeDtypeStruct((LANES, C), BF),
            jax.ShapeDtypeStruct((1, C), F32),
            jax.ShapeDtypeStruct((PART // 2, LANES), F32),
            jax.ShapeDtypeStruct((16, LANES), F32),
            jax.ShapeDtypeStruct((80, 80), F32),
        ),
        in_specs=[VMEM] + [HBM] * 7,
        out_specs=(VMEM,) * 9,
        scratch_shapes=[
            pltpu.VMEM((STRIP, C // LANES, FRAMES * WIDTH, LANES), F32),
            pltpu.VMEM((FRAMES * WIDTH, STRIP * C), BF),
            pltpu.VMEM((2, FRAMES * WIDTH, C), F32),
            pltpu.VMEM((PART, HID), BF),
            pltpu.VMEM((80, HID), BF),
            pltpu.VMEM((MAXF, HID), BF),
            pltpu.VMEM((1, HID), F32),
            pltpu.VMEM((LAT, C), BF),
            pltpu.VMEM((LANES, HID), BF),
            pltpu.SemaphoreType.DMA((6,)),
            pltpu.SemaphoreType.DMA((3, 3)),
        ],
        compiler_params=pltpu.CompilerParams(vmem_limit_bytes=32 * MIB),
        cost_estimate=pl.CostEstimate(flops=8_000_000_000, bytes_accessed=9 * MIB, transcendentals=MIB // 2),
        name="inner",
    )(stage, *map(in_hbm, operands))


def edge_row(place, halo, taps, sums, own, copies, gain, wide, cols, total):
    count = FRAMES * WIDTH
    tap = pl.multiple_of(place * 2 * C, C)
    by_column(halo[...], wide, cols, 0)
    total[...] = sums[place]
    for side in (1, 0, 2):
        begin, end = max(0, side - 1) * FRAMES, count - max(0, 1 - side) * FRAMES
        shift = (1 - side) * FRAMES
        total[begin + shift : end + shift, :] += dot(cols[begin:end], taps[side, pl.ds(tap, C), :])
    latent = latent_of(total[...], own[place], gain[...], copies[...])
    return in_patch(latent, place)


def outer_scratch():
    return [
        pltpu.VMEM((C // LANES, FRAMES * WIDTH, LANES), F32),
        pltpu.VMEM((FRAMES * WIDTH, C), BF),
        pltpu.VMEM((FRAMES * WIDTH, C), F32),
    ]


def outer_even_kernel(listed, halo, taps, sums, own, tokens, copies, gain, placed, parts, *scratch):
    *scratch, counts, sem = scratch
    load = pltpu.make_async_copy(listed, counts, sem)
    load.start()
    place = 1 - is_odd()
    for patch, value in enumerate(edge_row(place, halo, taps, sums, own, copies, gain, *scratch)):
        parts[patch] = tokens[place * 4 + patch] + value
    load.wait()
    frame = lax.broadcasted_iota(jnp.int32, (FRAMES, 1), 0)
    begin = jnp.zeros((FRAMES, 1), jnp.int32)
    start = 0
    for clip in range(CLIPS):
        begin = jnp.where(frame >= start, start, begin)
        start = start + counts[clip]
    position = jnp.zeros((FRAMES, LANES), F32)
    for offset in range(MAXF):
        position = position + jnp.where(frame - begin == offset, placed[offset : offset + 1, :], 0.0)
    high, low = split(position)
    parts[4] = high.astype(F32)
    parts[5] = low.astype(F32)


def outer_even(counts, halo, taps, sums, own, tokens, copies, gain, placed):
    return pl.pallas_call(
        outer_even_kernel,
        out_shape=jax.ShapeDtypeStruct((6, FRAMES, LANES), F32),
        in_specs=[HBM] + [VMEM] * 8,
        out_specs=VMEM,
        scratch_shapes=outer_scratch() + [pltpu.SMEM((CLIPS,), jnp.int32), pltpu.SemaphoreType.DMA],
        compiler_params=pltpu.CompilerParams(vmem_limit_bytes=24 * MIB),
        cost_estimate=pl.CostEstimate(flops=800_000_000, bytes_accessed=4 * MIB, transcendentals=MIB // 4),
        name="outer_even",
    )(in_hbm(counts), halo, taps, sums, own, tokens, copies, gain, placed)


def outer_odd_kernel(halo, taps, sums, own, tokens, copies, gain, parts, folded, message, *scratch):
    *scratch, flat = scratch
    place = is_odd()
    mine = edge_row(place, halo, taps, sums, own, copies, gain, *scratch)
    for patch in range(4):
        mine[patch] = mine[patch] + tokens[place * 4 + patch]
    for index in range(8):
        value = jnp.where(place == index // 4, mine[index % 4], parts[index % 4])
        if index < 2:
            value = value + parts[4 + index]
        flat[pl.ds(index, FRAMES, stride=8), :] = value
    rest = jnp.broadcast_to(folded[...][None], (FRAMES, PART // 2, LANES))
    message[...] = jnp.concatenate([flat[...].reshape(FRAMES, 8, LANES), rest], axis=1).astype(BF)


def outer_odd(halo, taps, sums, own, tokens, copies, gain, parts, folded):
    return pl.pallas_call(
        outer_odd_kernel,
        out_shape=jax.ShapeDtypeStruct((FRAMES, MESSAGE, LANES), BF),
        in_specs=[VMEM] * 9,
        out_specs=VMEM,
        scratch_shapes=outer_scratch() + [pltpu.VMEM((TOKENS, LANES), F32)],
        compiler_params=pltpu.CompilerParams(vmem_limit_bytes=24 * MIB),
        cost_estimate=pl.CostEstimate(flops=800_000_000, bytes_accessed=4 * MIB, transcendentals=MIB // 4),
        name="outer_odd",
    )(halo, taps, sums, own, tokens, copies, gain, parts, folded)


GROUP = 3


def project_kernel(listed, arrived, gram, spread, out, flat, columns, shift, held, counts, load_sem, sems):
    load = pltpu.make_async_copy(listed, counts, load_sem)
    load.start()
    got = arrived[...].astype(F32)
    flat[...] = got[:, 0:8].reshape(TOKENS, LANES)
    lane = lax.broadcasted_iota(jnp.int32, (TOKENS, LANES), 1)
    token = jnp.where(lane < 64, flat[...], 0.0)
    query = (token + pltpu.roll(token, 64, 1)).astype(BF)
    rest = got[:, 8:MESSAGE]
    lane = lax.broadcasted_iota(jnp.int32, rest.shape, 2)
    low, high = jnp.where(lane < 64, rest, 0.0), jnp.where(lane < 64, 0.0, rest)
    columns[...] = jnp.concatenate([low, high], axis=1).reshape(HID, LANES).astype(BF)
    lane = lax.broadcasted_iota(jnp.int32, (FRAMES, LANES), 1)
    piece = jnp.where(
        lane < 64, pltpu.roll(flat[pl.ds(0, FRAMES, stride=8), :], 64, 1), flat[pl.ds(1, FRAMES, stride=8), :]
    )
    laid = dot(piece.astype(BF), spread[...])
    lane = lax.broadcasted_iota(jnp.int32, (8, 8 * PART), 1)
    line = lax.broadcasted_iota(jnp.int32, (8, 8 * PART), 0) * PART
    mask = (lane >= line) & (lane < line + PART)
    for block in range(8):
        shift[:, block * 8 * PART : (block + 1) * 8 * PART] = jnp.sum(
            jnp.where(mask, laid[block * 8 : (block + 1) * 8], 0.0), axis=0, keepdims=True
        )
    own = lax.axis_index("cp")
    load.wait()

    def clip(at, carry):
        start, begin = carry
        begin = jnp.where(start <= own, start, begin)
        return start + counts[at], begin

    _, begin = lax.fori_loop(0, CLIPS, clip, (0, 0))
    matrix = gram[...]
    line = lax.broadcasted_iota(jnp.int32, (16, 80), 0)
    position = jnp.sum(jnp.where(line == own - begin, matrix[64:], 0.0), axis=0, keepdims=True)
    lane = lax.broadcasted_iota(jnp.int32, (1, 80), 1)
    square = jnp.sum(jnp.where(lane == 64 + own - begin, position, 0.0), axis=1, keepdims=True)
    token = token[:, 0:64]
    total = jnp.zeros((TOKENS, 64), F32) + 2.0 * position[:, 0:64]
    matrix = matrix[:64, :64]
    for _ in range(3):
        part = matrix.astype(BF)
        total = total + dot(token.astype(BF), part)
        matrix = matrix - part.astype(F32)
    total = jnp.sum(total * token, axis=-1, keepdims=True) + square
    scale = lax.rsqrt(jnp.maximum(total, 0.0) * (1.0 / HID) + EPSILON)
    copies = []
    for group in range(HEADS // GROUP):
        at = slice(group * GROUP * HEAD_DIM, (group + 1) * GROUP * HEAD_DIM)
        value = ((nt(query, columns[at, :]) + shift[:, at]) * scale).astype(BF)
        for head in range(GROUP):
            held[group * GROUP + head] = value[:, head * HEAD_DIM : (head + 1) * HEAD_DIM]
        heads = pl.ds(group * GROUP, GROUP)
        copies.append(pltpu.make_async_copy(held.at[heads], out.at[heads], sems.at[group]))
        copies[-1].start()
    for copy in copies:
        copy.wait()


def project(counts, arrived, gram, spread):
    return pl.pallas_call(
        project_kernel,
        out_shape=jax.ShapeDtypeStruct((HEADS, TOKENS, HEAD_DIM), BF),
        in_specs=[HBM, VMEM, VMEM, VMEM],
        out_specs=HBM,
        scratch_shapes=[
            pltpu.VMEM((TOKENS, LANES), F32),
            pltpu.VMEM((HID, LANES), BF),
            pltpu.VMEM((1, HID), F32),
            pltpu.VMEM((HEADS, TOKENS, HEAD_DIM), BF),
            pltpu.SMEM((CLIPS,), jnp.int32),
            pltpu.SemaphoreType.DMA,
            pltpu.SemaphoreType.DMA((HEADS // GROUP,)),
        ],
        compiler_params=pltpu.CompilerParams(vmem_limit_bytes=24 * MIB),
        cost_estimate=pl.CostEstimate(flops=800_000_000, bytes_accessed=5 * MIB, transcendentals=0),
        name="project",
    )(in_hbm(counts), arrived, gram, spread)


def spread_table():
    table = np.zeros((LANES, 8 * PART), np.float32)
    lane = np.arange(8 * PART)
    table[lane % PART, lane] = 1.0
    table[64 + lane % PART, lane] = 1.0
    return table


def local(
    frame_rows,
    frame_counts,
    conv_weight,
    norm_gain,
    latent_proj,
    patch_weight,
    frame_embed,
    query_gain,
    query_weight,
):
    devices = lax.axis_size("cp")
    pairs = [[(i, i + 1) for i in range(begin, devices - 1, 2)] for begin in (1, 0)]
    swaps = [pair + [(j, i) for i, j in pair] for pair in pairs]
    odd_rows, even_rows, stage = fetch(frame_counts, frame_rows)
    odd_pair = lax.ppermute(odd_rows, "cp", swaps[0])
    even_pair = lax.ppermute(even_rows, "cp", swaps[1])
    sums, own, tokens, taps, copies, gain, folded, placed, gram = inner(
        stage,
        conv_weight,
        query_weight.T,
        patch_weight,
        frame_embed,
        query_gain[None, :],
        latent_proj.T,
        norm_gain[None, :],
    )
    parts = outer_even(frame_counts, even_pair, taps, sums, own, tokens, copies, gain, placed)
    message = outer_odd(odd_pair, taps, sums, own, tokens, copies, gain, parts, folded)
    arrived = lax.all_to_all(message, "cp", split_axis=0, concat_axis=0, tiled=True)
    return project(frame_counts, arrived, gram, jnp.asarray(spread_table(), BF))


def solution(mesh):
    return jax.shard_map(
        local,
        mesh=mesh,
        in_specs=(P("dp", "cp", None, None), P("dp"), P(), P(), P(), P(), P(), P(), P(None, "cp")),
        out_specs=P(None, ("dp", "cp"), None),
        check_vma=False,
    )
```

time: 55 us -> 50.1 us (0.911)
  Pallas kernels: 24.6 us -> 21 us
  blocking collectives: 24.9 us -> 23.6 us
    pallas_call x1, Pallas kernels: 5.33 us -> 2.95 us  [project(): pl.pallas_call(project_kernel, out_shape=jax.ShapeDtypeStruct((HEADS, TOK...]
    all_to_all x1, blocking collectives: 24.9 us -> 23.6 us  [local(): lax.all_to_all(message, 'cp', split_axis=0, concat_axis=0, tiled=True)]
    pallas_call x2 -> x3, Pallas kernels: 6.36 us -> 5.73 us  [the longest x1 2.38 us: fetch(): pl.pallas_call(fetch_kernel, out_shape=(pltpu.VMEM((FRAMES, WIDTH, C), BF...]
    pallas_call x1, Pallas kernels: 12.9 us -> 12.3 us  [inner(): pl.pallas_call(inner_kernel, out_shape=(jax.ShapeDtypeStruct((2, FRAMES *...]
  transfers between devices with their start and end apart: 2 -> 2, of which waited for: 0 -> 0; matrix products, arithmetic and copies ran while one was open for 0% -> 0% of each run, Pallas kernels for 24% -> 28%
where the time goes in v4:
time: 50.1 us; the launch traced here: 49.9 us
  blocking collectives  23.6 us (47%)
  Pallas kernels  21 us (42%)
  starting transfers between devices  5.22 us (10%)
    all_to_all x1, blocking collectives, local(): lax.all_to_all(message, 'cp', split_axis=0, concat_axis=0, tiled=True)  23.6 us
    pallas_call x1, Pallas kernels, inner(): pl.pallas_call(inner_kernel, out_shape=(jax.ShapeDtypeStruct((2, FRAMES *...  12.3 us
    ppermute x1, starting transfers between devices, local(): even_pair = lax.ppermute(even_rows, 'cp', swaps[1])  4.53 us
    pallas_call x1, Pallas kernels, project(): pl.pallas_call(project_kernel, out_shape=jax.ShapeDtypeStruct((HEADS, TOK...  2.95 us
    pallas_call x1, Pallas kernels, fetch(): pl.pallas_call(fetch_kernel, out_shape=(pltpu.VMEM((FRAMES, WIDTH, C), BF...  2.38 us
    pallas_call x1, Pallas kernels, outer_even(): pl.pallas_call(outer_even_kernel, out_shape=jax.ShapeDtypeStruct((6, FRAM...  1.71 us
    pallas_call x1, Pallas kernels, outer_odd(): pl.pallas_call(outer_odd_kernel, out_shape=jax.ShapeDtypeStruct((FRAMES,...  1.64 us
  transfers between devices with their start and end apart: 2, of which 0 were waited for; matrix products, arithmetic and copies ran while one was open for 0% of the time, Pallas kernels for 28%

profile of v4, /device:TPU:0, one launch (start us, length us, event | category | flops | bytes accessed | tf_op | source)
XLA Modules:
  0.0 49.9 jit_solution(6362076710888144578)
XLA Ops:
  0.0 2.4 %fetch.1 = (bf16[64,8,512]{2,1,0:T(8,128)(2,1)S(1)}, bf16[64,8,512]{2,1,0:T(8,128)(2,1)S(1)}, bf16[64,4,8,512]{3,2,1,0:T(8,128)(2,1)S(1)}) custom-call(s32[16]{0:T(128)} %listed.3, bf16[96,4,8,512]{3,2,1,0:T(8,128)(2,1)} %frames.1), custom_call_target="tpu_custom_call" | custom-call | bytes 4194304 | tf_op jit(solution)/shard_map/fetch/pallas_call | solution.py:77
  2.4 0.7 %collective-permute-start = (bf16[64,8,512]{2,1,0:T(8,128)(2,1)S(1)}, bf16[64,8,512]{2,1,0:T(8,128)(2,1)S(1)}, u32[]{:S(2)}, u32[]{:S(2)}) collective-permute-start(bf16[64,8,512]{2,1,0:T(8,128)(2,1)S(1)} %get-tuple-element.17), channel_id=1, source_target_pairs={{2,4},{6,8},{10,12},{14,16},{18,20},{22,24},{26,28},{30,32},{34,36... | collective-permute-start | bytes 1572872 | tf_op jit(solution)/shard_map/ppermute | solution.py:459
  3.1 4.5 %collective-permute-start.1 = (bf16[64,8,512]{2,1,0:T(8,128)(2,1)S(1)}, bf16[64,8,512]{2,1,0:T(8,128)(2,1)S(1)}, u32[]{:S(2)}, u32[]{:S(2)}) collective-permute-start(bf16[64,8,512]{2,1,0:T(8,128)(2,1)S(1)} %get-tuple-element.25), channel_id=1, source_target_pairs={{0,2},{4,6},{8,10},{12,14},{16,18},{20,22},{24,26},{28,30},{32,34}... | collective-permute-start | bytes 1572872 | tf_op jit(solution)/shard_map/ppermute | solution.py:460
  7.6 12.3 %inner.1 = (f32[2,512,512]{2,1,0:T(8,128)S(1)}, bf16[2,512,512]{2,1,0:T(8,128)(2,1)S(1)}, f32[8,64,128]{2,1,0:T(8,128)S(1)}, bf16[3,1536,512]{2,1,0:T(8,128)(2,1...) custom-call(bf16[64,4,8,512]{3,2,1,0:T(8,128)(2,1)S(1)} %get-tuple-e, ...), custom_call_target="tpu_custom_call" | custom-call | flops 8000000000 | bytes 9437184 | tf_op jit(solution)/shard_map/inner/pallas_call | solution.py:234
  19.9 0.0 collective-permute-done.1.halo
  19.9 1.7 %outer_even.1.parts = f32[6,64,128]{2,1,0:T(8,128)S(1)} custom-call(s32[16]{0:T(128)} %listed.3, bf16[64,8,512]{2,1,0:T(8,128)(2,1)S(1)} %collective-permute-done.1.halo, bf16[3,1536,512]{2,1,0:T(8,128)(2,1)S(1)} %get-tuple-element.19.taps, f32[2,512,512]{2,1,0:T(8,128)S(1)} %get-tuple-element.20.sums, bf16[2,512,512]{2,1,0:T(8,128)(2,1)S(1)} %get-tuple-element.21.own, ...), custom_call_target="tpu_custom_call" | custom-call | flops 800000000 | bytes 4194304 | tf_op jit(solution)/shard_map/outer_even/pallas_call | solution.py:312
  21.7 0.0 collective-permute-done.halo
  21.7 0.0 copy-start
  21.7 1.6 %outer_odd.1 = bf16[64,32,128]{2,1,0:T(8,128)(2,1)S(1)} custom-call(bf16[64,8,512]{2,1,0:T(8,128)(2,1)S(1)} %collective-permute-done.halo, bf16[3,1536,512]{2,1,0:T(8,128)(2,1)S(1)} %get-tuple-element.19.taps, f32[2,512,512]{2,1,0:T(8,128)S(1)} %get-tuple-element.20.sums, bf16[2,512,512]{2,1,0:T(8,128)(2,1)S(1)} %get-tuple-element.21.own, ...), custom_call_target="tpu_custom_call" | custom-call | flops 800000000 | bytes 4194304 | tf_op jit(solution)/shard_map/outer_odd/pallas_call | solution.py:340
  23.3 23.6 %all_to_all.5.arrived = bf16[64,32,128]{2,1,0:T(8,128)(2,1)S(1)} all-to-all(bf16[64,32,128]{2,1,0:T(8,128)(2,1)S(1)} %outer_odd.1), channel_id=1, replica_groups=mesh['cp'=64,'dp'=2] {'cp'}, dimensions={0} | all-to-all | bytes 1048576 | tf_op jit(solution)/shard_map/all_to_all | solution.py:473
  46.9 0.0 copy-done
  46.9 2.9 %project.1 = bf16[24,512,128]{2,1,0:T(8,128)(2,1)} custom-call(s32[16]{0:T(128)} %listed.3, bf16[64,32,128]{2,1,0:T(8,128)(2,1)S(1)} %all_to_all.5.arrived, f32[80,80]{1,0:T(8,128)S(1)} %get-tuple-element.28.gram, bf16[128,384]{1,0:T(8,128)(2,1)S(1)} %copy-done), custom_call_target="tpu_custom_call" | custom-call | flops 800000000 | bytes 5242880 | tf_op jit(solution)/shard_map/project/pallas_call | solution.py:416
Async XLA Ops:
  2.4 19.3 %collective-permute-start = (bf16[64,8,512]{2,1,0:T(8,128)(2,1)S(1)}, bf16[64,8,512]{2,1,0:T(8,128)(2,1)S(1)}, u32[]{:S(2)}, u32[]{:S(2)}) collective-permute-start(bf16[64,8,512]{2,1,0:T(8,128)(2,1)S(1)} %get-tuple-element.17), channel_id=1, source_target_pairs={{2,4},{6,8},{10,12},{14,16},{18,20},{22,24},{26,28},{30,32},{34,36... | collective-permute-start | bytes 1572872 | tf_op jit(solution)/shard_map/ppermute | solution.py:459
  3.1 16.8 %collective-permute-start.1 = (bf16[64,8,512]{2,1,0:T(8,128)(2,1)S(1)}, bf16[64,8,512]{2,1,0:T(8,128)(2,1)S(1)}, u32[]{:S(2)}, u32[]{:S(2)}) collective-permute-start(bf16[64,8,512]{2,1,0:T(8,128)(2,1)S(1)} %get-tuple-element.25), channel_id=1, source_target_pairs={{0,2},{4,6},{8,10},{12,14},{16,18},{20,22},{24,26},{28,30},{32,34}... | collective-permute-start | bytes 1572872 | tf_op jit(solution)/shard_map/ppermute | solution.py:460
  21.7 25.2 %copy-start = (bf16[128,384]{1,0:T(8,128)(2,1)S(1)}, bf16[128,384]{1,0:T(8,128)(2,1)}, u32[]{:S(2)}) copy-start(bf16[128,384]{1,0:T(8,128)(2,1)} %constant.2.clone.spread) | copy-start | bytes 294916

commit v5 on v4

--- a/solution.py
+++ b/solution.py
@@ -125,25 +125,9 @@
         cols[column * FRAMES : (column + 1) * FRAMES, lane : lane + C] = block
 
 
-def fold(weight, table, scale, padded, folded, placed, gram):
-    padded[...] = jnp.zeros_like(padded)
-    padded[64 : 64 + PART, :] = weight[...]
-    high, low = split(table[...].astype(F32) * scale)
-    both = nt(weight[...], jnp.concatenate([high[:64], high[:64]], axis=0))
-    both = both + nt(weight[...], jnp.concatenate([low[:64], low[:64]], axis=0))
-    lane = lax.broadcasted_iota(jnp.int32, (PART // 2, LANES), 1)
-    folded[...] = jnp.where(lane < 64, both[: PART // 2], both[PART // 2 :])
-    placed[...] = nt(high[64:], padded[...]) + nt(low[64:], padded[...])
-    gram[...] = nt(table[...], table[...])
-
-
 def inner_kernel(
     stage,
     weight,
-    columns,
-    patch,
-    embed,
-    scale,
     proj,
     gain,
     sums,
@@ -152,66 +136,39 @@
     taps,
     copies,
     norm,
-    folded,
-    placed,
-    gram,
     wide,
     cols,
     total,
-    held,
-    table,
-    embeds,
-    scales,
     projs,
-    padded,
     small_sems,
     sems,
 ):
     small = [
         pltpu.make_async_copy(source, target, small_sems.at[place])
-        for place, (source, target) in enumerate(
-            (
-                (columns, held),
-                (patch, table.at[pl.ds(0, 64)]),
-                (embed, embeds),
-                (scale, scales),
-                (proj, projs),
-                (gain, norm),
-            )
-        )
+        for place, (source, target) in enumerate(((proj, projs), (gain, norm)))
     ]
-    for copy in small:
-        copy.start()
     order = (1, 0, 2)
     loads = {}
     for side in order:
-        for row in range(3):
+        for row in (1, 2, 0):
             loads[side, row] = pltpu.make_async_copy(
                 weight.at[row, side], taps.at[side, pl.ds(row * C, C)], sems.at[side, row]
             )
             loads[side, row].start()
-    for row in range(2):
+    for copy in small:
+        copy.start()
+    for row in range(STRIP):
         by_column(stage[:, row], wide.at[row], cols, row * C)
-    for copy in small:
-        copy.wait()
-    table[64:80, :] = jnp.concatenate(
-        [embeds[...].astype(F32), jnp.zeros((16 - MAXF, HID), F32)], axis=0
-    ).astype(BF)
-    fold(held, table, scales[...], padded, folded, placed, gram)
-    spread_proj(projs, copies)
+    for place, row in enumerate((0, STRIP - 1)):
+        own[place] = cols[:, row * C : (row + 1) * C]
     count = FRAMES * WIDTH
-    ready = 2
     for side in order:
         begin, end = max(0, side - 1) * FRAMES, count - max(0, 1 - side) * FRAMES
         shift = (1 - side) * FRAMES
         for row in range(STRIP):
             low, high = max(row - 1, 0), min(row + 2, STRIP)
-            while ready < high:
-                by_column(stage[:, ready], wide.at[ready], cols, ready * C)
-                ready += 1
-            if row == 0:
-                for tap in range(3):
-                    loads[side, tap].wait()
+            for tap in ((1, 2), (0,), (), ())[row]:
+                loads[side, tap].wait()
             skip = low - (row - 1)
             part = dot(
                 cols[begin:end, low * C : high * C],
@@ -222,8 +179,9 @@
                 target[...] = part
             else:
                 target[begin + shift : end + shift, :] += part
-    for place, row in enumerate((0, STRIP - 1)):
-        own[place] = cols[:, row * C : (row + 1) * C]
+    for copy in small:
+        copy.wait()
+    spread_proj(projs, copies)
     for row in (1, 2):
         latent = latent_of(total[row - 1], cols[:, row * C : (row + 1) * C], norm[...], copies[...])
         for patch_index, value in enumerate(in_patch(latent, row % 2)):
@@ -240,23 +198,15 @@
             jax.ShapeDtypeStruct((3, 3 * C, C), BF),
             jax.ShapeDtypeStruct((LANES, C), BF),
             jax.ShapeDtypeStruct((1, C), F32),
-            jax.ShapeDtypeStruct((PART // 2, LANES), F32),
-            jax.ShapeDtypeStruct((16, LANES), F32),
-            jax.ShapeDtypeStruct((80, 80), F32),
         ),
-        in_specs=[VMEM] + [HBM] * 7,
-        out_specs=(VMEM,) * 9,
+        in_specs=[VMEM] + [HBM] * 3,
+        out_specs=(VMEM,) * 6,
         scratch_shapes=[
             pltpu.VMEM((STRIP, C // LANES, FRAMES * WIDTH, LANES), F32),
             pltpu.VMEM((FRAMES * WIDTH, STRIP * C), BF),
             pltpu.VMEM((2, FRAMES * WIDTH, C), F32),
-            pltpu.VMEM((PART, HID), BF),
-            pltpu.VMEM((80, HID), BF),
-            pltpu.VMEM((MAXF, HID), BF),
-            pltpu.VMEM((1, HID), F32),
             pltpu.VMEM((LAT, C), BF),
-            pltpu.VMEM((LANES, HID), BF),
-            pltpu.SemaphoreType.DMA((6,)),
+            pltpu.SemaphoreType.DMA((2,)),
             pltpu.SemaphoreType.DMA((3, 3)),
         ],
         compiler_params=pltpu.CompilerParams(vmem_limit_bytes=32 * MIB),
@@ -349,12 +299,68 @@
     )(halo, taps, sums, own, tokens, copies, gain, parts, folded)
 
 
+def fold_kernel(after, counts, columns, patch, embed, scale, folded, placed, gram, added, table, rows):
+    del after
+    table[0:64, :] = patch[...]
+    table[64:80, :] = jnp.concatenate(
+        [embed[...].astype(F32), jnp.zeros((16 - MAXF, HID), F32)], axis=0
+    ).astype(BF)
+    high, low = split(table[...].astype(F32) * scale[...])
+    rows[0:64, :] = high[:64]
+    rows[64:128, :] = low[:64]
+    rows[128:144, :] = high[64:]
+    rows[144:160, :] = low[64:]
+    product = nt(rows[...], columns[...])
+    product = jnp.concatenate([product, jnp.zeros((160, LANES - PART), F32)], axis=1)
+    both = (product[:64] + product[64:128]).T
+    both = jnp.concatenate([both, both], axis=1)
+    lane = lax.broadcasted_iota(jnp.int32, (PART // 2, LANES), 1)
+    folded[...] = jnp.where(lane < 64, both[: PART // 2], both[PART // 2 : PART])
+    placed[...] = pltpu.roll(product[128:144] + product[144:160], 64, 1)
+    product = nt(table[...], table[...])
+    matrix = product[:64, :64]
+    for part in range(3):
+        piece = matrix.astype(BF)
+        gram[part] = piece
+        matrix = matrix - piece.astype(F32)
+    own = lax.axis_index("cp")
+
+    def clip(at, carry):
+        start, begin = carry
+        begin = jnp.where(start <= own, start, begin)
+        return start + counts[at], begin
+
+    _, begin = lax.fori_loop(0, CLIPS, clip, (0, 0))
+    line = lax.broadcasted_iota(jnp.int32, (16, 80), 0)
+    position = jnp.sum(jnp.where(line == own - begin, product[64:], 0.0), axis=0, keepdims=True)
+    lane = lax.broadcasted_iota(jnp.int32, (1, 80), 1)
+    square = jnp.sum(jnp.where(lane == 64 + own - begin, position, 0.0), axis=1, keepdims=True)
+    added[0:1, :] = 2.0 * position[:, :64]
+    added[1:2, :] = jnp.broadcast_to(square, (1, 64))
+
+
+def fold(after, counts, columns, patch, embed, scale):
+    return pl.pallas_call(
+        fold_kernel,
+        out_shape=(
+            jax.ShapeDtypeStruct((PART // 2, LANES), F32),
+            jax.ShapeDtypeStruct((16, LANES), F32),
+            jax.ShapeDtypeStruct((3, 64, 64), BF),
+            jax.ShapeDtypeStruct((2, 64), F32),
+        ),
+        in_specs=[VMEM, SMEM] + [VMEM] * 4,
+        out_specs=(VMEM,) * 4,
+        scratch_shapes=[pltpu.VMEM((80, HID), BF), pltpu.VMEM((160, HID), BF)],
+        compiler_params=pltpu.CompilerParams(vmem_limit_bytes=8 * MIB),
+        cost_estimate=pl.CostEstimate(flops=1_000_000_000, bytes_accessed=MIB, transcendentals=0),
+        name="fold",
+    )(after, counts, columns, patch, embed, scale)
+
+
 GROUP = 3
 
 
-def project_kernel(listed, arrived, gram, spread, out, flat, columns, shift, held, counts, load_sem, sems):
-    load = pltpu.make_async_copy(listed, counts, load_sem)
-    load.start()
+def project_kernel(arrived, gram, added, spread, out, flat, columns, shift, held, sems):
     got = arrived[...].astype(F32)
     flat[...] = got[:, 0:8].reshape(TOKENS, LANES)
     lane = lax.broadcasted_iota(jnp.int32, (TOKENS, LANES), 1)
@@ -376,28 +382,11 @@
         shift[:, block * 8 * PART : (block + 1) * 8 * PART] = jnp.sum(
             jnp.where(mask, laid[block * 8 : (block + 1) * 8], 0.0), axis=0, keepdims=True
         )
-    own = lax.axis_index("cp")
-    load.wait()
-
-    def clip(at, carry):
-        start, begin = carry
-        begin = jnp.where(start <= own, start, begin)
-        return start + counts[at], begin
-
-    _, begin = lax.fori_loop(0, CLIPS, clip, (0, 0))
-    matrix = gram[...]
-    line = lax.broadcasted_iota(jnp.int32, (16, 80), 0)
-    position = jnp.sum(jnp.where(line == own - begin, matrix[64:], 0.0), axis=0, keepdims=True)
-    lane = lax.broadcasted_iota(jnp.int32, (1, 80), 1)
-    square = jnp.sum(jnp.where(lane == 64 + own - begin, position, 0.0), axis=1, keepdims=True)
     token = token[:, 0:64]
-    total = jnp.zeros((TOKENS, 64), F32) + 2.0 * position[:, 0:64]
-    matrix = matrix[:64, :64]
-    for _ in range(3):
-        part = matrix.astype(BF)
-        total = total + dot(token.astype(BF), part)
-        matrix = matrix - part.astype(F32)
-    total = jnp.sum(total * token, axis=-1, keepdims=True) + square
+    total = jnp.zeros((TOKENS, 64), F32) + added[0:1, :]
+    for part in range(3):
+        total = total + dot(token.astype(BF), gram[part])
+    total = jnp.sum(total * token, axis=-1, keepdims=True) + added[1:2, 0:1]
     scale = lax.rsqrt(jnp.maximum(total, 0.0) * (1.0 / HID) + EPSILON)
     copies = []
     for group in range(HEADS // GROUP):
@@ -412,25 +401,23 @@
         copy.wait()
 
 
-def project(counts, arrived, gram, spread):
+def project(arrived, gram, added, spread):
     return pl.pallas_call(
         project_kernel,
         out_shape=jax.ShapeDtypeStruct((HEADS, TOKENS, HEAD_DIM), BF),
-        in_specs=[HBM, VMEM, VMEM, VMEM],
+        in_specs=[VMEM] * 4,
         out_specs=HBM,
         scratch_shapes=[
             pltpu.VMEM((TOKENS, LANES), F32),
             pltpu.VMEM((HID, LANES), BF),
             pltpu.VMEM((1, HID), F32),
             pltpu.VMEM((HEADS, TOKENS, HEAD_DIM), BF),
-            pltpu.SMEM((CLIPS,), jnp.int32),
-            pltpu.SemaphoreType.DMA,
             pltpu.SemaphoreType.DMA((HEADS // GROUP,)),
         ],
         compiler_params=pltpu.CompilerParams(vmem_limit_bytes=24 * MIB),
         cost_estimate=pl.CostEstimate(flops=800_000_000, bytes_accessed=5 * MIB, transcendentals=0),
         name="project",
-    )(in_hbm(counts), arrived, gram, spread)
+    )(arrived, gram, added, spread)
 
 
 def spread_table():
@@ -456,22 +443,18 @@
     pairs = [[(i, i + 1) for i in range(begin, devices - 1, 2)] for begin in (1, 0)]
     swaps = [pair + [(j, i) for i, j in pair] for pair in pairs]
     odd_rows, even_rows, stage = fetch(frame_counts, frame_rows)
+    even_pair = lax.ppermute(even_rows, "cp", swaps[1])
     odd_pair = lax.ppermute(odd_rows, "cp", swaps[0])
-    even_pair = lax.ppermute(even_rows, "cp", swaps[1])
-    sums, own, tokens, taps, copies, gain, folded, placed, gram = inner(
-        stage,
-        conv_weight,
-        query_weight.T,
-        patch_weight,
-        frame_embed,
-        query_gain[None, :],
-        latent_proj.T,
-        norm_gain[None, :],
+    sums, own, tokens, taps, copies, gain = inner(
+        stage, conv_weight, latent_proj.T, norm_gain[None, :]
+    )
+    folded, placed, gram, added = fold(
+        gain, frame_counts, query_weight.T, patch_weight, frame_embed, query_gain[None, :]
     )
     parts = outer_even(frame_counts, even_pair, taps, sums, own, tokens, copies, gain, placed)
     message = outer_odd(odd_pair, taps, sums, own, tokens, copies, gain, parts, folded)
     arrived = lax.all_to_all(message, "cp", split_axis=0, concat_axis=0, tiled=True)
-    return project(frame_counts, arrived, gram, jnp.asarray(spread_table(), BF))
+    return project(arrived, gram, added, jnp.asarray(spread_table(), BF))
 
 
 def solution(mesh):

time: 50.1 us -> 49.6 us (0.990)
  Pallas kernels: 21 us -> 20.3 us
    pallas_call x1, Pallas kernels: 12.3 us -> 10.6 us  [inner(): pl.pallas_call(inner_kernel, out_shape=(jax.ShapeDtypeStruct((2, FRAMES *...]
    pallas_call x0 -> x1, Pallas kernels: none -> 1.39 us  [fold(): pl.pallas_call(fold_kernel, out_shape=(jax.ShapeDtypeStruct((PART // 2, L...]
where the time goes in v5:
time: 49.6 us; the launch traced here: 49.5 us
  blocking collectives  23.8 us (48%)
  Pallas kernels  20.3 us (41%)
  starting transfers between devices  5.22 us (11%)
    all_to_all x1, blocking collectives, local(): lax.all_to_all(message, 'cp', split_axis=0, concat_axis=0, tiled=True)  23.8 us
    pallas_call x1, Pallas kernels, inner(): pl.pallas_call(inner_kernel, out_shape=(jax.ShapeDtypeStruct((2, FRAMES *...  10.6 us
    ppermute x1, starting transfers between devices, local(): even_pair = lax.ppermute(even_rows, 'cp', swaps[1])  4.53 us
    pallas_call x1, Pallas kernels, project(): pl.pallas_call(project_kernel, out_shape=jax.ShapeDtypeStruct((HEADS, TOK...  2.56 us
    pallas_call x1, Pallas kernels, fetch(): pl.pallas_call(fetch_kernel, out_shape=(pltpu.VMEM((FRAMES, WIDTH, C), BF...  2.39 us
    pallas_call x1, Pallas kernels, outer_even(): pl.pallas_call(outer_even_kernel, out_shape=jax.ShapeDtypeStruct((6, FRAM...  1.71 us
    pallas_call x1, Pallas kernels, outer_odd(): pl.pallas_call(outer_odd_kernel, out_shape=jax.ShapeDtypeStruct((FRAMES,...  1.65 us
    pallas_call x1, Pallas kernels, fold(): pl.pallas_call(fold_kernel, out_shape=(jax.ShapeDtypeStruct((PART // 2, L...  1.39 us
  transfers between devices with their start and end apart: 2, of which 0 were waited for; matrix products, arithmetic and copies ran while one was open for 0% of the time, Pallas kernels for 28%

profile of v5, /device:TPU:0, one launch (start us, length us, event | category | flops | bytes accessed | tf_op | source)
XLA Modules:
  0.0 49.5 jit_solution(693796908435445706)
XLA Ops:
  0.0 2.4 %fetch.1 = (bf16[64,8,512]{2,1,0:T(8,128)(2,1)S(1)}, bf16[64,8,512]{2,1,0:T(8,128)(2,1)S(1)}, bf16[64,4,8,512]{3,2,1,0:T(8,128)(2,1)S(1)}) custom-call(s32[16]{0:T(128)} %listed.1, bf16[96,4,8,512]{3,2,1,0:T(8,128)(2,1)} %frames.1), custom_call_target="tpu_custom_call" | custom-call | bytes 4194304 | tf_op jit(solution)/shard_map/fetch/pallas_call | solution.py:77
  2.4 0.7 %collective-permute-start = (bf16[64,8,512]{2,1,0:T(8,128)(2,1)S(1)}, bf16[64,8,512]{2,1,0:T(8,128)(2,1)S(1)}, u32[]{:S(2)}, u32[]{:S(2)}) collective-permute-start(bf16[64,8,512]{2,1,0:T(8,128)(2,1)S(1)} %get-tuple-element.18), channel_id=1, source_target_pairs={{2,4},{6,8},{10,12},{14,16},{18,20},{22,24},{26,28},{30,32},{34,36... | collective-permute-start | bytes 1572872 | tf_op jit(solution)/shard_map/ppermute | solution.py:447
  3.1 4.5 %collective-permute-start.1 = (bf16[64,8,512]{2,1,0:T(8,128)(2,1)S(1)}, bf16[64,8,512]{2,1,0:T(8,128)(2,1)S(1)}, u32[]{:S(2)}, u32[]{:S(2)}) collective-permute-start(bf16[64,8,512]{2,1,0:T(8,128)(2,1)S(1)} %get-tuple-element.26), channel_id=1, source_target_pairs={{0,2},{4,6},{8,10},{12,14},{16,18},{20,22},{24,26},{28,30},{32,34}... | collective-permute-start | bytes 1572872 | tf_op jit(solution)/shard_map/ppermute | solution.py:446
  7.6 0.0 copy-start.1
  7.6 0.0 copy-start.2
  7.6 0.0 copy-start.3
  7.6 0.0 copy-start.4
  7.6 0.0 copy-start.5
  7.7 10.6 %inner.1 = (f32[2,512,512]{2,1,0:T(8,128)S(1)}, bf16[2,512,512]{2,1,0:T(8,128)(2,1)S(1)}, f32[8,64,128]{2,1,0:T(8,128)S(1)}, bf16[3,1536,512]{2,1,0:T(8,128)(2,1...) custom-call(bf16[64,4,8,512]{3,2,1,0:T(8,128)(2,1)S(1)} %get-tuple-element.19.stage, ...), custom_call_target="tpu_custom_call" | custom-call | flops 8000000000 | bytes 9437184 | tf_op jit(solution)/shard_map/inner/pallas_call | solution.py:192
  18.3 0.0 copy-done.1
  18.3 0.0 copy-done.2
  18.3 0.0 copy-done.3
  18.3 0.0 copy-done.4
  18.3 0.0 copy-done.5
  18.3 1.4 %fold.1 = (f32[24,128]{1,0:T(8,128)S(1)}, f32[16,128]{1,0:T(8,128)S(1)}, bf16[3,64,64]{2,1,0:T(8,128)(2,1)S(1)}, f32[2,64]{1,0:T(2,128)S(1)}) custom-call(f32[1,512]{1,0:T(1,128)S(1)} %get-tuple-element.25.after.gain, s32[16]{0:T(128)S(1)} %copy-done.1, bf16[48,3072]{1,0:T(8,128)(2,1)S(1)} %bitcast.4, bf16[64,3072]{1,0:T(8,128)(2,1)S(1)} %copy-done.2, ...), custom_call_target="tpu_custom_call" | custom-call | flops 1000000000 | bytes 1048576 | tf_op jit(solution)/shard_map/fold/pallas_call | solution.py:343
  19.7 0.0 collective-permute-done.1.halo
  19.7 1.7 %outer_even.1.parts = f32[6,64,128]{2,1,0:T(8,128)S(1)} custom-call(s32[16]{0:T(128)} %listed.1, bf16[64,8,512]{2,1,0:T(8,128)(2,1)S(1)} %collective-permute-done.1.halo, bf16[3,1536,512]{2,1,0:T(8,128)(2,1)S(1)} %get-tuple-element.20.taps, f32[2,512,512]{2,1,0:T(8,128)S(1)} %get-tuple-element.21.sums, bf16[2,512,512]{2,1,0:T(8,128)(2,1)S(1)} %get-tuple-element.22.own, ...), custom_call_target="tpu_custom_call" | custom-call | flops 800000000 | bytes 4194304 | tf_op jit(solution)/shard_map/outer_even/pallas_call | solution.py:262
  21.5 0.0 collective-permute-done.halo
  21.5 0.0 copy-start
  21.5 1.6 %outer_odd.1 = bf16[64,32,128]{2,1,0:T(8,128)(2,1)S(1)} custom-call(bf16[64,8,512]{2,1,0:T(8,128)(2,1)S(1)} %collective-permute-done.halo, bf16[3,1536,512]{2,1,0:T(8,128)(2,1)S(1)} %get-tuple-element.20.taps, f32[2,512,512]{2,1,0:T(8,128)S(1)} %get-tuple-element.21.sums, bf16[2,512,512]{2,1,0:T(8,128)(2,1)S(1)} %get-tuple-element.22.own, ...), custom_call_target="tpu_custom_call" | custom-call | flops 800000000 | bytes 4194304 | tf_op jit(solution)/shard_map/outer_odd/pallas_call | solution.py:290
  23.1 23.8 %all_to_all.5.arrived = bf16[64,32,128]{2,1,0:T(8,128)(2,1)S(1)} all-to-all(bf16[64,32,128]{2,1,0:T(8,128)(2,1)S(1)} %outer_odd.1), channel_id=1, replica_groups=mesh['cp'=64,'dp'=2] {'cp'}, dimensions={0} | all-to-all | bytes 1048576 | tf_op jit(solution)/shard_map/all_to_all | solution.py:456
  46.9 0.0 copy-done
  46.9 2.6 %project.1 = bf16[24,512,128]{2,1,0:T(8,128)(2,1)} custom-call(bf16[64,32,128]{2,1,0:T(8,128)(2,1)S(1)} %all_to_all.5.arrived, bf16[3,64,64]{2,1,0:T(8,128)(2,1)S(1)} %get-tuple-element.29.gram, f32[2,64]{1,0:T(2,128)S(1)} %get-tuple-element.30.added, bf16[128,384]{1,0:T(8,128)(2,1)S(1)} %copy-done), custom_call_target="tpu_custom_call" | custom-call | flops 800000000 | bytes 5242880 | tf_op jit(solution)/shard_map/project/pallas_call | solution.py:405
Async XLA Ops:
  2.4 19.1 %collective-permute-start = (bf16[64,8,512]{2,1,0:T(8,128)(2,1)S(1)}, bf16[64,8,512]{2,1,0:T(8,128)(2,1)S(1)}, u32[]{:S(2)}, u32[]{:S(2)}) collective-permute-start(bf16[64,8,512]{2,1,0:T(8,128)(2,1)S(1)} %get-tuple-element.18), channel_id=1, source_target_pairs={{2,4},{6,8},{10,12},{14,16},{18,20},{22,24},{26,28},{30,32},{34,36... | collective-permute-start | bytes 1572872 | tf_op jit(solution)/shard_map/ppermute | solution.py:447
  3.1 16.6 %collective-permute-start.1 = (bf16[64,8,512]{2,1,0:T(8,128)(2,1)S(1)}, bf16[64,8,512]{2,1,0:T(8,128)(2,1)S(1)}, u32[]{:S(2)}, u32[]{:S(2)}) collective-permute-start(bf16[64,8,512]{2,1,0:T(8,128)(2,1)S(1)} %get-tuple-element.26), channel_id=1, source_target_pairs={{0,2},{4,6},{8,10},{12,14},{16,18},{20,22},{24,26},{28,30},{32,34}... | collective-permute-start | bytes 1572872 | tf_op jit(solution)/shard_map/ppermute | solution.py:446
  7.6 10.7 %copy-start.1 = (s32[16]{0:T(128)S(1)}, s32[16]{0:T(128)}, u32[]{:S(2)}) copy-start(s32[16]{0:T(128)} %listed.1) | copy-start | bytes 196
  7.6 10.7 %copy-start.2 = (bf16[64,3072]{1,0:T(8,128)(2,1)S(1)}, bf16[64,3072]{1,0:T(8,128)(2,1)}, u32[]{:S(2)}) copy-start(bf16[64,3072]{1,0:T(8,128)(2,1)} %patch.1) | copy-start | bytes 1179652
  7.6 10.7 %copy-start.3 = (bf16[3072,48]{0,1:T(8,128)(2,1)S(1)}, bf16[3072,48]{0,1:T(8,128)(2,1)}, u32[]{:S(2)}) copy-start(bf16[3072,48]{0,1:T(8,128)(2,1)} %param.18) | copy-start | bytes 884740
  7.6 10.7 %copy-start.4 = (bf16[6,3072]{1,0:T(8,128)(2,1)S(1)}, bf16[6,3072]{1,0:T(8,128)(2,1)}, u32[]{:S(2)}) copy-start(bf16[6,3072]{1,0:T(8,128)(2,1)} %embed.1) | copy-start | bytes 110596
  7.6 10.7 %copy-start.5 = (f32[3072]{0:T(1024)S(1)}, f32[3072]{0:T(1024)}, u32[]{:S(2)}) copy-start(f32[3072]{0:T(1024)} %param.17) | copy-start | bytes 36868
  21.5 25.4 %copy-start = (bf16[128,384]{1,0:T(8,128)(2,1)S(1)}, bf16[128,384]{1,0:T(8,128)(2,1)}, u32[]{:S(2)}) copy-start(bf16[128,384]{1,0:T(8,128)(2,1)} %constant.2.clone.spread) | copy-start | bytes 294916

commit v6 on v5

--- a/solution.py
+++ b/solution.py
@@ -49,11 +49,10 @@
 
 
 def each_clip(counts, body):
-    def step(clip, start):
+    start = 0
+    for clip in range(CLIPS):
         body(clip, start, counts[clip])
-        return start + counts[clip]
-
-    lax.fori_loop(0, CLIPS, step, 0)
+        start = start + counts[clip]
 
 
 def is_odd():
@@ -93,7 +92,7 @@
     residual = frame.astype(F32) + 0.5 * summed * (1.0 + jnp.tanh(0.5 * summed))
     mean = jnp.mean(residual * residual, axis=-1, keepdims=True)
     normed = (residual * lax.rsqrt(mean + EPSILON) * gain).astype(BF)
-    return nt(normed, proj)
+    return dot(normed, proj)
 
 
 def in_patch(latent, below):
@@ -110,9 +109,8 @@
 
 
 def spread_proj(proj, copies):
-    copies[...] = jnp.zeros_like(copies)
-    for copy in range(4):
-        copies[copy * LAT : (copy + 1) * LAT, :] = proj[...]
+    four = jnp.concatenate([proj[...].astype(F32)] * 4 + [jnp.zeros((LANES - 4 * LAT, C), F32)], axis=0)
+    copies[...] = four.T.astype(BF)
 
 
 def by_column(row, wide, cols, lane):
@@ -196,7 +194,7 @@
             jax.ShapeDtypeStruct((2, FRAMES * WIDTH, C), BF),
             jax.ShapeDtypeStruct((8, FRAMES, LANES), F32),
             jax.ShapeDtypeStruct((3, 3 * C, C), BF),
-            jax.ShapeDtypeStruct((LANES, C), BF),
+            jax.ShapeDtypeStruct((C, LANES), BF),
             jax.ShapeDtypeStruct((1, C), F32),
         ),
         in_specs=[VMEM] + [HBM] * 3,
@@ -299,8 +297,10 @@
     )(halo, taps, sums, own, tokens, copies, gain, parts, folded)
 
 
-def fold_kernel(after, counts, columns, patch, embed, scale, folded, placed, gram, added, table, rows):
+def fold_kernel(after, listed, columns, patch, embed, scale, folded, placed, gram, added, table, rows, counts, sem):
     del after
+    load = pltpu.make_async_copy(listed, counts, sem)
+    load.start()
     table[0:64, :] = patch[...]
     table[64:80, :] = jnp.concatenate(
         [embed[...].astype(F32), jnp.zeros((16 - MAXF, HID), F32)], axis=0
@@ -319,24 +319,24 @@
     placed[...] = pltpu.roll(product[128:144] + product[144:160], 64, 1)
     product = nt(table[...], table[...])
     matrix = product[:64, :64]
-    for part in range(3):
-        piece = matrix.astype(BF)
-        gram[part] = piece
-        matrix = matrix - piece.astype(F32)
+    pieces = []
+    for _ in range(3):
+        pieces.append(matrix.astype(BF).astype(F32))
+        matrix = matrix - pieces[-1]
+    pieces = jnp.concatenate([*pieces, jnp.zeros((64, 64), F32)], axis=1)
+    gram[...] = jnp.concatenate([pieces, jnp.zeros((64, 256), F32)], axis=0).astype(BF)
     own = lax.axis_index("cp")
-
-    def clip(at, carry):
-        start, begin = carry
+    load.wait()
+    start, begin = 0, 0
+    for clip in range(CLIPS):
         begin = jnp.where(start <= own, start, begin)
-        return start + counts[at], begin
-
-    _, begin = lax.fori_loop(0, CLIPS, clip, (0, 0))
+        start = start + counts[clip]
     line = lax.broadcasted_iota(jnp.int32, (16, 80), 0)
     position = jnp.sum(jnp.where(line == own - begin, product[64:], 0.0), axis=0, keepdims=True)
     lane = lax.broadcasted_iota(jnp.int32, (1, 80), 1)
     square = jnp.sum(jnp.where(lane == 64 + own - begin, position, 0.0), axis=1, keepdims=True)
-    added[0:1, :] = 2.0 * position[:, :64]
-    added[1:2, :] = jnp.broadcast_to(square, (1, 64))
+    added[0:1, :] = jnp.concatenate([2.0 * position[:, :64], jnp.zeros((1, 64), F32)], axis=1)
+    added[1:2, :] = jnp.broadcast_to(square, (1, LANES))
 
 
 def fold(after, counts, columns, patch, embed, scale):
@@ -345,19 +345,24 @@
         out_shape=(
             jax.ShapeDtypeStruct((PART // 2, LANES), F32),
             jax.ShapeDtypeStruct((16, LANES), F32),
-            jax.ShapeDtypeStruct((3, 64, 64), BF),
-            jax.ShapeDtypeStruct((2, 64), F32),
+            jax.ShapeDtypeStruct((LANES, 256), BF),
+            jax.ShapeDtypeStruct((2, LANES), F32),
         ),
-        in_specs=[VMEM, SMEM] + [VMEM] * 4,
+        in_specs=[VMEM, HBM] + [VMEM] * 4,
         out_specs=(VMEM,) * 4,
-        scratch_shapes=[pltpu.VMEM((80, HID), BF), pltpu.VMEM((160, HID), BF)],
+        scratch_shapes=[
+            pltpu.VMEM((80, HID), BF),
+            pltpu.VMEM((160, HID), BF),
+            pltpu.SMEM((CLIPS,), jnp.int32),
+            pltpu.SemaphoreType.DMA,
+        ],
         compiler_params=pltpu.CompilerParams(vmem_limit_bytes=8 * MIB),
         cost_estimate=pl.CostEstimate(flops=1_000_000_000, bytes_accessed=MIB, transcendentals=0),
         name="fold",
-    )(after, counts, columns, patch, embed, scale)
-
-
-GROUP = 3
+    )(after, in_hbm(counts), columns, patch, embed, scale)
+
+
+GROUP = 4
 
 
 def project_kernel(arrived, gram, added, spread, out, flat, columns, shift, held, sems):
@@ -365,7 +370,12 @@
     flat[...] = got[:, 0:8].reshape(TOKENS, LANES)
     lane = lax.broadcasted_iota(jnp.int32, (TOKENS, LANES), 1)
     token = jnp.where(lane < 64, flat[...], 0.0)
-    query = (token + pltpu.roll(token, 64, 1)).astype(BF)
+    token = token + pltpu.roll(token, 64, 1)
+    query = token.astype(BF)
+    product = dot(query, gram[...])
+    total = (product[:, :LANES] + product[:, LANES:] + added[0:1, :]) * token
+    total = jnp.sum(total, axis=-1, keepdims=True) + added[1:2, 0:1]
+    scale = lax.rsqrt(jnp.maximum(total, 0.0) * (1.0 / HID) + EPSILON)
     rest = got[:, 8:MESSAGE]
     lane = lax.broadcasted_iota(jnp.int32, rest.shape, 2)
     low, high = jnp.where(lane < 64, rest, 0.0), jnp.where(lane < 64, 0.0, rest)
@@ -382,12 +392,6 @@
         shift[:, block * 8 * PART : (block + 1) * 8 * PART] = jnp.sum(
             jnp.where(mask, laid[block * 8 : (block + 1) * 8], 0.0), axis=0, keepdims=True
         )
-    token = token[:, 0:64]
-    total = jnp.zeros((TOKENS, 64), F32) + added[0:1, :]
-    for part in range(3):
-        total = total + dot(token.astype(BF), gram[part])
-    total = jnp.sum(total * token, axis=-1, keepdims=True) + added[1:2, 0:1]
-    scale = lax.rsqrt(jnp.maximum(total, 0.0) * (1.0 / HID) + EPSILON)
     copies = []
     for group in range(HEADS // GROUP):
         at = slice(group * GROUP * HEAD_DIM, (group + 1) * GROUP * HEAD_DIM)

time: 49.6 us -> 49.4 us (level)
  Pallas kernels: 20.3 us -> 19.5 us
    pallas_call x1, Pallas kernels: 1.39 us -> 0.79 us  [fold(): pl.pallas_call(fold_kernel, out_shape=(jax.ShapeDtypeStruct((PART // 2, L...]
  transfers between devices with their start and end apart: 2 -> 2, of which waited for: 0 -> 1; matrix products, arithmetic and copies ran while one was open for 0% -> 0% of each run, Pallas kernels for 28% -> 27%
where the time goes in v6:
time: 49.4 us; the launch traced here: 49.2 us
  blocking collectives  24.2 us (49%)
  Pallas kernels  19.5 us (39%)
  starting transfers between devices  5.22 us (11%)
    all_to_all x1, blocking collectives, local(): lax.all_to_all(message, 'cp', split_axis=0, concat_axis=0, tiled=True)  24.2 us
    pallas_call x1, Pallas kernels, inner(): pl.pallas_call(inner_kernel, out_shape=(jax.ShapeDtypeStruct((2, FRAMES *...  10.7 us
    ppermute x1, starting transfers between devices, local(): even_pair = lax.ppermute(even_rows, 'cp', swaps[1])  4.53 us
    pallas_call x1, Pallas kernels, fetch(): pl.pallas_call(fetch_kernel, out_shape=(pltpu.VMEM((FRAMES, WIDTH, C), BF...  2.36 us
    pallas_call x1, Pallas kernels, project(): pl.pallas_call(project_kernel, out_shape=jax.ShapeDtypeStruct((HEADS, TOK...  2.32 us
    pallas_call x1, Pallas kernels, outer_even(): pl.pallas_call(outer_even_kernel, out_shape=jax.ShapeDtypeStruct((6, FRAM...  1.71 us
    pallas_call x1, Pallas kernels, outer_odd(): pl.pallas_call(outer_odd_kernel, out_shape=jax.ShapeDtypeStruct((FRAMES,...  1.65 us
  transfers between devices with their start and end apart: 2, of which 1 were waited for; matrix products, arithmetic and copies ran while one was open for 0% of the time, Pallas kernels for 27%

profile of v6, /device:TPU:0, one launch (start us, length us, event | category | flops | bytes accessed | tf_op | source)
XLA Modules:
  0.0 49.2 jit_solution(17450291504635462347)
XLA Ops:
  0.0 2.4 %fetch.1 = (bf16[64,8,512]{2,1,0:T(8,128)(2,1)S(1)}, bf16[64,8,512]{2,1,0:T(8,128)(2,1)S(1)}, bf16[64,4,8,512]{3,2,1,0:T(8,128)(2,1)S(1)}) custom-call(s32[16]{0:T(128)} %listed.3, bf16[96,4,8,512]{3,2,1,0:T(8,128)(2,1)} %frames.1), custom_call_target="tpu_custom_call" | custom-call | bytes 4194304 | tf_op jit(solution)/shard_map/fetch/pallas_call | solution.py:76
  2.4 0.7 %collective-permute-start = (bf16[64,8,512]{2,1,0:T(8,128)(2,1)S(1)}, bf16[64,8,512]{2,1,0:T(8,128)(2,1)S(1)}, u32[]{:S(2)}, u32[]{:S(2)}) collective-permute-start(bf16[64,8,512]{2,1,0:T(8,128)(2,1)S(1)} %get-tuple-element.18), channel_id=1, source_target_pairs={{2,4},{6,8},{10,12},{14,16},{18,20},{22,24},{26,28},{30,32},{34,36... | collective-permute-start | bytes 1572872 | tf_op jit(solution)/shard_map/ppermute | solution.py:451
  3.1 4.5 %collective-permute-start.1 = (bf16[64,8,512]{2,1,0:T(8,128)(2,1)S(1)}, bf16[64,8,512]{2,1,0:T(8,128)(2,1)S(1)}, u32[]{:S(2)}, u32[]{:S(2)}) collective-permute-start(bf16[64,8,512]{2,1,0:T(8,128)(2,1)S(1)} %get-tuple-element.26), channel_id=1, source_target_pairs={{0,2},{4,6},{8,10},{12,14},{16,18},{20,22},{24,26},{28,30},{32,34}... | collective-permute-start | bytes 1572872 | tf_op jit(solution)/shard_map/ppermute | solution.py:450
  7.6 0.0 copy-start.1
  7.6 0.0 copy-start.2
  7.6 0.0 copy-start.3
  7.6 0.0 copy-start.4
  7.6 10.7 %inner.1 = (f32[2,512,512]{2,1,0:T(8,128)S(1)}, bf16[2,512,512]{2,1,0:T(8,128)(2,1)S(1)}, f32[8,64,128]{2,1,0:T(8,128)S(1)}, bf16[3,1536,512]{2,1,0:T(8,128)(2,1...) custom-call(bf16[64,4,8,512]{3,2,1,0:T(8,128)(2,1)S(1)} %get-tuple-element.19.stage, ...), custom_call_target="tpu_custom_call" | custom-call | flops 8000000000 | bytes 9437184 | tf_op jit(solution)/shard_map/inner/pallas_call | solution.py:190
  18.3 0.0 copy-done.1
  18.3 0.0 copy-done.2
  18.3 0.0 copy-done.3
  18.4 0.0 copy-done.4
  18.4 0.8 %fold.1 = (f32[24,128]{1,0:T(8,128)S(1)}, f32[16,128]{1,0:T(8,128)S(1)}, bf16[128,256]{1,0:T(8,128)(2,1)S(1)}, f32[2,128]{1,0:T(2,128)S(1)}) custom-call(f32[1,512]{1,0:T(1,128)S(1)} %get-tuple-element.25.after.gain, s32[16]{0:T(128)} %listed.3, bf16[48,3072]{1,0:T(8,128)(2,1)S(1)} %bitcast.4, bf16[64,3072]{1,0:T(8,128)(2,1)S(1)} %copy-done.1, ...), custom_call_target="tpu_custom_call" | custom-call | flops 1000000000 | bytes 1048576 | tf_op jit(solution)/shard_map/fold/pallas_call | solution.py:343
  19.2 0.1 collective-permute-done.1.halo
  19.2 1.7 %outer_even.1.parts = f32[6,64,128]{2,1,0:T(8,128)S(1)} custom-call(s32[16]{0:T(128)} %listed.3, bf16[64,8,512]{2,1,0:T(8,128)(2,1)S(1)} %collective-permute-done.1.halo, bf16[3,1536,512]{2,1,0:T(8,128)(2,1)S(1)} %get-tuple-element.20.taps, f32[2,512,512]{2,1,0:T(8,128)S(1)} %get-tuple-element.21.sums, bf16[2,512,512]{2,1,0:T(8,128)(2,1)S(1)} %get-tuple-element.22.own, ...), custom_call_target="tpu_custom_call" | custom-call | flops 800000000 | bytes 4194304 | tf_op jit(solution)/shard_map/outer_even/pallas_call | solution.py:260
  21.0 0.0 collective-permute-done.halo
  21.0 0.0 copy-start
  21.0 1.6 %outer_odd.1 = bf16[64,32,128]{2,1,0:T(8,128)(2,1)S(1)} custom-call(bf16[64,8,512]{2,1,0:T(8,128)(2,1)S(1)} %collective-permute-done.halo, bf16[3,1536,512]{2,1,0:T(8,128)(2,1)S(1)} %get-tuple-element.20.taps, f32[2,512,512]{2,1,0:T(8,128)S(1)} %get-tuple-element.21.sums, bf16[2,512,512]{2,1,0:T(8,128)(2,1)S(1)} %get-tuple-element.22.own, ...), custom_call_target="tpu_custom_call" | custom-call | flops 800000000 | bytes 4194304 | tf_op jit(solution)/shard_map/outer_odd/pallas_call | solution.py:288
  22.6 24.2 %all_to_all.5.arrived = bf16[64,32,128]{2,1,0:T(8,128)(2,1)S(1)} all-to-all(bf16[64,32,128]{2,1,0:T(8,128)(2,1)S(1)} %outer_odd.1), channel_id=1, replica_groups=mesh['cp'=64,'dp'=2] {'cp'}, dimensions={0} | all-to-all | bytes 1048576 | tf_op jit(solution)/shard_map/all_to_all | solution.py:460
  46.9 0.0 copy-done
  46.9 2.3 %project.1 = bf16[24,512,128]{2,1,0:T(8,128)(2,1)} custom-call(bf16[64,32,128]{2,1,0:T(8,128)(2,1)S(1)} %all_to_all.5.arrived, bf16[128,256]{1,0:T(8,128)(2,1)S(1)} %get-tuple-element.29.gram, f32[2,128]{1,0:T(2,128)S(1)} %get-tuple-element.30.added, bf16[128,384]{1,0:T(8,128)(2,1)S(1)} %copy-done), custom_call_target="tpu_custom_call" | custom-call | flops 800000000 | bytes 5242880 | tf_op jit(solution)/shard_map/project/pallas_call | solution.py:409
Async XLA Ops:
  2.4 18.6 %collective-permute-start = (bf16[64,8,512]{2,1,0:T(8,128)(2,1)S(1)}, bf16[64,8,512]{2,1,0:T(8,128)(2,1)S(1)}, u32[]{:S(2)}, u32[]{:S(2)}) collective-permute-start(bf16[64,8,512]{2,1,0:T(8,128)(2,1)S(1)} %get-tuple-element.18), channel_id=1, source_target_pairs={{2,4},{6,8},{10,12},{14,16},{18,20},{22,24},{26,28},{30,32},{34,36... | collective-permute-start | bytes 1572872 | tf_op jit(solution)/shard_map/ppermute | solution.py:451
  3.1 16.2 %collective-permute-start.1 = (bf16[64,8,512]{2,1,0:T(8,128)(2,1)S(1)}, bf16[64,8,512]{2,1,0:T(8,128)(2,1)S(1)}, u32[]{:S(2)}, u32[]{:S(2)}) collective-permute-start(bf16[64,8,512]{2,1,0:T(8,128)(2,1)S(1)} %get-tuple-element.26), channel_id=1, source_target_pairs={{0,2},{4,6},{8,10},{12,14},{16,18},{20,22},{24,26},{28,30},{32,34}... | collective-permute-start | bytes 1572872 | tf_op jit(solution)/shard_map/ppermute | solution.py:450
  7.6 10.7 %copy-start.1 = (bf16[64,3072]{1,0:T(8,128)(2,1)S(1)}, bf16[64,3072]{1,0:T(8,128)(2,1)}, u32[]{:S(2)}) copy-start(bf16[64,3072]{1,0:T(8,128)(2,1)} %patch.1) | copy-start | bytes 1179652
  7.6 10.7 %copy-start.2 = (bf16[3072,48]{0,1:T(8,128)(2,1)S(1)}, bf16[3072,48]{0,1:T(8,128)(2,1)}, u32[]{:S(2)}) copy-start(bf16[3072,48]{0,1:T(8,128)(2,1)} %param.18) | copy-start | bytes 884740
  7.6 10.7 %copy-start.3 = (bf16[6,3072]{1,0:T(8,128)(2,1)S(1)}, bf16[6,3072]{1,0:T(8,128)(2,1)}, u32[]{:S(2)}) copy-start(bf16[6,3072]{1,0:T(8,128)(2,1)} %embed.1) | copy-start | bytes 110596
  7.6 10.8 %copy-start.4 = (f32[3072]{0:T(1024)S(1)}, f32[3072]{0:T(1024)}, u32[]{:S(2)}) copy-start(f32[3072]{0:T(1024)} %param.17) | copy-start | bytes 36868
  21.0 25.9 %copy-start = (bf16[128,384]{1,0:T(8,128)(2,1)S(1)}, bf16[128,384]{1,0:T(8,128)(2,1)}, u32[]{:S(2)}) copy-start(bf16[128,384]{1,0:T(8,128)(2,1)} %constant.2.clone.spread) | copy-start | bytes 294916

commit v7 on v6

--- a/solution.py
+++ b/solution.py
@@ -20,6 +20,7 @@
 CLIPS = 16
 PART = HID // FRAMES
 TOKENS = 512
+SPARE = 64
 LANES = 128
 MESSAGE = 32
 EPSILON = 1e-06
@@ -116,7 +117,7 @@
 def by_column(row, wide, cols, lane):
     row = row.astype(F32).reshape(FRAMES * WIDTH, C)
     for piece in range(C // LANES):
-        wide[piece] = row[:, piece * LANES : (piece + 1) * LANES]
+        wide[piece, 0 : FRAMES * WIDTH] = row[:, piece * LANES : (piece + 1) * LANES]
     for column in range(WIDTH):
         blocks = [wide[piece, pl.ds(column, FRAMES, stride=WIDTH), :] for piece in range(C // LANES)]
         block = jnp.concatenate(blocks, axis=1).astype(BF)
@@ -200,7 +201,7 @@
         in_specs=[VMEM] + [HBM] * 3,
         out_specs=(VMEM,) * 6,
         scratch_shapes=[
-            pltpu.VMEM((STRIP, C // LANES, FRAMES * WIDTH, LANES), F32),
+            pltpu.VMEM((STRIP, C // LANES, FRAMES * WIDTH + SPARE, LANES), F32),
             pltpu.VMEM((FRAMES * WIDTH, STRIP * C), BF),
             pltpu.VMEM((2, FRAMES * WIDTH, C), F32),
             pltpu.VMEM((LAT, C), BF),
@@ -228,7 +229,7 @@
 
 def outer_scratch():
     return [
-        pltpu.VMEM((C // LANES, FRAMES * WIDTH, LANES), F32),
+        pltpu.VMEM((C // LANES, FRAMES * WIDTH + SPARE, LANES), F32),
         pltpu.VMEM((FRAMES * WIDTH, C), BF),
         pltpu.VMEM((FRAMES * WIDTH, C), F32),
     ]
@@ -281,7 +282,7 @@
             value = value + parts[4 + index]
         flat[pl.ds(index, FRAMES, stride=8), :] = value
     rest = jnp.broadcast_to(folded[...][None], (FRAMES, PART // 2, LANES))
-    message[...] = jnp.concatenate([flat[...].reshape(FRAMES, 8, LANES), rest], axis=1).astype(BF)
+    message[...] = jnp.concatenate([flat[0:TOKENS].reshape(FRAMES, 8, LANES), rest], axis=1).astype(BF)
 
 
 def outer_odd(halo, taps, sums, own, tokens, copies, gain, parts, folded):
@@ -290,7 +291,7 @@
         out_shape=jax.ShapeDtypeStruct((FRAMES, MESSAGE, LANES), BF),
         in_specs=[VMEM] * 9,
         out_specs=VMEM,
-        scratch_shapes=outer_scratch() + [pltpu.VMEM((TOKENS, LANES), F32)],
+        scratch_shapes=outer_scratch() + [pltpu.VMEM((TOKENS + SPARE, LANES), F32)],
         compiler_params=pltpu.CompilerParams(vmem_limit_bytes=24 * MIB),
         cost_estimate=pl.CostEstimate(flops=800_000_000, bytes_accessed=4 * MIB, transcendentals=MIB // 4),
         name="outer_odd",
@@ -367,9 +368,10 @@
 
 def project_kernel(arrived, gram, added, spread, out, flat, columns, shift, held, sems):
     got = arrived[...].astype(F32)
-    flat[...] = got[:, 0:8].reshape(TOKENS, LANES)
+    rows = got[:, 0:8].reshape(TOKENS, LANES)
+    flat[0:TOKENS] = rows
     lane = lax.broadcasted_iota(jnp.int32, (TOKENS, LANES), 1)
-    token = jnp.where(lane < 64, flat[...], 0.0)
+    token = jnp.where(lane < 64, rows, 0.0)
     token = token + pltpu.roll(token, 64, 1)
     query = token.astype(BF)
     product = dot(query, gram[...])
@@ -412,7 +414,7 @@
         in_specs=[VMEM] * 4,
         out_specs=HBM,
         scratch_shapes=[
-            pltpu.VMEM((TOKENS, LANES), F32),
+            pltpu.VMEM((TOKENS + SPARE, LANES), F32),
             pltpu.VMEM((HID, LANES), BF),
             pltpu.VMEM((1, HID), F32),
             pltpu.VMEM((HEADS, TOKENS, HEAD_DIM), BF),

time: 49.4 us -> 49.4 us (level)
  no operation moved by 1% of the time
where the time goes in v7:
time: 49.4 us; the launch traced here: 49.2 us
  blocking collectives  24.3 us (49%)
  Pallas kernels  19.5 us (39%)
  starting transfers between devices  5.22 us (11%)
    all_to_all x1, blocking collectives, local(): lax.all_to_all(message, 'cp', split_axis=0, concat_axis=0, tiled=True)  24.3 us
    pallas_call x1, Pallas kernels, inner(): pl.pallas_call(inner_kernel, out_shape=(jax.ShapeDtypeStruct((2, FRAMES *...  10.7 us
    ppermute x1, starting transfers between devices, local(): even_pair = lax.ppermute(even_rows, 'cp', swaps[1])  4.53 us
    pallas_call x1, Pallas kernels, fetch(): pl.pallas_call(fetch_kernel, out_shape=(pltpu.VMEM((FRAMES, WIDTH, C), BF...  2.34 us
    pallas_call x1, Pallas kernels, project(): pl.pallas_call(project_kernel, out_shape=jax.ShapeDtypeStruct((HEADS, TOK...  2.34 us
    pallas_call x1, Pallas kernels, outer_even(): pl.pallas_call(outer_even_kernel, out_shape=jax.ShapeDtypeStruct((6, FRAM...  1.71 us
    pallas_call x1, Pallas kernels, outer_odd(): pl.pallas_call(outer_odd_kernel, out_shape=jax.ShapeDtypeStruct((FRAMES,...  1.65 us
  transfers between devices with their start and end apart: 2, of which 1 were waited for; matrix products, arithmetic and copies ran while one was open for 0% of the time, Pallas kernels for 27%

profile of v7, /device:TPU:0, one launch (start us, length us, event | category | flops | bytes accessed | tf_op | source)
XLA Modules:
  0.0 49.2 jit_solution(13270252499847355440)
XLA Ops:
  0.0 2.3 %fetch.1 = (bf16[64,8,512]{2,1,0:T(8,128)(2,1)S(1)}, bf16[64,8,512]{2,1,0:T(8,128)(2,1)S(1)}, bf16[64,4,8,512]{3,2,1,0:T(8,128)(2,1)S(1)}) custom-call(s32[16]{0:T(128)} %listed.3, bf16[96,4,8,512]{3,2,1,0:T(8,128)(2,1)} %frames.1), custom_call_target="tpu_custom_call" | custom-call | bytes 4194304 | tf_op jit(solution)/shard_map/fetch/pallas_call | solution.py:77
  2.4 0.7 %collective-permute-start = (bf16[64,8,512]{2,1,0:T(8,128)(2,1)S(1)}, bf16[64,8,512]{2,1,0:T(8,128)(2,1)S(1)}, u32[]{:S(2)}, u32[]{:S(2)}) collective-permute-start(bf16[64,8,512]{2,1,0:T(8,128)(2,1)S(1)} %get-tuple-element.18), channel_id=1, source_target_pairs={{2,4},{6,8},{10,12},{14,16},{18,20},{22,24},{26,28},{30,32},{34,36... | collective-permute-start | bytes 1572872 | tf_op jit(solution)/shard_map/ppermute | solution.py:453
  3.1 4.5 %collective-permute-start.1 = (bf16[64,8,512]{2,1,0:T(8,128)(2,1)S(1)}, bf16[64,8,512]{2,1,0:T(8,128)(2,1)S(1)}, u32[]{:S(2)}, u32[]{:S(2)}) collective-permute-start(bf16[64,8,512]{2,1,0:T(8,128)(2,1)S(1)} %get-tuple-element.26), channel_id=1, source_target_pairs={{0,2},{4,6},{8,10},{12,14},{16,18},{20,22},{24,26},{28,30},{32,34}... | collective-permute-start | bytes 1572872 | tf_op jit(solution)/shard_map/ppermute | solution.py:452
  7.6 0.0 copy-start.1
  7.6 0.0 copy-start.2
  7.6 0.0 copy-start.3
  7.6 0.0 copy-start.4
  7.6 10.7 %inner.1 = (f32[2,512,512]{2,1,0:T(8,128)S(1)}, bf16[2,512,512]{2,1,0:T(8,128)(2,1)S(1)}, f32[8,64,128]{2,1,0:T(8,128)S(1)}, bf16[3,1536,512]{2,1,0:T(8,128)(2,1...) custom-call(bf16[64,4,8,512]{3,2,1,0:T(8,128)(2,1)S(1)} %get-tuple-element.19.stage, ...), custom_call_target="tpu_custom_call" | custom-call | flops 8000000000 | bytes 9437184 | tf_op jit(solution)/shard_map/inner/pallas_call | solution.py:191
  18.3 0.0 copy-done.1
  18.3 0.0 copy-done.2
  18.3 0.0 copy-done.3
  18.3 0.0 copy-done.4
  18.4 0.8 %fold.1 = (f32[24,128]{1,0:T(8,128)S(1)}, f32[16,128]{1,0:T(8,128)S(1)}, bf16[128,256]{1,0:T(8,128)(2,1)S(1)}, f32[2,128]{1,0:T(2,128)S(1)}) custom-call(f32[1,512]{1,0:T(1,128)S(1)} %get-tuple-element.25.after.gain, s32[16]{0:T(128)} %listed.3, bf16[48,3072]{1,0:T(8,128)(2,1)S(1)} %bitcast.4, bf16[64,3072]{1,0:T(8,128)(2,1)S(1)} %copy-done.1, ...), custom_call_target="tpu_custom_call" | custom-call | flops 1000000000 | bytes 1048576 | tf_op jit(solution)/shard_map/fold/pallas_call | solution.py:344
  19.2 0.1 collective-permute-done.1.halo
  19.2 1.7 %outer_even.1.parts = f32[6,64,128]{2,1,0:T(8,128)S(1)} custom-call(s32[16]{0:T(128)} %listed.3, bf16[64,8,512]{2,1,0:T(8,128)(2,1)S(1)} %collective-permute-done.1.halo, bf16[3,1536,512]{2,1,0:T(8,128)(2,1)S(1)} %get-tuple-element.20.taps, f32[2,512,512]{2,1,0:T(8,128)S(1)} %get-tuple-element.21.sums, bf16[2,512,512]{2,1,0:T(8,128)(2,1)S(1)} %get-tuple-element.22.own, ...), custom_call_target="tpu_custom_call" | custom-call | flops 800000000 | bytes 4194304 | tf_op jit(solution)/shard_map/outer_even/pallas_call | solution.py:261
  21.0 0.0 collective-permute-done.halo
  21.0 0.0 copy-start
  21.0 1.6 %outer_odd.1 = bf16[64,32,128]{2,1,0:T(8,128)(2,1)S(1)} custom-call(bf16[64,8,512]{2,1,0:T(8,128)(2,1)S(1)} %collective-permute-done.halo, bf16[3,1536,512]{2,1,0:T(8,128)(2,1)S(1)} %get-tuple-element.20.taps, f32[2,512,512]{2,1,0:T(8,128)S(1)} %get-tuple-element.21.sums, bf16[2,512,512]{2,1,0:T(8,128)(2,1)S(1)} %get-tuple-element.22.own, ...), custom_call_target="tpu_custom_call" | custom-call | flops 800000000 | bytes 4194304 | tf_op jit(solution)/shard_map/outer_odd/pallas_call | solution.py:289
  22.6 24.3 %all_to_all.5.arrived = bf16[64,32,128]{2,1,0:T(8,128)(2,1)S(1)} all-to-all(bf16[64,32,128]{2,1,0:T(8,128)(2,1)S(1)} %outer_odd.1), channel_id=1, replica_groups=mesh['cp'=64,'dp'=2] {'cp'}, dimensions={0} | all-to-all | bytes 1048576 | tf_op jit(solution)/shard_map/all_to_all | solution.py:462
  46.9 0.0 copy-done
  46.9 2.3 %project.1 = bf16[24,512,128]{2,1,0:T(8,128)(2,1)} custom-call(bf16[64,32,128]{2,1,0:T(8,128)(2,1)S(1)} %all_to_all.5.arrived, bf16[128,256]{1,0:T(8,128)(2,1)S(1)} %get-tuple-element.29.gram, f32[2,128]{1,0:T(2,128)S(1)} %get-tuple-element.30.added, bf16[128,384]{1,0:T(8,128)(2,1)S(1)} %copy-done), custom_call_target="tpu_custom_call" | custom-call | flops 800000000 | bytes 5242880 | tf_op jit(solution)/shard_map/project/pallas_call | solution.py:411
Async XLA Ops:
  2.4 18.6 %collective-permute-start = (bf16[64,8,512]{2,1,0:T(8,128)(2,1)S(1)}, bf16[64,8,512]{2,1,0:T(8,128)(2,1)S(1)}, u32[]{:S(2)}, u32[]{:S(2)}) collective-permute-start(bf16[64,8,512]{2,1,0:T(8,128)(2,1)S(1)} %get-tuple-element.18), channel_id=1, source_target_pairs={{2,4},{6,8},{10,12},{14,16},{18,20},{22,24},{26,28},{30,32},{34,36... | collective-permute-start | bytes 1572872 | tf_op jit(solution)/shard_map/ppermute | solution.py:453
  3.1 16.2 %collective-permute-start.1 = (bf16[64,8,512]{2,1,0:T(8,128)(2,1)S(1)}, bf16[64,8,512]{2,1,0:T(8,128)(2,1)S(1)}, u32[]{:S(2)}, u32[]{:S(2)}) collective-permute-start(bf16[64,8,512]{2,1,0:T(8,128)(2,1)S(1)} %get-tuple-element.26), channel_id=1, source_target_pairs={{0,2},{4,6},{8,10},{12,14},{16,18},{20,22},{24,26},{28,30},{32,34}... | collective-permute-start | bytes 1572872 | tf_op jit(solution)/shard_map/ppermute | solution.py:452
  7.6 10.7 %copy-start.1 = (bf16[64,3072]{1,0:T(8,128)(2,1)S(1)}, bf16[64,3072]{1,0:T(8,128)(2,1)}, u32[]{:S(2)}) copy-start(bf16[64,3072]{1,0:T(8,128)(2,1)} %patch.1) | copy-start | bytes 1179652
  7.6 10.7 %copy-start.2 = (bf16[3072,48]{0,1:T(8,128)(2,1)S(1)}, bf16[3072,48]{0,1:T(8,128)(2,1)}, u32[]{:S(2)}) copy-start(bf16[3072,48]{0,1:T(8,128)(2,1)} %param.18) | copy-start | bytes 884740
  7.6 10.7 %copy-start.3 = (bf16[6,3072]{1,0:T(8,128)(2,1)S(1)}, bf16[6,3072]{1,0:T(8,128)(2,1)}, u32[]{:S(2)}) copy-start(bf16[6,3072]{1,0:T(8,128)(2,1)} %embed.1) | copy-start | bytes 110596
  7.6 10.8 %copy-start.4 = (f32[3072]{0:T(1024)S(1)}, f32[3072]{0:T(1024)}, u32[]{:S(2)}) copy-start(f32[3072]{0:T(1024)} %param.17) | copy-start | bytes 36868
  21.0 25.9 %copy-start = (bf16[128,384]{1,0:T(8,128)(2,1)S(1)}, bf16[128,384]{1,0:T(8,128)(2,1)}, u32[]{:S(2)}) copy-start(bf16[128,384]{1,0:T(8,128)(2,1)} %constant.2.clone.spread) | copy-start | bytes 294916

commit v8 on v7

--- a/solution.py
+++ b/solution.py
@@ -90,10 +90,10 @@
 
 
 def latent_of(summed, frame, gain, proj):
-    residual = frame.astype(F32) + 0.5 * summed * (1.0 + jnp.tanh(0.5 * summed))
+    half = 0.5 * summed
+    residual = frame.astype(F32) + (half + half * jnp.tanh(half))
     mean = jnp.mean(residual * residual, axis=-1, keepdims=True)
-    normed = (residual * lax.rsqrt(mean + EPSILON) * gain).astype(BF)
-    return dot(normed, proj)
+    return dot((residual * gain).astype(BF), proj) * lax.rsqrt(mean + EPSILON)
 
 
 def in_patch(latent, below):
@@ -219,7 +219,7 @@
     tap = pl.multiple_of(place * 2 * C, C)
     by_column(halo[...], wide, cols, 0)
     total[...] = sums[place]
-    for side in (1, 0, 2):
+    for side in (0, 2, 1):
         begin, end = max(0, side - 1) * FRAMES, count - max(0, 1 - side) * FRAMES
         shift = (1 - side) * FRAMES
         total[begin + shift : end + shift, :] += dot(cols[begin:end], taps[side, pl.ds(tap, C), :])

time: 49.4 us -> 49.1 us (level)
  Pallas kernels: 19.5 us -> 18.9 us
  transfers between devices with their start and end apart: 2 -> 2, of which waited for: 1 -> 1; matrix products, arithmetic and copies ran while one was open for 0% -> 0% of each run, Pallas kernels for 27% -> 26%
where the time goes in v8:
time: 49.1 us; the launch traced here: 48.9 us
  blocking collectives  24.5 us (50%)
  Pallas kernels  18.9 us (38%)
  starting transfers between devices  5.22 us (11%)
    all_to_all x1, blocking collectives, local(): lax.all_to_all(message, 'cp', split_axis=0, concat_axis=0, tiled=True)  24.5 us
    pallas_call x1, Pallas kernels, inner(): pl.pallas_call(inner_kernel, out_shape=(jax.ShapeDtypeStruct((2, FRAMES *...  10.6 us
    ppermute x1, starting transfers between devices, local(): even_pair = lax.ppermute(even_rows, 'cp', swaps[1])  4.53 us
    pallas_call x1, Pallas kernels, fetch(): pl.pallas_call(fetch_kernel, out_shape=(pltpu.VMEM((FRAMES, WIDTH, C), BF...  2.39 us
    pallas_call x1, Pallas kernels, project(): pl.pallas_call(project_kernel, out_shape=jax.ShapeDtypeStruct((HEADS, TOK...  2.34 us
    pallas_call x1, Pallas kernels, outer_even(): pl.pallas_call(outer_even_kernel, out_shape=jax.ShapeDtypeStruct((6, FRAM...  1.42 us
    pallas_call x1, Pallas kernels, outer_odd(): pl.pallas_call(outer_odd_kernel, out_shape=jax.ShapeDtypeStruct((FRAMES,...  1.36 us
  transfers between devices with their start and end apart: 2, of which 1 were waited for; matrix products, arithmetic and copies ran while one was open for 0% of the time, Pallas kernels for 26%

profile of v8, /device:TPU:0, one launch (start us, length us, event | category | flops | bytes accessed | tf_op | source)
XLA Modules:
  0.0 48.9 jit_solution(9517608210682008381)
XLA Ops:
  0.0 2.4 %fetch.1 = (bf16[64,8,512]{2,1,0:T(8,128)(2,1)S(1)}, bf16[64,8,512]{2,1,0:T(8,128)(2,1)S(1)}, bf16[64,4,8,512]{3,2,1,0:T(8,128)(2,1)S(1)}) custom-call(s32[16]{0:T(128)} %listed.3, bf16[96,4,8,512]{3,2,1,0:T(8,128)(2,1)} %frames.1), custom_call_target="tpu_custom_call" | custom-call | bytes 4194304 | tf_op jit(solution)/shard_map/fetch/pallas_call | solution.py:77
  2.4 0.7 %collective-permute-start = (bf16[64,8,512]{2,1,0:T(8,128)(2,1)S(1)}, bf16[64,8,512]{2,1,0:T(8,128)(2,1)S(1)}, u32[]{:S(2)}, u32[]{:S(2)}) collective-permute-start(bf16[64,8,512]{2,1,0:T(8,128)(2,1)S(1)} %get-tuple-element.18), channel_id=1, source_target_pairs={{2,4},{6,8},{10,12},{14,16},{18,20},{22,24},{26,28},{30,32},{34,36... | collective-permute-start | bytes 1572872 | tf_op jit(solution)/shard_map/ppermute | solution.py:453
  3.1 4.5 %collective-permute-start.1 = (bf16[64,8,512]{2,1,0:T(8,128)(2,1)S(1)}, bf16[64,8,512]{2,1,0:T(8,128)(2,1)S(1)}, u32[]{:S(2)}, u32[]{:S(2)}) collective-permute-start(bf16[64,8,512]{2,1,0:T(8,128)(2,1)S(1)} %get-tuple-element.26), channel_id=1, source_target_pairs={{0,2},{4,6},{8,10},{12,14},{16,18},{20,22},{24,26},{28,30},{32,34}... | collective-permute-start | bytes 1572872 | tf_op jit(solution)/shard_map/ppermute | solution.py:452
  7.6 0.0 copy-start.1
  7.6 0.0 copy-start.2
  7.6 0.0 copy-start.3
  7.6 0.0 copy-start.4
  7.6 10.6 %inner.1 = (f32[2,512,512]{2,1,0:T(8,128)S(1)}, bf16[2,512,512]{2,1,0:T(8,128)(2,1)S(1)}, f32[8,64,128]{2,1,0:T(8,128)S(1)}, bf16[3,1536,512]{2,1,0:T(8,128)(2,1...) custom-call(bf16[64,4,8,512]{3,2,1,0:T(8,128)(2,1)S(1)} %get-tuple-element.19.stage, ...), custom_call_target="tpu_custom_call" | custom-call | flops 8000000000 | bytes 9437184 | tf_op jit(solution)/shard_map/inner/pallas_call | solution.py:191
  18.2 0.0 copy-done.1
  18.2 0.0 copy-done.2
  18.2 0.0 copy-done.3
  18.3 0.0 copy-done.4
  18.3 0.8 %fold.1 = (f32[24,128]{1,0:T(8,128)S(1)}, f32[16,128]{1,0:T(8,128)S(1)}, bf16[128,256]{1,0:T(8,128)(2,1)S(1)}, f32[2,128]{1,0:T(2,128)S(1)}) custom-call(f32[1,512]{1,0:T(1,128)S(1)} %get-tuple-element.25.after.gain, s32[16]{0:T(128)} %listed.3, bf16[48,3072]{1,0:T(8,128)(2,1)S(1)} %bitcast.4, bf16[64,3072]{1,0:T(8,128)(2,1)S(1)} %copy-done.1, ...), custom_call_target="tpu_custom_call" | custom-call | flops 1000000000 | bytes 1048576 | tf_op jit(solution)/shard_map/fold/pallas_call | solution.py:344
  19.1 0.2 collective-permute-done.1.halo
  19.2 1.4 %outer_even.1.parts = f32[6,64,128]{2,1,0:T(8,128)S(1)} custom-call(s32[16]{0:T(128)} %listed.3, bf16[64,8,512]{2,1,0:T(8,128)(2,1)S(1)} %collective-permute-done.1.halo, bf16[3,1536,512]{2,1,0:T(8,128)(2,1)S(1)} %get-tuple-element.20.taps, f32[2,512,512]{2,1,0:T(8,128)S(1)} %get-tuple-element.21.sums, bf16[2,512,512]{2,1,0:T(8,128)(2,1)S(1)} %get-tuple-element.22.own, ...), custom_call_target="tpu_custom_call" | custom-call | flops 800000000 | bytes 4194304 | tf_op jit(solution)/shard_map/outer_even/pallas_call | solution.py:261
  20.7 0.0 collective-permute-done.halo
  20.7 0.0 copy-start
  20.7 1.4 %outer_odd.1 = bf16[64,32,128]{2,1,0:T(8,128)(2,1)S(1)} custom-call(bf16[64,8,512]{2,1,0:T(8,128)(2,1)S(1)} %collective-permute-done.halo, bf16[3,1536,512]{2,1,0:T(8,128)(2,1)S(1)} %get-tuple-element.20.taps, f32[2,512,512]{2,1,0:T(8,128)S(1)} %get-tuple-element.21.sums, bf16[2,512,512]{2,1,0:T(8,128)(2,1)S(1)} %get-tuple-element.22.own, ...), custom_call_target="tpu_custom_call" | custom-call | flops 800000000 | bytes 4194304 | tf_op jit(solution)/shard_map/outer_odd/pallas_call | solution.py:289
  22.0 24.5 %all_to_all.5.arrived = bf16[64,32,128]{2,1,0:T(8,128)(2,1)S(1)} all-to-all(bf16[64,32,128]{2,1,0:T(8,128)(2,1)S(1)} %outer_odd.1), channel_id=1, replica_groups=mesh['cp'=64,'dp'=2] {'cp'}, dimensions={0} | all-to-all | bytes 1048576 | tf_op jit(solution)/shard_map/all_to_all | solution.py:462
  46.5 0.0 copy-done
  46.5 2.3 %project.1 = bf16[24,512,128]{2,1,0:T(8,128)(2,1)} custom-call(bf16[64,32,128]{2,1,0:T(8,128)(2,1)S(1)} %all_to_all.5.arrived, bf16[128,256]{1,0:T(8,128)(2,1)S(1)} %get-tuple-element.29.gram, f32[2,128]{1,0:T(2,128)S(1)} %get-tuple-element.30.added, bf16[128,384]{1,0:T(8,128)(2,1)S(1)} %copy-done), custom_call_target="tpu_custom_call" | custom-call | flops 800000000 | bytes 5242880 | tf_op jit(solution)/shard_map/project/pallas_call | solution.py:411
Async XLA Ops:
  2.4 18.3 %collective-permute-start = (bf16[64,8,512]{2,1,0:T(8,128)(2,1)S(1)}, bf16[64,8,512]{2,1,0:T(8,128)(2,1)S(1)}, u32[]{:S(2)}, u32[]{:S(2)}) collective-permute-start(bf16[64,8,512]{2,1,0:T(8,128)(2,1)S(1)} %get-tuple-element.18), channel_id=1, source_target_pairs={{2,4},{6,8},{10,12},{14,16},{18,20},{22,24},{26,28},{30,32},{34,36... | collective-permute-start | bytes 1572872 | tf_op jit(solution)/shard_map/ppermute | solution.py:453
  3.1 16.1 %collective-permute-start.1 = (bf16[64,8,512]{2,1,0:T(8,128)(2,1)S(1)}, bf16[64,8,512]{2,1,0:T(8,128)(2,1)S(1)}, u32[]{:S(2)}, u32[]{:S(2)}) collective-permute-start(bf16[64,8,512]{2,1,0:T(8,128)(2,1)S(1)} %get-tuple-element.26), channel_id=1, source_target_pairs={{0,2},{4,6},{8,10},{12,14},{16,18},{20,22},{24,26},{28,30},{32,34}... | collective-permute-start | bytes 1572872 | tf_op jit(solution)/shard_map/ppermute | solution.py:452
  7.6 10.6 %copy-start.1 = (bf16[64,3072]{1,0:T(8,128)(2,1)S(1)}, bf16[64,3072]{1,0:T(8,128)(2,1)}, u32[]{:S(2)}) copy-start(bf16[64,3072]{1,0:T(8,128)(2,1)} %patch.1) | copy-start | bytes 1179652
  7.6 10.6 %copy-start.2 = (bf16[3072,48]{0,1:T(8,128)(2,1)S(1)}, bf16[3072,48]{0,1:T(8,128)(2,1)}, u32[]{:S(2)}) copy-start(bf16[3072,48]{0,1:T(8,128)(2,1)} %param.18) | copy-start | bytes 884740
  7.6 10.6 %copy-start.3 = (bf16[6,3072]{1,0:T(8,128)(2,1)S(1)}, bf16[6,3072]{1,0:T(8,128)(2,1)}, u32[]{:S(2)}) copy-start(bf16[6,3072]{1,0:T(8,128)(2,1)} %embed.1) | copy-start | bytes 110596
  7.6 10.6 %copy-start.4 = (f32[3072]{0:T(1024)S(1)}, f32[3072]{0:T(1024)}, u32[]{:S(2)}) copy-start(f32[3072]{0:T(1024)} %param.17) | copy-start | bytes 36868
  20.7 25.9 %copy-start = (bf16[128,384]{1,0:T(8,128)(2,1)S(1)}, bf16[128,384]{1,0:T(8,128)(2,1)}, u32[]{:S(2)}) copy-start(bf16[128,384]{1,0:T(8,128)(2,1)} %constant.2.clone.spread) | copy-start | bytes 294916

commit v9 on v8

--- a/solution.py
+++ b/solution.py
@@ -235,42 +235,26 @@
     ]
 
 
-def outer_even_kernel(listed, halo, taps, sums, own, tokens, copies, gain, placed, parts, *scratch):
-    *scratch, counts, sem = scratch
-    load = pltpu.make_async_copy(listed, counts, sem)
-    load.start()
+def outer_even_kernel(halo, taps, sums, own, tokens, copies, gain, parts, *scratch):
     place = 1 - is_odd()
     for patch, value in enumerate(edge_row(place, halo, taps, sums, own, copies, gain, *scratch)):
         parts[patch] = tokens[place * 4 + patch] + value
-    load.wait()
-    frame = lax.broadcasted_iota(jnp.int32, (FRAMES, 1), 0)
-    begin = jnp.zeros((FRAMES, 1), jnp.int32)
-    start = 0
-    for clip in range(CLIPS):
-        begin = jnp.where(frame >= start, start, begin)
-        start = start + counts[clip]
-    position = jnp.zeros((FRAMES, LANES), F32)
-    for offset in range(MAXF):
-        position = position + jnp.where(frame - begin == offset, placed[offset : offset + 1, :], 0.0)
-    high, low = split(position)
-    parts[4] = high.astype(F32)
-    parts[5] = low.astype(F32)
-
-
-def outer_even(counts, halo, taps, sums, own, tokens, copies, gain, placed):
+
+
+def outer_even(halo, taps, sums, own, tokens, copies, gain):
     return pl.pallas_call(
         outer_even_kernel,
-        out_shape=jax.ShapeDtypeStruct((6, FRAMES, LANES), F32),
-        in_specs=[HBM] + [VMEM] * 8,
+        out_shape=jax.ShapeDtypeStruct((4, FRAMES, LANES), F32),
+        in_specs=[VMEM] * 7,
         out_specs=VMEM,
-        scratch_shapes=outer_scratch() + [pltpu.SMEM((CLIPS,), jnp.int32), pltpu.SemaphoreType.DMA],
+        scratch_shapes=outer_scratch(),
         compiler_params=pltpu.CompilerParams(vmem_limit_bytes=24 * MIB),
         cost_estimate=pl.CostEstimate(flops=800_000_000, bytes_accessed=4 * MIB, transcendentals=MIB // 4),
         name="outer_even",
-    )(in_hbm(counts), halo, taps, sums, own, tokens, copies, gain, placed)
-
-
-def outer_odd_kernel(halo, taps, sums, own, tokens, copies, gain, parts, folded, message, *scratch):
+    )(halo, taps, sums, own, tokens, copies, gain)
+
+
+def outer_odd_kernel(halo, taps, sums, own, tokens, copies, gain, parts, placed, folded, message, *scratch):
     *scratch, flat = scratch
     place = is_odd()
     mine = edge_row(place, halo, taps, sums, own, copies, gain, *scratch)
@@ -279,23 +263,23 @@
     for index in range(8):
         value = jnp.where(place == index // 4, mine[index % 4], parts[index % 4])
         if index < 2:
-            value = value + parts[4 + index]
+            value = value + placed[index]
         flat[pl.ds(index, FRAMES, stride=8), :] = value
     rest = jnp.broadcast_to(folded[...][None], (FRAMES, PART // 2, LANES))
     message[...] = jnp.concatenate([flat[0:TOKENS].reshape(FRAMES, 8, LANES), rest], axis=1).astype(BF)
 
 
-def outer_odd(halo, taps, sums, own, tokens, copies, gain, parts, folded):
+def outer_odd(halo, taps, sums, own, tokens, copies, gain, parts, placed, folded):
     return pl.pallas_call(
         outer_odd_kernel,
         out_shape=jax.ShapeDtypeStruct((FRAMES, MESSAGE, LANES), BF),
-        in_specs=[VMEM] * 9,
+        in_specs=[VMEM] * 10,
         out_specs=VMEM,
         scratch_shapes=outer_scratch() + [pltpu.VMEM((TOKENS + SPARE, LANES), F32)],
         compiler_params=pltpu.CompilerParams(vmem_limit_bytes=24 * MIB),
         cost_estimate=pl.CostEstimate(flops=800_000_000, bytes_accessed=4 * MIB, transcendentals=MIB // 4),
         name="outer_odd",
-    )(halo, taps, sums, own, tokens, copies, gain, parts, folded)
+    )(halo, taps, sums, own, tokens, copies, gain, parts, placed, folded)
 
 
 def fold_kernel(after, listed, columns, patch, embed, scale, folded, placed, gram, added, table, rows, counts, sem):
@@ -317,7 +301,7 @@
     both = jnp.concatenate([both, both], axis=1)
     lane = lax.broadcasted_iota(jnp.int32, (PART // 2, LANES), 1)
     folded[...] = jnp.where(lane < 64, both[: PART // 2], both[PART // 2 : PART])
-    placed[...] = pltpu.roll(product[128:144] + product[144:160], 64, 1)
+    offsets = pltpu.roll(product[128:144] + product[144:160], 64, 1)
     product = nt(table[...], table[...])
     matrix = product[:64, :64]
     pieces = []
@@ -329,9 +313,18 @@
     own = lax.axis_index("cp")
     load.wait()
     start, begin = 0, 0
+    frame = lax.broadcasted_iota(jnp.int32, (FRAMES, 1), 0)
+    begins = jnp.zeros((FRAMES, 1), jnp.int32)
     for clip in range(CLIPS):
         begin = jnp.where(start <= own, start, begin)
+        begins = jnp.where(frame >= start, start, begins)
         start = start + counts[clip]
+    position = jnp.zeros((FRAMES, LANES), F32)
+    for offset in range(MAXF):
+        position = position + jnp.where(frame - begins == offset, offsets[offset : offset + 1, :], 0.0)
+    high, low = split(position)
+    placed[0] = high.astype(F32)
+    placed[1] = low.astype(F32)
     line = lax.broadcasted_iota(jnp.int32, (16, 80), 0)
     position = jnp.sum(jnp.where(line == own - begin, product[64:], 0.0), axis=0, keepdims=True)
     lane = lax.broadcasted_iota(jnp.int32, (1, 80), 1)
@@ -345,7 +338,7 @@
         fold_kernel,
         out_shape=(
             jax.ShapeDtypeStruct((PART // 2, LANES), F32),
-            jax.ShapeDtypeStruct((16, LANES), F32),
+            jax.ShapeDtypeStruct((2, FRAMES, LANES), F32),
             jax.ShapeDtypeStruct((LANES, 256), BF),
             jax.ShapeDtypeStruct((2, LANES), F32),
         ),
@@ -457,8 +450,8 @@
     folded, placed, gram, added = fold(
         gain, frame_counts, query_weight.T, patch_weight, frame_embed, query_gain[None, :]
     )
-    parts = outer_even(frame_counts, even_pair, taps, sums, own, tokens, copies, gain, placed)
-    message = outer_odd(odd_pair, taps, sums, own, tokens, copies, gain, parts, folded)
+    parts = outer_even(even_pair, taps, sums, own, tokens, copies, gain)
+    message = outer_odd(odd_pair, taps, sums, own, tokens, copies, gain, parts, placed, folded)
     arrived = lax.all_to_all(message, "cp", split_axis=0, concat_axis=0, tiled=True)
     return project(arrived, gram, added, jnp.asarray(spread_table(), BF))
 

time: 49.1 us -> 49.1 us (level)
  no operation moved by 1% of the time
where the time goes in v9:
time: 49.1 us; the launch traced here: 49 us
  blocking collectives  24.6 us (50%)
  Pallas kernels  18.8 us (38%)
  starting transfers between devices  5.22 us (11%)
    all_to_all x1, blocking collectives, local(): lax.all_to_all(message, 'cp', split_axis=0, concat_axis=0, tiled=True)  24.6 us
    pallas_call x1, Pallas kernels, inner(): pl.pallas_call(inner_kernel, out_shape=(jax.ShapeDtypeStruct((2, FRAMES *...  10.6 us
    ppermute x1, starting transfers between devices, local(): even_pair = lax.ppermute(even_rows, 'cp', swaps[1])  4.53 us
    pallas_call x1, Pallas kernels, fetch(): pl.pallas_call(fetch_kernel, out_shape=(pltpu.VMEM((FRAMES, WIDTH, C), BF...  2.37 us
    pallas_call x1, Pallas kernels, project(): pl.pallas_call(project_kernel, out_shape=jax.ShapeDtypeStruct((HEADS, TOK...  2.34 us
    pallas_call x1, Pallas kernels, outer_odd(): pl.pallas_call(outer_odd_kernel, out_shape=jax.ShapeDtypeStruct((FRAMES,...  1.36 us
    pallas_call x1, Pallas kernels, outer_even(): pl.pallas_call(outer_even_kernel, out_shape=jax.ShapeDtypeStruct((4, FRAM...  1.32 us
  transfers between devices with their start and end apart: 2, of which 1 were waited for; matrix products, arithmetic and copies ran while one was open for 0% of the time, Pallas kernels for 26%

profile of v9, /device:TPU:0, one launch (start us, length us, event | category | flops | bytes accessed | tf_op | source)
XLA Modules:
  0.0 49.0 jit_solution(7626736458226631266)
XLA Ops:
  0.0 2.4 %fetch.1 = (bf16[64,8,512]{2,1,0:T(8,128)(2,1)S(1)}, bf16[64,8,512]{2,1,0:T(8,128)(2,1)S(1)}, bf16[64,4,8,512]{3,2,1,0:T(8,128)(2,1)S(1)}) custom-call(s32[16]{0:T(128)} %listed.1, bf16[96,4,8,512]{3,2,1,0:T(8,128)(2,1)} %frames.1), custom_call_target="tpu_custom_call" | custom-call | bytes 4194304 | tf_op jit(solution)/shard_map/fetch/pallas_call | solution.py:77
  2.4 0.7 %collective-permute-start = (bf16[64,8,512]{2,1,0:T(8,128)(2,1)S(1)}, bf16[64,8,512]{2,1,0:T(8,128)(2,1)S(1)}, u32[]{:S(2)}, u32[]{:S(2)}) collective-permute-start(bf16[64,8,512]{2,1,0:T(8,128)(2,1)S(1)} %get-tuple-element.18), channel_id=1, source_target_pairs={{2,4},{6,8},{10,12},{14,16},{18,20},{22,24},{26,28},{30,32},{34,36... | collective-permute-start | bytes 1572872 | tf_op jit(solution)/shard_map/ppermute | solution.py:446
  3.1 4.5 %collective-permute-start.1 = (bf16[64,8,512]{2,1,0:T(8,128)(2,1)S(1)}, bf16[64,8,512]{2,1,0:T(8,128)(2,1)S(1)}, u32[]{:S(2)}, u32[]{:S(2)}) collective-permute-start(bf16[64,8,512]{2,1,0:T(8,128)(2,1)S(1)} %get-tuple-element.26), channel_id=1, source_target_pairs={{0,2},{4,6},{8,10},{12,14},{16,18},{20,22},{24,26},{28,30},{32,34}... | collective-permute-start | bytes 1572872 | tf_op jit(solution)/shard_map/ppermute | solution.py:445
  7.6 0.0 copy-start.1
  7.6 0.0 copy-start.2
  7.6 0.0 copy-start.3
  7.6 0.0 copy-start.4
  7.6 10.6 %inner.1 = (f32[2,512,512]{2,1,0:T(8,128)S(1)}, bf16[2,512,512]{2,1,0:T(8,128)(2,1)S(1)}, f32[8,64,128]{2,1,0:T(8,128)S(1)}, bf16[3,1536,512]{2,1,0:T(8,128)(2,1...) custom-call(bf16[64,4,8,512]{3,2,1,0:T(8,128)(2,1)S(1)} %get-tuple-element.19.stage, ...), custom_call_target="tpu_custom_call" | custom-call | flops 8000000000 | bytes 9437184 | tf_op jit(solution)/shard_map/inner/pallas_call | solution.py:191
  18.2 0.0 copy-done.1
  18.2 0.0 copy-done.2
  18.2 0.0 copy-done.3
  18.2 0.0 copy-done.4
  18.2 0.8 %fold.1 = (f32[24,128]{1,0:T(8,128)S(1)}, f32[2,64,128]{2,1,0:T(8,128)S(1)}, bf16[128,256]{1,0:T(8,128)(2,1)S(1)}, f32[2,128]{1,0:T(2,128)S(1)}) custom-call(f32[1,512]{1,0:T(1,128)S(1)} %get-tuple-element.25.gain.after, s32[16]{0:T(128)} %listed.1, bf16[48,3072]{1,0:T(8,128)(2,1)S(1)} %bitcast.4, bf16[64,3072]{1,0:T(8,128)(2,1)S(1)} %copy-done.1, ...), custom_call_target="tpu_custom_call" | custom-call | flops 1000000000 | bytes 1048576 | tf_op jit(solution)/shard_map/fold/pallas_call | solution.py:337
  19.1 0.2 collective-permute-done.1.halo
  19.3 1.3 %outer_even.1.parts = f32[4,64,128]{2,1,0:T(8,128)S(1)} custom-call(bf16[64,8,512]{2,1,0:T(8,128)(2,1)S(1)} %collective-permute-done.1.halo, bf16[3,1536,512]{2,1,0:T(8,128)(2,1)S(1)} %get-tuple-element.20.taps, f32[2,512,512]{2,1,0:T(8,128)S(1)} %get-tuple-element.21.sums, bf16[2,512,512]{2,1,0:T(8,128)(2,1)S(1)} %get-tuple-element.22.own, ...), custom_call_target="tpu_custom_call" | custom-call | flops 800000000 | bytes 4194304 | tf_op jit(solution)/shard_map/outer_even/pallas_call | solution.py:245
  20.6 0.0 collective-permute-done.halo
  20.6 0.0 copy-start
  20.6 1.4 %outer_odd.1 = bf16[64,32,128]{2,1,0:T(8,128)(2,1)S(1)} custom-call(bf16[64,8,512]{2,1,0:T(8,128)(2,1)S(1)} %collective-permute-done.halo, bf16[3,1536,512]{2,1,0:T(8,128)(2,1)S(1)} %get-tuple-element.20.taps, f32[2,512,512]{2,1,0:T(8,128)S(1)} %get-tuple-element.21.sums, bf16[2,512,512]{2,1,0:T(8,128)(2,1)S(1)} %get-tuple-element.22.own, ...), custom_call_target="tpu_custom_call" | custom-call | flops 800000000 | bytes 4194304 | tf_op jit(solution)/shard_map/outer_odd/pallas_call | solution.py:273
  22.0 24.6 %all_to_all.5.arrived = bf16[64,32,128]{2,1,0:T(8,128)(2,1)S(1)} all-to-all(bf16[64,32,128]{2,1,0:T(8,128)(2,1)S(1)} %outer_odd.1), channel_id=1, replica_groups=mesh['cp'=64,'dp'=2] {'cp'}, dimensions={0} | all-to-all | bytes 1048576 | tf_op jit(solution)/shard_map/all_to_all | solution.py:455
  46.6 0.0 copy-done
  46.6 2.3 %project.1 = bf16[24,512,128]{2,1,0:T(8,128)(2,1)} custom-call(bf16[64,32,128]{2,1,0:T(8,128)(2,1)S(1)} %all_to_all.5.arrived, bf16[128,256]{1,0:T(8,128)(2,1)S(1)} %get-tuple-element.29.gram, f32[2,128]{1,0:T(2,128)S(1)} %get-tuple-element.30.added, bf16[128,384]{1,0:T(8,128)(2,1)S(1)} %copy-done), custom_call_target="tpu_custom_call" | custom-call | flops 800000000 | bytes 5242880 | tf_op jit(solution)/shard_map/project/pallas_call | solution.py:404
Async XLA Ops:
  2.4 18.2 %collective-permute-start = (bf16[64,8,512]{2,1,0:T(8,128)(2,1)S(1)}, bf16[64,8,512]{2,1,0:T(8,128)(2,1)S(1)}, u32[]{:S(2)}, u32[]{:S(2)}) collective-permute-start(bf16[64,8,512]{2,1,0:T(8,128)(2,1)S(1)} %get-tuple-element.18), channel_id=1, source_target_pairs={{2,4},{6,8},{10,12},{14,16},{18,20},{22,24},{26,28},{30,32},{34,36... | collective-permute-start | bytes 1572872 | tf_op jit(solution)/shard_map/ppermute | solution.py:446
  3.1 16.2 %collective-permute-start.1 = (bf16[64,8,512]{2,1,0:T(8,128)(2,1)S(1)}, bf16[64,8,512]{2,1,0:T(8,128)(2,1)S(1)}, u32[]{:S(2)}, u32[]{:S(2)}) collective-permute-start(bf16[64,8,512]{2,1,0:T(8,128)(2,1)S(1)} %get-tuple-element.26), channel_id=1, source_target_pairs={{0,2},{4,6},{8,10},{12,14},{16,18},{20,22},{24,26},{28,30},{32,34}... | collective-permute-start | bytes 1572872 | tf_op jit(solution)/shard_map/ppermute | solution.py:445
  7.6 10.6 %copy-start.1 = (bf16[64,3072]{1,0:T(8,128)(2,1)S(1)}, bf16[64,3072]{1,0:T(8,128)(2,1)}, u32[]{:S(2)}) copy-start(bf16[64,3072]{1,0:T(8,128)(2,1)} %patch.1) | copy-start | bytes 1179652
  7.6 10.6 %copy-start.2 = (bf16[3072,48]{0,1:T(8,128)(2,1)S(1)}, bf16[3072,48]{0,1:T(8,128)(2,1)}, u32[]{:S(2)}) copy-start(bf16[3072,48]{0,1:T(8,128)(2,1)} %param.18) | copy-start | bytes 884740
  7.6 10.6 %copy-start.3 = (bf16[6,3072]{1,0:T(8,128)(2,1)S(1)}, bf16[6,3072]{1,0:T(8,128)(2,1)}, u32[]{:S(2)}) copy-start(bf16[6,3072]{1,0:T(8,128)(2,1)} %embed.1) | copy-start | bytes 110596
  7.6 10.6 %copy-start.4 = (f32[3072]{0:T(1024)S(1)}, f32[3072]{0:T(1024)}, u32[]{:S(2)}) copy-start(f32[3072]{0:T(1024)} %param.17) | copy-start | bytes 36868
  20.6 26.0 %copy-start = (bf16[128,384]{1,0:T(8,128)(2,1)S(1)}, bf16[128,384]{1,0:T(8,128)(2,1)}, u32[]{:S(2)}) copy-start(bf16[128,384]{1,0:T(8,128)(2,1)} %constant.2.clone.spread) | copy-start | bytes 294916

commit v10 on v9

--- a/solution.py
+++ b/solution.py
@@ -62,9 +62,10 @@
 
 def fetch_kernel(counts, frames, odd_rows, even_rows, stage, sem):
     def clip(at, start, count):
-        pltpu.make_async_copy(
-            frames.at[pl.ds(at * MAXF, count)], stage.at[pl.ds(start, count)], sem
-        ).start()
+        slots, places = pl.ds(at * MAXF, count), pl.ds(start, count)
+        for row in (0, 2):
+            rows = pl.ds(row, 2)
+            pltpu.make_async_copy(frames.at[slots, rows], stage.at[places, rows], sem).start()
 
     each_clip(counts, clip)
     pltpu.make_async_copy(stage, stage, sem).wait()

time: 49.1 us -> 49.1 us (level)
  no operation moved by 1% of the time
where the time goes in v10:
time: 49.1 us; the launch traced here: 48.9 us
  blocking collectives  24.7 us (50%)
  Pallas kernels  18.7 us (38%)
  starting transfers between devices  5.22 us (11%)
    all_to_all x1, blocking collectives, local(): lax.all_to_all(message, 'cp', split_axis=0, concat_axis=0, tiled=True)  24.7 us
    pallas_call x1, Pallas kernels, inner(): pl.pallas_call(inner_kernel, out_shape=(jax.ShapeDtypeStruct((2, FRAMES *...  10.6 us
    ppermute x1, starting transfers between devices, local(): even_pair = lax.ppermute(even_rows, 'cp', swaps[1])  4.53 us
    pallas_call x1, Pallas kernels, project(): pl.pallas_call(project_kernel, out_shape=jax.ShapeDtypeStruct((HEADS, TOK...  2.34 us
    pallas_call x1, Pallas kernels, fetch(): pl.pallas_call(fetch_kernel, out_shape=(pltpu.VMEM((FRAMES, WIDTH, C), BF...  2.3 us
    pallas_call x1, Pallas kernels, outer_odd(): pl.pallas_call(outer_odd_kernel, out_shape=jax.ShapeDtypeStruct((FRAMES,...  1.36 us
    pallas_call x1, Pallas kernels, outer_even(): pl.pallas_call(outer_even_kernel, out_shape=jax.ShapeDtypeStruct((4, FRAM...  1.33 us
  transfers between devices with their start and end apart: 2, of which 1 were waited for; matrix products, arithmetic and copies ran while one was open for 0% of the time, Pallas kernels for 26%

profile of v10, /device:TPU:0, one launch (start us, length us, event | category | flops | bytes accessed | tf_op | source)
XLA Modules:
  0.0 48.9 jit_solution(15599124700890803036)
XLA Ops:
  0.0 2.3 %fetch.1 = (bf16[64,8,512]{2,1,0:T(8,128)(2,1)S(1)}, bf16[64,8,512]{2,1,0:T(8,128)(2,1)S(1)}, bf16[64,4,8,512]{3,2,1,0:T(8,128)(2,1)S(1)}) custom-call(s32[16]{0:T(128)} %listed.1, bf16[96,4,8,512]{3,2,1,0:T(8,128)(2,1)} %frames.1), custom_call_target="tpu_custom_call" | custom-call | bytes 4194304 | tf_op jit(solution)/shard_map/fetch/pallas_call | solution.py:78
  2.3 0.7 %collective-permute-start = (bf16[64,8,512]{2,1,0:T(8,128)(2,1)S(1)}, bf16[64,8,512]{2,1,0:T(8,128)(2,1)S(1)}, u32[]{:S(2)}, u32[]{:S(2)}) collective-permute-start(bf16[64,8,512]{2,1,0:T(8,128)(2,1)S(1)} %get-tuple-element.18), channel_id=1, source_target_pairs={{2,4},{6,8},{10,12},{14,16},{18,20},{22,24},{26,28},{30,32},{34,36... | collective-permute-start | bytes 1572872 | tf_op jit(solution)/shard_map/ppermute | solution.py:447
  3.0 4.5 %collective-permute-start.1 = (bf16[64,8,512]{2,1,0:T(8,128)(2,1)S(1)}, bf16[64,8,512]{2,1,0:T(8,128)(2,1)S(1)}, u32[]{:S(2)}, u32[]{:S(2)}) collective-permute-start(bf16[64,8,512]{2,1,0:T(8,128)(2,1)S(1)} %get-tuple-element.26), channel_id=1, source_target_pairs={{0,2},{4,6},{8,10},{12,14},{16,18},{20,22},{24,26},{28,30},{32,34}... | collective-permute-start | bytes 1572872 | tf_op jit(solution)/shard_map/ppermute | solution.py:446
  7.5 0.0 copy-start.1
  7.5 0.0 copy-start.2
  7.5 0.0 copy-start.3
  7.5 0.0 copy-start.4
  7.6 10.6 %inner.1 = (f32[2,512,512]{2,1,0:T(8,128)S(1)}, bf16[2,512,512]{2,1,0:T(8,128)(2,1)S(1)}, f32[8,64,128]{2,1,0:T(8,128)S(1)}, bf16[3,1536,512]{2,1,0:T(8,128)(2,1...) custom-call(bf16[64,4,8,512]{3,2,1,0:T(8,128)(2,1)S(1)} %get-tuple-element.19.stage, ...), custom_call_target="tpu_custom_call" | custom-call | flops 8000000000 | bytes 9437184 | tf_op jit(solution)/shard_map/inner/pallas_call | solution.py:192
  18.1 0.0 copy-done.1
  18.1 0.0 copy-done.2
  18.2 0.0 copy-done.3
  18.2 0.0 copy-done.4
  18.2 0.8 %fold.1 = (f32[24,128]{1,0:T(8,128)S(1)}, f32[2,64,128]{2,1,0:T(8,128)S(1)}, bf16[128,256]{1,0:T(8,128)(2,1)S(1)}, f32[2,128]{1,0:T(2,128)S(1)}) custom-call(f32[1,512]{1,0:T(1,128)S(1)} %get-tuple-element.25.gain.after, s32[16]{0:T(128)} %listed.1, bf16[48,3072]{1,0:T(8,128)(2,1)S(1)} %bitcast.4, bf16[64,3072]{1,0:T(8,128)(2,1)S(1)} %copy-done.1, ...), custom_call_target="tpu_custom_call" | custom-call | flops 1000000000 | bytes 1048576 | tf_op jit(solution)/shard_map/fold/pallas_call | solution.py:338
  19.0 0.2 collective-permute-done.1.halo
  19.2 1.3 %outer_even.1.parts = f32[4,64,128]{2,1,0:T(8,128)S(1)} custom-call(bf16[64,8,512]{2,1,0:T(8,128)(2,1)S(1)} %collective-permute-done.1.halo, bf16[3,1536,512]{2,1,0:T(8,128)(2,1)S(1)} %get-tuple-element.20.taps, f32[2,512,512]{2,1,0:T(8,128)S(1)} %get-tuple-element.21.sums, bf16[2,512,512]{2,1,0:T(8,128)(2,1)S(1)} %get-tuple-element.22.own, ...), custom_call_target="tpu_custom_call" | custom-call | flops 800000000 | bytes 4194304 | tf_op jit(solution)/shard_map/outer_even/pallas_call | solution.py:246
  20.5 0.0 collective-permute-done.halo
  20.6 0.0 copy-start
  20.6 1.4 %outer_odd.1 = bf16[64,32,128]{2,1,0:T(8,128)(2,1)S(1)} custom-call(bf16[64,8,512]{2,1,0:T(8,128)(2,1)S(1)} %collective-permute-done.halo, bf16[3,1536,512]{2,1,0:T(8,128)(2,1)S(1)} %get-tuple-element.20.taps, f32[2,512,512]{2,1,0:T(8,128)S(1)} %get-tuple-element.21.sums, bf16[2,512,512]{2,1,0:T(8,128)(2,1)S(1)} %get-tuple-element.22.own, ...), custom_call_target="tpu_custom_call" | custom-call | flops 800000000 | bytes 4194304 | tf_op jit(solution)/shard_map/outer_odd/pallas_call | solution.py:274
  21.9 24.7 %all_to_all.5.arrived = bf16[64,32,128]{2,1,0:T(8,128)(2,1)S(1)} all-to-all(bf16[64,32,128]{2,1,0:T(8,128)(2,1)S(1)} %outer_odd.1), channel_id=1, replica_groups=mesh['cp'=64,'dp'=2] {'cp'}, dimensions={0} | all-to-all | bytes 1048576 | tf_op jit(solution)/shard_map/all_to_all | solution.py:456
  46.6 0.0 copy-done
  46.6 2.3 %project.1 = bf16[24,512,128]{2,1,0:T(8,128)(2,1)} custom-call(bf16[64,32,128]{2,1,0:T(8,128)(2,1)S(1)} %all_to_all.5.arrived, bf16[128,256]{1,0:T(8,128)(2,1)S(1)} %get-tuple-element.29.gram, f32[2,128]{1,0:T(2,128)S(1)} %get-tuple-element.30.added, bf16[128,384]{1,0:T(8,128)(2,1)S(1)} %copy-done), custom_call_target="tpu_custom_call" | custom-call | flops 800000000 | bytes 5242880 | tf_op jit(solution)/shard_map/project/pallas_call | solution.py:405
Async XLA Ops:
  2.3 18.2 %collective-permute-start = (bf16[64,8,512]{2,1,0:T(8,128)(2,1)S(1)}, bf16[64,8,512]{2,1,0:T(8,128)(2,1)S(1)}, u32[]{:S(2)}, u32[]{:S(2)}) collective-permute-start(bf16[64,8,512]{2,1,0:T(8,128)(2,1)S(1)} %get-tuple-element.18), channel_id=1, source_target_pairs={{2,4},{6,8},{10,12},{14,16},{18,20},{22,24},{26,28},{30,32},{34,36... | collective-permute-start | bytes 1572872 | tf_op jit(solution)/shard_map/ppermute | solution.py:447
  3.0 16.2 %collective-permute-start.1 = (bf16[64,8,512]{2,1,0:T(8,128)(2,1)S(1)}, bf16[64,8,512]{2,1,0:T(8,128)(2,1)S(1)}, u32[]{:S(2)}, u32[]{:S(2)}) collective-permute-start(bf16[64,8,512]{2,1,0:T(8,128)(2,1)S(1)} %get-tuple-element.26), channel_id=1, source_target_pairs={{0,2},{4,6},{8,10},{12,14},{16,18},{20,22},{24,26},{28,30},{32,34}... | collective-permute-start | bytes 1572872 | tf_op jit(solution)/shard_map/ppermute | solution.py:446
  7.5 10.6 %copy-start.1 = (bf16[64,3072]{1,0:T(8,128)(2,1)S(1)}, bf16[64,3072]{1,0:T(8,128)(2,1)}, u32[]{:S(2)}) copy-start(bf16[64,3072]{1,0:T(8,128)(2,1)} %patch.1) | copy-start | bytes 1179652
  7.5 10.6 %copy-start.2 = (bf16[3072,48]{0,1:T(8,128)(2,1)S(1)}, bf16[3072,48]{0,1:T(8,128)(2,1)}, u32[]{:S(2)}) copy-start(bf16[3072,48]{0,1:T(8,128)(2,1)} %param.18) | copy-start | bytes 884740
  7.5 10.6 %copy-start.3 = (bf16[6,3072]{1,0:T(8,128)(2,1)S(1)}, bf16[6,3072]{1,0:T(8,128)(2,1)}, u32[]{:S(2)}) copy-start(bf16[6,3072]{1,0:T(8,128)(2,1)} %embed.1) | copy-start | bytes 110596
  7.5 10.6 %copy-start.4 = (f32[3072]{0:T(1024)S(1)}, f32[3072]{0:T(1024)}, u32[]{:S(2)}) copy-start(f32[3072]{0:T(1024)} %param.17) | copy-start | bytes 36868
  20.6 26.0 %copy-start = (bf16[128,384]{1,0:T(8,128)(2,1)S(1)}, bf16[128,384]{1,0:T(8,128)(2,1)}, u32[]{:S(2)}) copy-start(bf16[128,384]{1,0:T(8,128)(2,1)} %constant.2.clone.spread) | copy-start | bytes 294916

commit v11 on v9

--- a/solution.py
+++ b/solution.py
@@ -235,51 +235,49 @@
     ]
 
 
-def outer_even_kernel(halo, taps, sums, own, tokens, copies, gain, parts, *scratch):
+def outer_even_kernel(halo, taps, sums, own, tokens, copies, gain, placed, parts, *scratch):
     place = 1 - is_odd()
-    for patch, value in enumerate(edge_row(place, halo, taps, sums, own, copies, gain, *scratch)):
-        parts[patch] = tokens[place * 4 + patch] + value
-
-
-def outer_even(halo, taps, sums, own, tokens, copies, gain):
+    mine = edge_row(place, halo, taps, sums, own, copies, gain, *scratch)
+    for index in range(8):
+        value = tokens[index] + jnp.where(place == index // 4, mine[index % 4], 0.0)
+        parts[index] = value + placed[index] if index < 2 else value
+
+
+def outer_even(halo, taps, sums, own, tokens, copies, gain, placed):
     return pl.pallas_call(
         outer_even_kernel,
-        out_shape=jax.ShapeDtypeStruct((4, FRAMES, LANES), F32),
-        in_specs=[VMEM] * 7,
+        out_shape=jax.ShapeDtypeStruct((8, FRAMES, LANES), F32),
+        in_specs=[VMEM] * 8,
         out_specs=VMEM,
         scratch_shapes=outer_scratch(),
         compiler_params=pltpu.CompilerParams(vmem_limit_bytes=24 * MIB),
         cost_estimate=pl.CostEstimate(flops=800_000_000, bytes_accessed=4 * MIB, transcendentals=MIB // 4),
         name="outer_even",
-    )(halo, taps, sums, own, tokens, copies, gain)
-
-
-def outer_odd_kernel(halo, taps, sums, own, tokens, copies, gain, parts, placed, folded, message, *scratch):
+    )(halo, taps, sums, own, tokens, copies, gain, placed)
+
+
+def outer_odd_kernel(halo, taps, sums, own, copies, gain, parts, folded, message, *scratch):
     *scratch, flat = scratch
     place = is_odd()
     mine = edge_row(place, halo, taps, sums, own, copies, gain, *scratch)
-    for patch in range(4):
-        mine[patch] = mine[patch] + tokens[place * 4 + patch]
     for index in range(8):
-        value = jnp.where(place == index // 4, mine[index % 4], parts[index % 4])
-        if index < 2:
-            value = value + placed[index]
+        value = parts[index] + jnp.where(place == index // 4, mine[index % 4], 0.0)
         flat[pl.ds(index, FRAMES, stride=8), :] = value
     rest = jnp.broadcast_to(folded[...][None], (FRAMES, PART // 2, LANES))
     message[...] = jnp.concatenate([flat[0:TOKENS].reshape(FRAMES, 8, LANES), rest], axis=1).astype(BF)
 
 
-def outer_odd(halo, taps, sums, own, tokens, copies, gain, parts, placed, folded):
+def outer_odd(halo, taps, sums, own, copies, gain, parts, folded):
     return pl.pallas_call(
         outer_odd_kernel,
         out_shape=jax.ShapeDtypeStruct((FRAMES, MESSAGE, LANES), BF),
-        in_specs=[VMEM] * 10,
+        in_specs=[VMEM] * 8,
         out_specs=VMEM,
         scratch_shapes=outer_scratch() + [pltpu.VMEM((TOKENS + SPARE, LANES), F32)],
         compiler_params=pltpu.CompilerParams(vmem_limit_bytes=24 * MIB),
         cost_estimate=pl.CostEstimate(flops=800_000_000, bytes_accessed=4 * MIB, transcendentals=MIB // 4),
         name="outer_odd",
-    )(halo, taps, sums, own, tokens, copies, gain, parts, placed, folded)
+    )(halo, taps, sums, own, copies, gain, parts, folded)
 
 
 def fold_kernel(after, listed, columns, patch, embed, scale, folded, placed, gram, added, table, rows, counts, sem):
@@ -450,8 +448,8 @@
     folded, placed, gram, added = fold(
         gain, frame_counts, query_weight.T, patch_weight, frame_embed, query_gain[None, :]
     )
-    parts = outer_even(even_pair, taps, sums, own, tokens, copies, gain)
-    message = outer_odd(odd_pair, taps, sums, own, tokens, copies, gain, parts, placed, folded)
+    parts = outer_even(even_pair, taps, sums, own, tokens, copies, gain, placed)
+    message = outer_odd(odd_pair, taps, sums, own, copies, gain, parts, folded)
     arrived = lax.all_to_all(message, "cp", split_axis=0, concat_axis=0, tiled=True)
     return project(arrived, gram, added, jnp.asarray(spread_table(), BF))
 

time: 49.1 us -> 49.2 us (level)
  no operation moved by 1% of the time
where the time goes in v11:
time: 49.2 us; the launch traced here: 49 us
  blocking collectives  24.7 us (50%)
  Pallas kernels  18.8 us (38%)
  starting transfers between devices  5.22 us (11%)
    all_to_all x1, blocking collectives, local(): lax.all_to_all(message, 'cp', split_axis=0, concat_axis=0, tiled=True)  24.7 us
    pallas_call x1, Pallas kernels, inner(): pl.pallas_call(inner_kernel, out_shape=(jax.ShapeDtypeStruct((2, FRAMES *...  10.6 us
    ppermute x1, starting transfers between devices, local(): even_pair = lax.ppermute(even_rows, 'cp', swaps[1])  4.53 us
    pallas_call x1, Pallas kernels, fetch(): pl.pallas_call(fetch_kernel, out_shape=(pltpu.VMEM((FRAMES, WIDTH, C), BF...  2.35 us
    pallas_call x1, Pallas kernels, project(): pl.pallas_call(project_kernel, out_shape=jax.ShapeDtypeStruct((HEADS, TOK...  2.34 us
    pallas_call x1, Pallas kernels, outer_odd(): pl.pallas_call(outer_odd_kernel, out_shape=jax.ShapeDtypeStruct((FRAMES,...  1.36 us
    pallas_call x1, Pallas kernels, outer_even(): pl.pallas_call(outer_even_kernel, out_shape=jax.ShapeDtypeStruct((8, FRAM...  1.33 us
  transfers between devices with their start and end apart: 2, of which 1 were waited for; matrix products, arithmetic and copies ran while one was open for 0% of the time, Pallas kernels for 26%

profile of v11, /device:TPU:0, one launch (start us, length us, event | category | flops | bytes accessed | tf_op | source)
XLA Modules:
  0.0 49.0 jit_solution(7941078936595140808)
XLA Ops:
  0.0 2.3 %fetch.1 = (bf16[64,8,512]{2,1,0:T(8,128)(2,1)S(1)}, bf16[64,8,512]{2,1,0:T(8,128)(2,1)S(1)}, bf16[64,4,8,512]{3,2,1,0:T(8,128)(2,1)S(1)}) custom-call(s32[16]{0:T(128)} %listed.1, bf16[96,4,8,512]{3,2,1,0:T(8,128)(2,1)} %frames.1), custom_call_target="tpu_custom_call" | custom-call | bytes 4194304 | tf_op jit(solution)/shard_map/fetch/pallas_call | solution.py:77
  2.4 0.7 %collective-permute-start = (bf16[64,8,512]{2,1,0:T(8,128)(2,1)S(1)}, bf16[64,8,512]{2,1,0:T(8,128)(2,1)S(1)}, u32[]{:S(2)}, u32[]{:S(2)}) collective-permute-start(bf16[64,8,512]{2,1,0:T(8,128)(2,1)S(1)} %get-tuple-element.18), channel_id=1, source_target_pairs={{2,4},{6,8},{10,12},{14,16},{18,20},{22,24},{26,28},{30,32},{34,36... | collective-permute-start | bytes 1572872 | tf_op jit(solution)/shard_map/ppermute | solution.py:444
  3.1 4.5 %collective-permute-start.1 = (bf16[64,8,512]{2,1,0:T(8,128)(2,1)S(1)}, bf16[64,8,512]{2,1,0:T(8,128)(2,1)S(1)}, u32[]{:S(2)}, u32[]{:S(2)}) collective-permute-start(bf16[64,8,512]{2,1,0:T(8,128)(2,1)S(1)} %get-tuple-element.25), channel_id=1, source_target_pairs={{0,2},{4,6},{8,10},{12,14},{16,18},{20,22},{24,26},{28,30},{32,34}... | collective-permute-start | bytes 1572872 | tf_op jit(solution)/shard_map/ppermute | solution.py:443
  7.6 0.0 copy-start.1
  7.6 0.0 copy-start.2
  7.6 0.0 copy-start.3
  7.6 0.0 copy-start.4
  7.6 10.6 %inner.1 = (f32[2,512,512]{2,1,0:T(8,128)S(1)}, bf16[2,512,512]{2,1,0:T(8,128)(2,1)S(1)}, f32[8,64,128]{2,1,0:T(8,128)S(1)}, bf16[3,1536,512]{2,1,0:T(8,128)(2,1...) custom-call(bf16[64,4,8,512]{3,2,1,0:T(8,128)(2,1)S(1)} %get-tuple-element.19.stage, ...), custom_call_target="tpu_custom_call" | custom-call | flops 8000000000 | bytes 9437184 | tf_op jit(solution)/shard_map/inner/pallas_call | solution.py:191
  18.2 0.0 copy-done.1
  18.2 0.0 copy-done.2
  18.2 0.0 copy-done.3
  18.2 0.0 copy-done.4
  18.2 0.8 %fold.1 = (f32[24,128]{1,0:T(8,128)S(1)}, f32[2,64,128]{2,1,0:T(8,128)S(1)}, bf16[128,256]{1,0:T(8,128)(2,1)S(1)}, f32[2,128]{1,0:T(2,128)S(1)}) custom-call(f32[1,512]{1,0:T(1,128)S(1)} %get-tuple-element.24.after.gain, s32[16]{0:T(128)} %listed.1, bf16[48,3072]{1,0:T(8,128)(2,1)S(1)} %bitcast.4, bf16[64,3072]{1,0:T(8,128)(2,1)S(1)} %copy-done.1, ...), custom_call_target="tpu_custom_call" | custom-call | flops 1000000000 | bytes 1048576 | tf_op jit(solution)/shard_map/fold/pallas_call | solution.py:335
  19.1 0.2 collective-permute-done.1.halo
  19.3 1.3 %outer_even.1.parts = f32[8,64,128]{2,1,0:T(8,128)S(1)} custom-call(bf16[64,8,512]{2,1,0:T(8,128)(2,1)S(1)} %collective-permute-done.1.halo, bf16[3,1536,512]{2,1,0:T(8,128)(2,1)S(1)} %get-tuple-element.20.taps, f32[2,512,512]{2,1,0:T(8,128)S(1)} %get-tuple-element.21.sums, bf16[2,512,512]{2,1,0:T(8,128)(2,1)S(1)} %get-tuple-element.22.own, ...), custom_call_target="tpu_custom_call" | custom-call | flops 800000000 | bytes 4194304 | tf_op jit(solution)/shard_map/outer_even/pallas_call | solution.py:247
  20.6 0.0 collective-permute-done.halo
  20.6 0.0 copy-start
  20.6 1.4 %outer_odd.1 = bf16[64,32,128]{2,1,0:T(8,128)(2,1)S(1)} custom-call(bf16[64,8,512]{2,1,0:T(8,128)(2,1)S(1)} %collective-permute-done.halo, bf16[3,1536,512]{2,1,0:T(8,128)(2,1)S(1)} %get-tuple-element.20.taps, f32[2,512,512]{2,1,0:T(8,128)S(1)} %get-tuple-element.21.sums, bf16[2,512,512]{2,1,0:T(8,128)(2,1)S(1)} %get-tuple-element.22.own, ...), custom_call_target="tpu_custom_call" | custom-call | flops 800000000 | bytes 4194304 | tf_op jit(solution)/shard_map/outer_odd/pallas_call | solution.py:271
  22.0 24.7 %all_to_all.5.arrived = bf16[64,32,128]{2,1,0:T(8,128)(2,1)S(1)} all-to-all(bf16[64,32,128]{2,1,0:T(8,128)(2,1)S(1)} %outer_odd.1), channel_id=1, replica_groups=mesh['cp'=64,'dp'=2] {'cp'}, dimensions={0} | all-to-all | bytes 1048576 | tf_op jit(solution)/shard_map/all_to_all | solution.py:453
  46.7 0.0 copy-done
  46.7 2.3 %project.1 = bf16[24,512,128]{2,1,0:T(8,128)(2,1)} custom-call(bf16[64,32,128]{2,1,0:T(8,128)(2,1)S(1)} %all_to_all.5.arrived, bf16[128,256]{1,0:T(8,128)(2,1)S(1)} %get-tuple-element.29.gram, f32[2,128]{1,0:T(2,128)S(1)} %get-tuple-element.30.added, bf16[128,384]{1,0:T(8,128)(2,1)S(1)} %copy-done), custom_call_target="tpu_custom_call" | custom-call | flops 800000000 | bytes 5242880 | tf_op jit(solution)/shard_map/project/pallas_call | solution.py:402
Async XLA Ops:
  2.4 18.3 %collective-permute-start = (bf16[64,8,512]{2,1,0:T(8,128)(2,1)S(1)}, bf16[64,8,512]{2,1,0:T(8,128)(2,1)S(1)}, u32[]{:S(2)}, u32[]{:S(2)}) collective-permute-start(bf16[64,8,512]{2,1,0:T(8,128)(2,1)S(1)} %get-tuple-element.18), channel_id=1, source_target_pairs={{2,4},{6,8},{10,12},{14,16},{18,20},{22,24},{26,28},{30,32},{34,36... | collective-permute-start | bytes 1572872 | tf_op jit(solution)/shard_map/ppermute | solution.py:444
  3.1 16.2 %collective-permute-start.1 = (bf16[64,8,512]{2,1,0:T(8,128)(2,1)S(1)}, bf16[64,8,512]{2,1,0:T(8,128)(2,1)S(1)}, u32[]{:S(2)}, u32[]{:S(2)}) collective-permute-start(bf16[64,8,512]{2,1,0:T(8,128)(2,1)S(1)} %get-tuple-element.25), channel_id=1, source_target_pairs={{0,2},{4,6},{8,10},{12,14},{16,18},{20,22},{24,26},{28,30},{32,34}... | collective-permute-start | bytes 1572872 | tf_op jit(solution)/shard_map/ppermute | solution.py:443
  7.6 10.6 %copy-start.1 = (bf16[64,3072]{1,0:T(8,128)(2,1)S(1)}, bf16[64,3072]{1,0:T(8,128)(2,1)}, u32[]{:S(2)}) copy-start(bf16[64,3072]{1,0:T(8,128)(2,1)} %patch.1) | copy-start | bytes 1179652
  7.6 10.6 %copy-start.2 = (bf16[3072,48]{0,1:T(8,128)(2,1)S(1)}, bf16[3072,48]{0,1:T(8,128)(2,1)}, u32[]{:S(2)}) copy-start(bf16[3072,48]{0,1:T(8,128)(2,1)} %param.18) | copy-start | bytes 884740
  7.6 10.6 %copy-start.3 = (bf16[6,3072]{1,0:T(8,128)(2,1)S(1)}, bf16[6,3072]{1,0:T(8,128)(2,1)}, u32[]{:S(2)}) copy-start(bf16[6,3072]{1,0:T(8,128)(2,1)} %embed.1) | copy-start | bytes 110596
  7.6 10.6 %copy-start.4 = (f32[3072]{0:T(1024)S(1)}, f32[3072]{0:T(1024)}, u32[]{:S(2)}) copy-start(f32[3072]{0:T(1024)} %param.17) | copy-start | bytes 36868
  20.6 26.0 %copy-start = (bf16[128,384]{1,0:T(8,128)(2,1)S(1)}, bf16[128,384]{1,0:T(8,128)(2,1)}, u32[]{:S(2)}) copy-start(bf16[128,384]{1,0:T(8,128)(2,1)} %constant.2.clone.spread) | copy-start | bytes 294916
